TPU v7x, 256 devices: a whole 4x4x8 slice. The times are simulated.
256 devices in a mesh: tm: 32 (over z, y), space: 8 (over x, core).
Axes of the slice: x: 4, y: 4, z: 8, core: 2. Of those that a mesh axis runs over, the one named last changes fastest.
Arguments:
- c_values: float32 [32, 2, 512, 512], P('tm', None, 'space'), may hold values from -2.5 to 2.5
- viscosity: float32 [512, 512], P('space'), may hold values from 0.05 to 0.2
Outputs:
- corrected: float32 [32, 2, 512, 512], P('tm', None, 'space')
- advanced: float32 [32, 2, 512, 512], P('tm', None, 'space')
- defect: float32 [32, 2, 512, 512], P('tm', None, 'space')
All inputs are finite; a program needn't handle non-finite values.
Results may differ from a plain program's by a relative error of at most 0.00002.
Values sent between devices are 32-bit elements; how exact they have to be, the bound alone decides.
No kernel may reach another device: no remote copies, remote signals or barrier semaphores. Data moves between devices by JAX's collectives and lax.ppermute only.
A program may use at most 256 MiB of HBM per device.

v0:
```python
import jax
import jax.numpy as jnp
from jax import lax
from jax.sharding import PartitionSpec as P

STEPS = 8


advect_scale = 0.1
coarse_size = 1.0


def padded(block, sides, width):
    for axis, dim in sides:
        count = lax.axis_size(axis)
        forward = [(i, i + 1) for i in range(count - 1)]
        forward.append((count - 1, 0))
        backward = [(target, source) for source, target in forward]
        low = lax.ppermute(
            lax.slice_in_dim(block, block.shape[dim] - width, None, axis=dim), axis, forward
        )
        high = lax.ppermute(lax.slice_in_dim(block, 0, width, axis=dim), axis, backward)
        block = jnp.concatenate([low, block, high], axis=dim)
    return block


def from_behind(value, axis, steps):
    count = lax.axis_size(axis)
    initial, last = (max(0, -steps), min(count, count - steps))
    return lax.ppermute(value, axis, [(source, source + steps) for source in range(initial, last)])


def tendency(extended, visc_rows):
    u_part = extended[0]
    v_part = extended[1]
    visc_mid = visc_rows[1:-1]
    face_xp = 0.5 * (visc_mid + visc_rows[2:])
    face_xm = 0.5 * (visc_rows[:-2] + visc_mid)
    face_yp = 0.5 * (visc_mid + jnp.roll(visc_mid, -1, -1))
    face_ym = jnp.roll(face_yp, 1, -1)
    u_mid = u_part[1:-1]
    v_mid = v_part[1:-1]

    def one_field(field):
        centre = field[1:-1]
        below = field[2:]
        above = field[:-2]
        right_cell = jnp.roll(centre, -1, -1)
        left_cell = jnp.roll(centre, 1, -1)
        carried = u_mid * (0.5 * (below - above)) + v_mid * (0.5 * (right_cell - left_cell))
        spread = (
            face_xp * (below - centre)
            - face_xm * (centre - above)
            + face_yp * (right_cell - centre)
            - face_ym * (centre - left_cell)
        )
        return -advect_scale * carried + spread

    return jnp.stack([one_field(u_part), one_field(v_part)], axis=0)


def heun_step(extended, visc_rows, size):
    first = tendency(extended, visc_rows)
    midpoint = extended[:, 1:-1] + size * first
    second = tendency(midpoint, visc_rows[1:-1])
    return extended[:, 2:-2] + 0.5 * size * (first[:, 1:-1] + second)


def fine_march(state, visc_wide):
    rows = state.shape[1]
    margin = 2 * STEPS
    fine_size = coarse_size / STEPS
    for step in range(STEPS):
        extended = padded(state, (("space", 1),), 2)
        state = heun_step(extended, visc_wide[margin - 2 : rows + margin + 2], fine_size)
    return state


def coarse_step(state, visc_wide):
    rows = state.shape[1]
    margin = 2 * STEPS
    extended = padded(state, (("space", 1),), 2)
    return heun_step(extended, visc_wide[margin - 2 : rows + margin + 2], coarse_size)


def shards(c_values, viscosity):
    state = c_values[0]
    visc_wide = padded(viscosity, (("space", 0),), 2 * STEPS)
    position = lax.axis_index("tm")
    forward = fine_march(state, visc_wide)
    tau_term = forward - coarse_step(state, visc_wide)
    handed = from_behind(forward, "tm", 1)
    defect = jnp.where(position == 0, jnp.zeros_like(state), handed - state)
    count = lax.axis_size("tm")

    def turn(turn_index, current):
        candidate = coarse_step(current, visc_wide) + tau_term
        received = from_behind(candidate, "tm", 1)
        return jnp.where(position == turn_index + 1, received, current)

    corrected = lax.fori_loop(0, count - 1, turn, state)
    advanced = fine_march(corrected, visc_wide)
    return (corrected[None], advanced[None], defect[None])


def solution(mesh):
    return jax.shard_map(
        shards,
        mesh=mesh,
        in_specs=(P("tm", None, "space", None), P("space", None)),
        out_specs=(
            P("tm", None, "space", None),
            P("tm", None, "space", None),
            P("tm", None, "space", None),
        ),
        check_vma=False,
    )
```

profile of v0, /device:TPU:120, one launch (start us, length us, event | category | flops | bytes accessed | tf_op | source)
XLA Modules:
  0.0 1130.1 jit_solution(10397819425308007632)
XLA Ops:
  77.4 987.1 %while.15 = (s32[]{:T(128)}, f32[2,64,512]{1,2,0:T(8,128)S(1)}, s32[]{:T(128)}, f32[66,512]{0,1:T(8,128)S(1)}, f32[66,512]{0,1:T(8,128)S(1)}, /*index=5*/f32[66,...) while((s32[]{:T(128)}, f32[2,64,512]{1,2,0:T(8,128)S(1)}, ...), condition=%wide.region_1.2_spmd, body=%wide.region_0.1_spmd.sunk | while | flops 4396035 | bytes 15536395 | solution.py:101
  124.1 7.4 collective-permute-start.2
  156.4 7.4 collective-permute-start.2
  188.7 7.4 collective-permute-start.2
  196.1 7.7 collective-permute-done.2
  220.8 7.4 collective-permute-start.2
  228.2 8.1 collective-permute-done.2
  252.8 7.4 collective-permute-start.2
  260.2 8.2 collective-permute-done.2
  284.7 7.4 collective-permute-start.2
  292.2 8.3 collective-permute-done.2
  316.6 7.4 collective-permute-start.2
  324.0 8.4 collective-permute-done.2
  348.4 7.4 collective-permute-start.2
  355.8 8.4 collective-permute-done.2
  380.2 7.4 collective-permute-start.2
  387.6 8.4 collective-permute-done.2
  419.4 8.4 collective-permute-done.2
  443.7 7.4 collective-permute-start.2
  451.1 8.4 collective-permute-done.2
  475.5 7.4 collective-permute-start.2
  482.9 8.4 collective-permute-done.2
  514.6 8.4 collective-permute-done.2
  539.0 7.4 collective-permute-start.2
  546.4 8.4 collective-permute-done.2
  578.1 8.2 collective-permute-done.2
  602.6 8.4 collective-permute-start.2
  611.0 8.4 collective-permute-done.2
  635.3 7.4 collective-permute-start.2
  642.7 8.3 collective-permute-done.2
  667.2 7.4 collective-permute-start.2
  674.6 8.4 collective-permute-done.2
  698.9 7.4 collective-permute-start.2
  706.3 8.3 collective-permute-done.2
  730.7 7.4 collective-permute-start.2
  738.2 8.4 collective-permute-done.2
  762.5 7.4 collective-permute-start.2
  769.9 8.3 collective-permute-done.2
  801.7 8.4 collective-permute-done.2
  833.5 8.3 collective-permute-done.2
  865.3 8.4 collective-permute-done.2
  897.1 8.3 collective-permute-done.2
  928.9 8.4 collective-permute-done.2
  960.6 8.3 collective-permute-done.2
  992.5 8.4 collective-permute-done.2
  1024.2 8.3 collective-permute-done.2
  1056.1 8.4 collective-permute-done.2
  1113.8 7.7 collective-permute-start.37
  (1566 shorter events, 745.7 us)
Async XLA Ops:
  80.1 9.8 collective-permute-start.1
  94.4 11.7 %collective-permute-start.2 = (f32[2,64,512]{1,2,0:T(8,128)}, f32[2,64,512]{1,2,0:T(8,128)}, u32[]{:S(2)}, u32[]{:S(2)}) collective-permute-start(f32[2,64,512]{1,2,0:T(8,128)} %fusion.381), channel_id=1, source_target_pairs={{0,8},{8,16},{16,24},{24,32},{32,40},{40,48},{48,56},{56,64},{64,7... | collective-permute-start | bytes 786440 | tf_op jit(solution)/shard_map/while/body/eval_jaxpr/ppermute | solution.py:30
  106.4 10.0 collective-permute-start
  109.7 9.8 collective-permute-start.1
  124.1 14.4 %collective-permute-start.2 = (f32[2,64,512]{1,2,0:T(8,128)}, f32[2,64,512]{1,2,0:T(8,128)}, u32[]{:S(2)}, u32[]{:S(2)}) collective-permute-start(f32[2,64,512]{1,2,0:T(8,128)} %fusion.381), channel_id=1, source_target_pairs={{0,8},{8,16},{16,24},{24,32},{32,40},{40,48},{48,56},{56,64},{64,7... | collective-permute-start | bytes 786440 | tf_op jit(solution)/shard_map/while/body/eval_jaxpr/ppermute | solution.py:30
  138.8 10.0 collective-permute-start
  142.1 9.8 collective-permute-start.1
  156.4 14.5 %collective-permute-start.2 = (f32[2,64,512]{1,2,0:T(8,128)}, f32[2,64,512]{1,2,0:T(8,128)}, u32[]{:S(2)}, u32[]{:S(2)}) collective-permute-start(f32[2,64,512]{1,2,0:T(8,128)} %fusion.381), channel_id=1, source_target_pairs={{0,8},{8,16},{16,24},{24,32},{32,40},{40,48},{48,56},{56,64},{64,7... | collective-permute-start | bytes 786440 | tf_op jit(solution)/shard_map/while/body/eval_jaxpr/ppermute | solution.py:30
  171.2 9.8 collective-permute-start
  174.3 9.8 collective-permute-start.1
  188.7 15.2 %collective-permute-start.2 = (f32[2,64,512]{1,2,0:T(8,128)}, f32[2,64,512]{1,2,0:T(8,128)}, u32[]{:S(2)}, u32[]{:S(2)}) collective-permute-start(f32[2,64,512]{1,2,0:T(8,128)} %fusion.381), channel_id=1, source_target_pairs={{0,8},{8,16},{16,24},{24,32},{32,40},{40,48},{48,56},{56,64},{64,7... | collective-permute-start | bytes 786440 | tf_op jit(solution)/shard_map/while/body/eval_jaxpr/ppermute | solution.py:30
  206.5 9.8 collective-permute-start.1
  220.8 15.5 %collective-permute-start.2 = (f32[2,64,512]{1,2,0:T(8,128)}, f32[2,64,512]{1,2,0:T(8,128)}, u32[]{:S(2)}, u32[]{:S(2)}) collective-permute-start(f32[2,64,512]{1,2,0:T(8,128)} %fusion.381), channel_id=1, source_target_pairs={{0,8},{8,16},{16,24},{24,32},{32,40},{40,48},{48,56},{56,64},{64,7... | collective-permute-start | bytes 786440 | tf_op jit(solution)/shard_map/while/body/eval_jaxpr/ppermute | solution.py:30
  238.5 9.8 collective-permute-start.1
  252.8 15.6 %collective-permute-start.2 = (f32[2,64,512]{1,2,0:T(8,128)}, f32[2,64,512]{1,2,0:T(8,128)}, u32[]{:S(2)}, u32[]{:S(2)}) collective-permute-start(f32[2,64,512]{1,2,0:T(8,128)} %fusion.381), channel_id=1, source_target_pairs={{0,8},{8,16},{16,24},{24,32},{32,40},{40,48},{48,56},{56,64},{64,7... | collective-permute-start | bytes 786440 | tf_op jit(solution)/shard_map/while/body/eval_jaxpr/ppermute | solution.py:30
  270.4 9.8 collective-permute-start.1
  284.7 15.7 %collective-permute-start.2 = (f32[2,64,512]{1,2,0:T(8,128)}, f32[2,64,512]{1,2,0:T(8,128)}, u32[]{:S(2)}, u32[]{:S(2)}) collective-permute-start(f32[2,64,512]{1,2,0:T(8,128)} %fusion.381), channel_id=1, source_target_pairs={{0,8},{8,16},{16,24},{24,32},{32,40},{40,48},{48,56},{56,64},{64,7... | collective-permute-start | bytes 786440 | tf_op jit(solution)/shard_map/while/body/eval_jaxpr/ppermute | solution.py:30
  302.3 9.8 collective-permute-start.1
  316.6 15.8 %collective-permute-start.2 = (f32[2,64,512]{1,2,0:T(8,128)}, f32[2,64,512]{1,2,0:T(8,128)}, u32[]{:S(2)}, u32[]{:S(2)}) collective-permute-start(f32[2,64,512]{1,2,0:T(8,128)} %fusion.381), channel_id=1, source_target_pairs={{0,8},{8,16},{16,24},{24,32},{32,40},{40,48},{48,56},{56,64},{64,7... | collective-permute-start | bytes 786440 | tf_op jit(solution)/shard_map/while/body/eval_jaxpr/ppermute | solution.py:30
  334.1 9.8 collective-permute-start.1
  348.4 15.8 %collective-permute-start.2 = (f32[2,64,512]{1,2,0:T(8,128)}, f32[2,64,512]{1,2,0:T(8,128)}, u32[]{:S(2)}, u32[]{:S(2)}) collective-permute-start(f32[2,64,512]{1,2,0:T(8,128)} %fusion.381), channel_id=1, source_target_pairs={{0,8},{8,16},{16,24},{24,32},{32,40},{40,48},{48,56},{56,64},{64,7... | collective-permute-start | bytes 786440 | tf_op jit(solution)/shard_map/while/body/eval_jaxpr/ppermute | solution.py:30
  380.2 15.8 %collective-permute-start.2 = (f32[2,64,512]{1,2,0:T(8,128)}, f32[2,64,512]{1,2,0:T(8,128)}, u32[]{:S(2)}, u32[]{:S(2)}) collective-permute-start(f32[2,64,512]{1,2,0:T(8,128)} %fusion.381), channel_id=1, source_target_pairs={{0,8},{8,16},{16,24},{24,32},{32,40},{40,48},{48,56},{56,64},{64,7... | collective-permute-start | bytes 786440 | tf_op jit(solution)/shard_map/while/body/eval_jaxpr/ppermute | solution.py:30
  411.9 15.8 %collective-permute-start.2 = (f32[2,64,512]{1,2,0:T(8,128)}, f32[2,64,512]{1,2,0:T(8,128)}, u32[]{:S(2)}, u32[]{:S(2)}) collective-permute-start(f32[2,64,512]{1,2,0:T(8,128)} %fusion.381), channel_id=1, source_target_pairs={{0,8},{8,16},{16,24},{24,32},{32,40},{40,48},{48,56},{56,64},{64,7... | collective-permute-start | bytes 786440 | tf_op jit(solution)/shard_map/while/body/eval_jaxpr/ppermute | solution.py:30
  443.7 15.8 %collective-permute-start.2 = (f32[2,64,512]{1,2,0:T(8,128)}, f32[2,64,512]{1,2,0:T(8,128)}, u32[]{:S(2)}, u32[]{:S(2)}) collective-permute-start(f32[2,64,512]{1,2,0:T(8,128)} %fusion.381), channel_id=1, source_target_pairs={{0,8},{8,16},{16,24},{24,32},{32,40},{40,48},{48,56},{56,64},{64,7... | collective-permute-start | bytes 786440 | tf_op jit(solution)/shard_map/while/body/eval_jaxpr/ppermute | solution.py:30
  475.5 15.8 %collective-permute-start.2 = (f32[2,64,512]{1,2,0:T(8,128)}, f32[2,64,512]{1,2,0:T(8,128)}, u32[]{:S(2)}, u32[]{:S(2)}) collective-permute-start(f32[2,64,512]{1,2,0:T(8,128)} %fusion.381), channel_id=1, source_target_pairs={{0,8},{8,16},{16,24},{24,32},{32,40},{40,48},{48,56},{56,64},{64,7... | collective-permute-start | bytes 786440 | tf_op jit(solution)/shard_map/while/body/eval_jaxpr/ppermute | solution.py:30
  507.1 15.8 %collective-permute-start.2 = (f32[2,64,512]{1,2,0:T(8,128)}, f32[2,64,512]{1,2,0:T(8,128)}, u32[]{:S(2)}, u32[]{:S(2)}) collective-permute-start(f32[2,64,512]{1,2,0:T(8,128)} %fusion.381), channel_id=1, source_target_pairs={{0,8},{8,16},{16,24},{24,32},{32,40},{40,48},{48,56},{56,64},{64,7... | collective-permute-start | bytes 786440 | tf_op jit(solution)/shard_map/while/body/eval_jaxpr/ppermute | solution.py:30
  539.0 15.8 %collective-permute-start.2 = (f32[2,64,512]{1,2,0:T(8,128)}, f32[2,64,512]{1,2,0:T(8,128)}, u32[]{:S(2)}, u32[]{:S(2)}) collective-permute-start(f32[2,64,512]{1,2,0:T(8,128)} %fusion.381), channel_id=1, source_target_pairs={{0,8},{8,16},{16,24},{24,32},{32,40},{40,48},{48,56},{56,64},{64,7... | collective-permute-start | bytes 786440 | tf_op jit(solution)/shard_map/while/body/eval_jaxpr/ppermute | solution.py:30
  571.7 14.6 %collective-permute-start.2 = (f32[2,64,512]{1,2,0:T(8,128)}, f32[2,64,512]{1,2,0:T(8,128)}, u32[]{:S(2)}, u32[]{:S(2)}) collective-permute-start(f32[2,64,512]{1,2,0:T(8,128)} %fusion.381), channel_id=1, source_target_pairs={{0,8},{8,16},{16,24},{24,32},{32,40},{40,48},{48,56},{56,64},{64,7... | collective-permute-start | bytes 786440 | tf_op jit(solution)/shard_map/while/body/eval_jaxpr/ppermute | solution.py:30
  602.6 16.9 %collective-permute-start.2 = (f32[2,64,512]{1,2,0:T(8,128)}, f32[2,64,512]{1,2,0:T(8,128)}, u32[]{:S(2)}, u32[]{:S(2)}) collective-permute-start(f32[2,64,512]{1,2,0:T(8,128)} %fusion.381), channel_id=1, source_target_pairs={{0,8},{8,16},{16,24},{24,32},{32,40},{40,48},{48,56},{56,64},{64,7... | collective-permute-start | bytes 786440 | tf_op jit(solution)/shard_map/while/body/eval_jaxpr/ppermute | solution.py:30
  635.3 15.7 %collective-permute-start.2 = (f32[2,64,512]{1,2,0:T(8,128)}, f32[2,64,512]{1,2,0:T(8,128)}, u32[]{:S(2)}, u32[]{:S(2)}) collective-permute-start(f32[2,64,512]{1,2,0:T(8,128)} %fusion.381), channel_id=1, source_target_pairs={{0,8},{8,16},{16,24},{24,32},{32,40},{40,48},{48,56},{56,64},{64,7... | collective-permute-start | bytes 786440 | tf_op jit(solution)/shard_map/while/body/eval_jaxpr/ppermute | solution.py:30
  667.2 15.8 %collective-permute-start.2 = (f32[2,64,512]{1,2,0:T(8,128)}, f32[2,64,512]{1,2,0:T(8,128)}, u32[]{:S(2)}, u32[]{:S(2)}) collective-permute-start(f32[2,64,512]{1,2,0:T(8,128)} %fusion.381), channel_id=1, source_target_pairs={{0,8},{8,16},{16,24},{24,32},{32,40},{40,48},{48,56},{56,64},{64,7... | collective-permute-start | bytes 786440 | tf_op jit(solution)/shard_map/while/body/eval_jaxpr/ppermute | solution.py:30
  698.9 15.7 %collective-permute-start.2 = (f32[2,64,512]{1,2,0:T(8,128)}, f32[2,64,512]{1,2,0:T(8,128)}, u32[]{:S(2)}, u32[]{:S(2)}) collective-permute-start(f32[2,64,512]{1,2,0:T(8,128)} %fusion.381), channel_id=1, source_target_pairs={{0,8},{8,16},{16,24},{24,32},{32,40},{40,48},{48,56},{56,64},{64,7... | collective-permute-start | bytes 786440 | tf_op jit(solution)/shard_map/while/body/eval_jaxpr/ppermute | solution.py:30
  730.7 15.8 %collective-permute-start.2 = (f32[2,64,512]{1,2,0:T(8,128)}, f32[2,64,512]{1,2,0:T(8,128)}, u32[]{:S(2)}, u32[]{:S(2)}) collective-permute-start(f32[2,64,512]{1,2,0:T(8,128)} %fusion.381), channel_id=1, source_target_pairs={{0,8},{8,16},{16,24},{24,32},{32,40},{40,48},{48,56},{56,64},{64,7... | collective-permute-start | bytes 786440 | tf_op jit(solution)/shard_map/while/body/eval_jaxpr/ppermute | solution.py:30
  762.5 15.7 %collective-permute-start.2 = (f32[2,64,512]{1,2,0:T(8,128)}, f32[2,64,512]{1,2,0:T(8,128)}, u32[]{:S(2)}, u32[]{:S(2)}) collective-permute-start(f32[2,64,512]{1,2,0:T(8,128)} %fusion.381), channel_id=1, source_target_pairs={{0,8},{8,16},{16,24},{24,32},{32,40},{40,48},{48,56},{56,64},{64,7... | collective-permute-start | bytes 786440 | tf_op jit(solution)/shard_map/while/body/eval_jaxpr/ppermute | solution.py:30
  794.3 15.8 %collective-permute-start.2 = (f32[2,64,512]{1,2,0:T(8,128)}, f32[2,64,512]{1,2,0:T(8,128)}, u32[]{:S(2)}, u32[]{:S(2)}) collective-permute-start(f32[2,64,512]{1,2,0:T(8,128)} %fusion.381), channel_id=1, source_target_pairs={{0,8},{8,16},{16,24},{24,32},{32,40},{40,48},{48,56},{56,64},{64,7... | collective-permute-start | bytes 786440 | tf_op jit(solution)/shard_map/while/body/eval_jaxpr/ppermute | solution.py:30
  811.7 9.8 collective-permute-start.1
  826.1 15.7 %collective-permute-start.2 = (f32[2,64,512]{1,2,0:T(8,128)}, f32[2,64,512]{1,2,0:T(8,128)}, u32[]{:S(2)}, u32[]{:S(2)}) collective-permute-start(f32[2,64,512]{1,2,0:T(8,128)} %fusion.381), channel_id=1, source_target_pairs={{0,8},{8,16},{16,24},{24,32},{32,40},{40,48},{48,56},{56,64},{64,7... | collective-permute-start | bytes 786440 | tf_op jit(solution)/shard_map/while/body/eval_jaxpr/ppermute | solution.py:30
  857.9 15.8 %collective-permute-start.2 = (f32[2,64,512]{1,2,0:T(8,128)}, f32[2,64,512]{1,2,0:T(8,128)}, u32[]{:S(2)}, u32[]{:S(2)}) collective-permute-start(f32[2,64,512]{1,2,0:T(8,128)} %fusion.381), channel_id=1, source_target_pairs={{0,8},{8,16},{16,24},{24,32},{32,40},{40,48},{48,56},{56,64},{64,7... | collective-permute-start | bytes 786440 | tf_op jit(solution)/shard_map/while/body/eval_jaxpr/ppermute | solution.py:30
  889.6 15.7 %collective-permute-start.2 = (f32[2,64,512]{1,2,0:T(8,128)}, f32[2,64,512]{1,2,0:T(8,128)}, u32[]{:S(2)}, u32[]{:S(2)}) collective-permute-start(f32[2,64,512]{1,2,0:T(8,128)} %fusion.381), channel_id=1, source_target_pairs={{0,8},{8,16},{16,24},{24,32},{32,40},{40,48},{48,56},{56,64},{64,7... | collective-permute-start | bytes 786440 | tf_op jit(solution)/shard_map/while/body/eval_jaxpr/ppermute | solution.py:30
  907.2 9.8 collective-permute-start.1
  921.5 15.8 %collective-permute-start.2 = (f32[2,64,512]{1,2,0:T(8,128)}, f32[2,64,512]{1,2,0:T(8,128)}, u32[]{:S(2)}, u32[]{:S(2)}) collective-permute-start(f32[2,64,512]{1,2,0:T(8,128)} %fusion.381), channel_id=1, source_target_pairs={{0,8},{8,16},{16,24},{24,32},{32,40},{40,48},{48,56},{56,64},{64,7... | collective-permute-start | bytes 786440 | tf_op jit(solution)/shard_map/while/body/eval_jaxpr/ppermute | solution.py:30
  953.2 15.7 %collective-permute-start.2 = (f32[2,64,512]{1,2,0:T(8,128)}, f32[2,64,512]{1,2,0:T(8,128)}, u32[]{:S(2)}, u32[]{:S(2)}) collective-permute-start(f32[2,64,512]{1,2,0:T(8,128)} %fusion.381), channel_id=1, source_target_pairs={{0,8},{8,16},{16,24},{24,32},{32,40},{40,48},{48,56},{56,64},{64,7... | collective-permute-start | bytes 786440 | tf_op jit(solution)/shard_map/while/body/eval_jaxpr/ppermute | solution.py:30
  985.1 15.8 %collective-permute-start.2 = (f32[2,64,512]{1,2,0:T(8,128)}, f32[2,64,512]{1,2,0:T(8,128)}, u32[]{:S(2)}, u32[]{:S(2)}) collective-permute-start(f32[2,64,512]{1,2,0:T(8,128)} %fusion.381), channel_id=1, source_target_pairs={{0,8},{8,16},{16,24},{24,32},{32,40},{40,48},{48,56},{56,64},{64,7... | collective-permute-start | bytes 786440 | tf_op jit(solution)/shard_map/while/body/eval_jaxpr/ppermute | solution.py:30
  1016.8 15.7 %collective-permute-start.2 = (f32[2,64,512]{1,2,0:T(8,128)}, f32[2,64,512]{1,2,0:T(8,128)}, u32[]{:S(2)}, u32[]{:S(2)}) collective-permute-start(f32[2,64,512]{1,2,0:T(8,128)} %fusion.381), channel_id=1, source_target_pairs={{0,8},{8,16},{16,24},{24,32},{32,40},{40,48},{48,56},{56,64},{64,7... | collective-permute-start | bytes 786440 | tf_op jit(solution)/shard_map/while/body/eval_jaxpr/ppermute | solution.py:30
  1048.6 15.8 %collective-permute-start.2 = (f32[2,64,512]{1,2,0:T(8,128)}, f32[2,64,512]{1,2,0:T(8,128)}, u32[]{:S(2)}, u32[]{:S(2)}) collective-permute-start(f32[2,64,512]{1,2,0:T(8,128)} %fusion.381), channel_id=1, source_target_pairs={{0,8},{8,16},{16,24},{24,32},{32,40},{40,48},{48,56},{56,64},{64,7... | collective-permute-start | bytes 786440 | tf_op jit(solution)/shard_map/while/body/eval_jaxpr/ppermute | solution.py:30
  1110.8 10.7 collective-permute-start.35
  1110.8 10.7 collective-permute-start.36
  1113.8 15.5 %collective-permute-start.37 = (f32[2,64,512]{2,1,0:T(8,128)}, f32[2,64,512]{2,1,0:T(8,128)S(1)}, u32[]{:S(2)}, u32[]{:S(2)}) collective-permute-start(f32[2,64,512]{2,1,0:T(8,128)} %get-tuple-element.190), channel_id=1, source_target_pairs={{0,8},{8,16},{16,24},{24,32},{32,40},{40,48},{48,56},{56,64},{64,7... | collective-permute-start | bytes 786440 | tf_op jit(solution)/shard_map/ppermute | solution.py:30
  (214 other events, 1372.9 us)
where the time goes:
time: 1130 us
  waiting for transfers between devices  575 us (51%)
  starting transfers between devices  335 us (30%)
  other arithmetic  143 us (13%)
  local copies, waits for them, and re-layouts  67.2 us (6%)
    ppermute x32, waiting for transfers between devices, from_behind(): lax.ppermute(value, axis, [(source, source + steps) for source in range(i...  254 us
    ppermute x32, starting transfers between devices, from_behind(): lax.ppermute(value, axis, [(source, source + steps) for source in range(i...  234 us
    ppermute x48, waiting for transfers between devices, padded(): lax.ppermute(lax.slice_in_dim(block, 0, width, axis=dim), axis, backward)  205 us
    ppermute x48, waiting for transfers between devices, padded(): lax.ppermute(lax.slice_in_dim(block, block.shape[dim] - width, None, axis...  115 us
    ppermute x48, starting transfers between devices, padded(): lax.ppermute(lax.slice_in_dim(block, 0, width, axis=dim), axis, backward)  101 us
    add x124, other arithmetic, one_field(): return -advect_scale * carried + spread  54.9 us
    add x31, other arithmetic, turn(): candidate = coarse_step(current, visc_wide) + tau_term  32.5 us
  transfers between devices with their start and end apart: 128, of which 108 were waited for; matrix products, arithmetic and copies ran while one was open for 1% of the time, Pallas kernels for 0%

commit v1 on v0

v1 whole, which is shorter than its diff:
```python
import functools

import jax
import jax.numpy as jnp
from jax import lax
from jax.experimental import pallas as pl
from jax.experimental.pallas import tpu as pltpu
from jax.sharding import PartitionSpec as P

STEPS = 8
GROUP = 8
STRIP = 8
HALO = 16
LANES = 128
WINDOW = STRIP + 2 * HALO
advect_scale = 0.1
coarse_size = 1.0
f32 = jnp.float32


def shift_up(plane):
    return pltpu.roll(plane, 1, 0)


def shift_down(plane):
    return pltpu.roll(plane, plane.shape[0] - 1, 0)


def left_of(x):
    return pltpu.roll(x, 1, 1)


def right_of(x):
    return pltpu.roll(x, x.shape[1] - 1, 1)


def make_coefs(planes, size, coef):
    cx, cyp, cym, dd = coef
    n = len(planes)
    faces = []
    for i in range(n):
        below = planes[i + 1] if i + 1 < n else shift_down(planes[0])
        faces.append((0.5 * size) * (planes[i] + below))
    first = shift_up(faces[n - 1])
    cx[0] = first
    for i in range(n):
        cx[i + 1] = faces[i]
        nyp = (0.5 * size) * (planes[i] + right_of(planes[i]))
        nym = left_of(nyp)
        cyp[i] = nyp
        cym[i] = nym
        nxm = faces[i - 1] if i > 0 else first
        dd[i] = 1.0 - ((faces[i] + nxm) + (nyp + nym))


def euler(src, coef, size, n, emit):
    cx, cyp, cym, dd = coef
    k = 0.5 * advect_scale * size
    above = [shift_up(src[c, n - 1]) for c in range(2)]
    here = [src[c, 0] for c in range(2)]
    first = here
    for i in range(n):
        if i + 1 < n:
            below = [src[c, i + 1] for c in range(2)]
        else:
            below = [shift_down(first[c]) for c in range(2)]
        ku = k * here[0]
        kv = k * here[1]
        wxp = cx[i + 1] - ku
        wxm = cx[i] + ku
        wyp = cyp[i] - kv
        wym = cym[i] + kv
        d = dd[i]
        res = []
        for c in range(2):
            f = here[c]
            res.append(
                (d * f + (wxp * below[c] + wxm * above[c]))
                + (wyp * right_of(f) + wym * left_of(f))
            )
        emit(i, res)
        above, here = here, below


def heun(src, mid, dst, coef, size, n, extra=None):
    def to_mid(i, res):
        for c in range(2):
            mid[c, i] = res[c]

    euler(src, coef, size, n, to_mid)

    def to_dst(i, res):
        for c in range(2):
            out = 0.5 * (src[c, i] + res[c])
            if extra is not None:
                out = out + extra(c, i)
            dst[c, i] = out

    euler(mid, coef, size, n, to_dst)


def plane(nat, i, n):
    return jnp.concatenate([nat[b, pl.ds(i, 8, stride=n), :] for b in range(nat.shape[0])], axis=1)


def put_plane(nat, i, n, value):
    for b in range(nat.shape[0]):
        nat[b, pl.ds(i, 8, stride=n), :] = value[:, b * LANES : (b + 1) * LANES]


def load_planes(nat, n):
    return [plane(nat, i, n) for i in range(n)]


def fill(nat, at, ref, start, count):
    for b in range(nat.shape[0]):
        nat[b, at : at + count, :] = ref[start : start + count, b * LANES : (b + 1) * LANES]


def whole(nat, start, count):
    return jnp.concatenate([nat[b, start : start + count, :] for b in range(nat.shape[0])], axis=1)


def forward_kernel(where_ref, c_ref, clo_ref, chi_ref, n_ref, nlo_ref, nhi_ref,
                   fwd_ref, tau_ref, nwin_ref,
                   nat, vnat, w, mid, tau, cf, cc):
    n = 16
    rows = c_ref.shape[1]
    edge = 2 * HALO
    for c in range(2):
        fill(nat.at[c], 0, clo_ref.at[c], rows - edge, edge)
        fill(nat.at[c], edge, c_ref.at[c], 0, rows)
        fill(nat.at[c], edge + rows, chi_ref.at[c], 0, edge)
    fill(vnat, 0, nlo_ref, rows - edge, edge)
    fill(vnat, edge, n_ref, 0, rows)
    fill(vnat, edge + rows, nhi_ref, 0, edge)
    position = where_ref[0]
    start = pl.multiple_of(lax.rem(position, GROUP) * STRIP + HALO, 8)
    nwin_ref[...] = vnat[:, pl.ds(start, WINDOW), :]

    visc = load_planes(vnat, n)
    make_coefs(visc, coarse_size, [cc.at[0], cc.at[1], cc.at[2], cc.at[3]])
    fine = coarse_size / STEPS
    make_coefs(visc, fine, [cf.at[0], cf.at[1], cf.at[2], cf.at[3]])
    coef_c = [cc.at[i] for i in range(4)]
    coef_f = [cf.at[i] for i in range(4)]
    for c in range(2):
        for i in range(n):
            w[c, i] = plane(nat.at[c], i, n)
    heun(w, mid, tau, coef_c, coarse_size, n)

    def step(_, carry):
        heun(w, mid, w, coef_f, fine, n)
        return carry

    lax.fori_loop(0, STEPS, step, 0)
    keep = jnp.where(position == 0, 0.0, 1.0).astype(f32)
    for c in range(2):
        for i in range(n):
            put_plane(nat.at[c], i, n, w[c, i])
        fwd_ref[c] = whole(nat.at[c], edge, rows)
        for i in range(n):
            put_plane(nat.at[c], i, n, w[c, i] - keep * tau[c, i])
        for p in range(GROUP):
            tau_ref[p, c] = nat[c, :, HALO + p * STRIP : HALO + p * STRIP + WINDOW, :]


def chain_kernel(stage, where_ref, tau_ref, nwin_ref, m2, m1, own, p1, p2, corr_in,
                 corr_ref, last_ref,
                 nat, w, mid, cc, part, sem):
    n = 5
    position = where_ref[0]

    @pl.when(position // GROUP == stage)
    def _():
        visc = load_planes(nwin_ref, n)
        coef = [cc.at[i] for i in range(4)]
        make_coefs(visc, coarse_size, coef)

        def keep(t):
            for c in range(2):
                for i in range(n):
                    put_plane(nat.at[c], i, n, w[c, i])
                part[t, c] = nat[c, :, HALO : HALO + STRIP, :]

        if stage == 0:
            for c in range(2):
                part[0, c] = jnp.zeros_like(part[0, c])
                for i in range(n):
                    w[c, i] = plane(tau_ref.at[0, c], i, n)
        else:
            for c in range(2):
                for k, ref in enumerate((m2, m1, own, p1, p2)):
                    nat[c, :, k * STRIP : (k + 1) * STRIP, :] = ref[c]
                part[0, c] = own[c]
                for i in range(n):
                    w[c, i] = plane(nat.at[c], i, n)
            heun(w, mid, w, coef, coarse_size, n,
                 lambda c, i: plane(tau_ref.at[0, c], i, n))
        keep(1)

        def step(t, carry):
            heun(w, mid, w, coef, coarse_size, n,
                 lambda c, i: plane(tau_ref.at[t, c], i, n))
            keep(t + 1)
            return carry

        lax.fori_loop(1, GROUP, step, 0)
        last_ref[...] = part[GROUP]
        copy = pltpu.make_async_copy(part.at[pl.ds(0, GROUP)], corr_ref, sem)
        copy.start()
        copy.wait()


def final_kernel(where_ref, got_ref, lo_ref, hi_ref, c_ref, clo_ref, chi_ref,
                 n_ref, nlo_ref, nhi_ref, handed_ref,
                 corr_ref, adv_ref, defect_ref,
                 nat, vnat, w, mid, cf):
    n = 12
    rows = c_ref.shape[1]
    position = where_ref[0]
    fill(vnat, 0, nlo_ref, rows - HALO, HALO)
    fill(vnat, HALO, n_ref, 0, rows)
    fill(vnat, HALO + rows, nhi_ref, 0, HALO)
    fine = coarse_size / STEPS
    coef = [cf.at[i] for i in range(4)]
    make_coefs(load_planes(vnat, n), fine, coef)

    @pl.when(position == 0)
    def _():
        for c in range(2):
            fill(nat.at[c], 0, clo_ref.at[c], rows - HALO, HALO)
            fill(nat.at[c], HALO, c_ref.at[c], 0, rows)
            fill(nat.at[c], HALO + rows, chi_ref.at[c], 0, HALO)
            defect_ref[0, c] = jnp.zeros_like(c_ref[c])

    @pl.when(position != 0)
    def _():
        for c in range(2):
            for k in range(2):
                nat[c, :, k * STRIP : (k + 1) * STRIP, :] = lo_ref[k, c]
                nat[c, :, HALO + rows + k * STRIP : HALO + rows + (k + 1) * STRIP, :] = hi_ref[k, c]
            for p in range(GROUP):
                nat[c, :, HALO + p * STRIP : HALO + (p + 1) * STRIP, :] = got_ref[p, c]
            defect_ref[0, c] = handed_ref[c] - c_ref[c]

    for c in range(2):
        corr_ref[0, c] = whole(nat.at[c], HALO, rows)
        for i in range(n):
            w[c, i] = plane(nat.at[c], i, n)

    def step(_, carry):
        heun(w, mid, w, coef, fine, n)
        return carry

    lax.fori_loop(0, STEPS, step, 0)
    for c in range(2):
        for i in range(n):
            put_plane(nat.at[c], i, n, w[c, i])
        adv_ref[0, c] = whole(nat.at[c], HALO, rows)


VMEM = pl.BlockSpec(memory_space=pltpu.VMEM)
SMEM = pl.BlockSpec(memory_space=pltpu.SMEM)
ANY = pl.BlockSpec(memory_space=pl.ANY)
LIMIT = 48 * 1024 * 1024


def shards(c_values, viscosity):
    c = c_values[0]
    _, rows, cols = c.shape
    ring = lax.axis_size("space")
    intervals = lax.axis_size("tm")
    up = [(i, (i + 1) % ring) for i in range(ring)]
    down = [(b, a) for a, b in up]
    where = lax.axis_index("tm").reshape(1).astype(jnp.int32)
    shape = lambda *s: jax.ShapeDtypeStruct(s, f32)
    vm = lambda *s: pltpu.VMEM(s, f32)

    clo = lax.ppermute(c, "space", up)
    chi = lax.ppermute(c, "space", down)
    nlo = lax.ppermute(viscosity, "space", up)
    nhi = lax.ppermute(viscosity, "space", down)

    blocks = cols // LANES
    n = 16
    forward, tau, nwin = pl.pallas_call(
        forward_kernel,
        out_shape=(shape(2, rows, cols), shape(GROUP, 2, blocks, WINDOW, LANES), shape(blocks, WINDOW, LANES)),
        in_specs=[SMEM] + [VMEM] * 6,
        out_specs=(VMEM, VMEM, VMEM),
        scratch_shapes=[
            vm(2, blocks, 128, LANES), vm(blocks, 128, LANES), vm(2, n, 8, cols), vm(2, n, 8, cols), vm(2, n, 8, cols),
            vm(4, n + 1, 8, cols), vm(4, n + 1, 8, cols),
        ],
        compiler_params=pltpu.CompilerParams(vmem_limit_bytes=LIMIT),
        name="forward",
    )(where, c, clo, chi, viscosity, nlo, nhi)

    groups = [[g * GROUP + j for j in range(GROUP)] for g in range(intervals // GROUP)]
    taus = lax.all_to_all(tau, "tm", 0, 0, axis_index_groups=groups)
    handed = lax.ppermute(forward, "tm", [(i, i + 1) for i in range(intervals - 1)])

    strips = ring * GROUP
    pieces = [jnp.zeros((2, blocks, STRIP, LANES), f32)] * 5
    corr = jnp.zeros((GROUP, 2, blocks, STRIP, LANES), f32)
    for stage in range(intervals // GROUP):
        n = 5
        corr, last = pl.pallas_call(
            functools.partial(chain_kernel, stage),
            out_shape=(shape(GROUP, 2, blocks, STRIP, LANES), shape(2, blocks, STRIP, LANES)),
            in_specs=[SMEM] + [VMEM] * 7 + [ANY],
            out_specs=(ANY, VMEM),
            scratch_shapes=[
                vm(2, blocks, WINDOW, LANES), vm(2, n, 8, cols), vm(2, n, 8, cols), vm(4, n + 1, 8, cols),
                vm(GROUP + 1, 2, blocks, STRIP, LANES), pltpu.SemaphoreType.DMA,
            ],
            input_output_aliases={8: 0},
            compiler_params=pltpu.CompilerParams(vmem_limit_bytes=LIMIT),
            name="chain%d" % stage,
        )(where, taus, nwin, *pieces, corr)
        if stage + 1 < intervals // GROUP:
            pieces = []
            for delta in (2, 1, 0, -1, -2):
                pairs = []
                for j in range(GROUP):
                    for s in range(ring):
                        to = (s * GROUP + j + delta) % strips
                        source = (stage * GROUP + j) * ring + s
                        target = ((stage + 1) * GROUP + to % GROUP) * ring + to // GROUP
                        pairs.append((source, target))
                pieces.append(lax.ppermute(last, ("tm", "space"), pairs))

    got = lax.all_to_all(corr, "tm", 0, 0, axis_index_groups=groups)
    lo = lax.ppermute(got[GROUP - 2 :], "space", up)
    hi = lax.ppermute(got[:2], "space", down)

    n = 12
    return pl.pallas_call(
        final_kernel,
        out_shape=(shape(1, 2, rows, cols),) * 3,
        in_specs=[SMEM] + [VMEM] * 10,
        out_specs=(VMEM,) * 3,
        scratch_shapes=[
            vm(2, blocks, 96, LANES), vm(blocks, 96, LANES), vm(2, n, 8, cols), vm(2, n, 8, cols), vm(4, n + 1, 8, cols),
        ],
        compiler_params=pltpu.CompilerParams(vmem_limit_bytes=LIMIT),
        name="final",
    )(where, got, lo, hi, c, clo, chi, viscosity, nlo, nhi, handed)


def solution(mesh):
    return jax.shard_map(
        shards,
        mesh=mesh,
        in_specs=(P("tm", None, "space", None), P("space", None)),
        out_specs=(P("tm", None, "space", None),) * 3,
        check_vma=False,
    )
```

time: 1130 us -> 116 us (0.10)
  the two profiles are of different devices: /device:TPU:120 before, /device:TPU:192 now
where the time goes in v1:
time: 116 us; the launch traced here: 114 us
  waiting for transfers between devices  37.6 us (32%)
  starting transfers between devices  33.8 us (29%)
  blocking collectives  23.6 us (20%)
  Pallas kernels  15.8 us (14%)
  local copies, waits for them, and re-layouts  2.6 us (2%)
    ppermute x15, waiting for transfers between devices, shards(): pieces.append(lax.ppermute(last, ('tm', 'space'), pairs))  28.1 us
    all_to_all x1, blocking collectives, shards(): taus = lax.all_to_all(tau, 'tm', 0, 0, axis_index_groups=groups)  23.6 us
    ppermute x15, starting transfers between devices, shards(): pieces.append(lax.ppermute(last, ('tm', 'space'), pairs))  13.2 us
    ppermute x1, starting transfers between devices, shards(): hi = lax.ppermute(got[:2], 'space', down)  7.4 us
    pallas_call x1, Pallas kernels, shards(): pl.pallas_call(forward_kernel, out_shape=(shape(2, rows, cols), shape(GRO...  6.88 us
    pallas_call x1, Pallas kernels, shards(): pl.pallas_call(final_kernel, out_shape=(shape(1, 2, rows, cols),) * 3, in...  5.39 us
    all_to_all x1, waiting for transfers between devices, shards(): got = lax.all_to_all(corr, 'tm', 0, 0, axis_index_groups=groups)  4.77 us
    ppermute x1, starting transfers between devices, shards(): lax.ppermute(forward, 'tm', [(i, i + 1) for i in range(intervals - 1)])  3.82 us
  transfers between devices with their start and end apart: 23, of which 7 were waited for; matrix products, arithmetic and copies ran while one was open for 0% of the time, Pallas kernels for 0%

profile of v1, /device:TPU:192, one launch (start us, length us, event | category | flops | bytes accessed | tf_op | source)
XLA Modules:
  0.0 114.4 jit_solution(8336739478978270798)
XLA Ops:
  0.6 0.0 collective-permute-start
  0.7 2.9 %collective-permute-start.1 = (f32[2,64,512]{2,1,0:T(8,128)}, f32[2,64,512]{2,1,0:T(8,128)S(1)}, u32[]{:S(2)}, u32[]{:S(2)}) collective-permute-start(f32[2,64,512]{2,1,0:T(8,128)} %bitcast.3), channel_id=1, source_target_pairs={{1,0},{2,1},{3,2},{4,3},{5,4},{6,5},{7,6},{0,7},{9,8},{10,9},{11,1... | collective-permute-start | bytes 786440 | tf_op jit(solution)/shard_map/ppermute | solution.py:281
  3.6 0.0 collective-permute-start.2
  3.6 3.0 %collective-permute-start.3 = (f32[64,512]{1,0:T(8,128)}, f32[64,512]{1,0:T(8,128)S(1)}, u32[]{:S(2)}, u32[]{:S(2)}) collective-permute-start(f32[64,512]{1,0:T(8,128)} %n_ref.3), channel_id=1, source_target_pairs={{1,0},{2,1},{3,2},{4,3},{5,4},{6,5},{7,6},{0,7},{9,8},{10,9},{11,1... | collective-permute-start | bytes 393224 | tf_op jit(solution)/shard_map/ppermute | solution.py:283
  6.6 2.9 %collective-permute-done.2.nlo_ref = f32[64,512]{1,0:T(8,128)S(1)} collective-permute-done((f32[64,512]{1,0:T(8,128)}, f32[64,512]{1,0:T(8,128)S(1)}, u32[]{:S(2)}, u32[]{:S(2)}) %collective-permute-start.2) | collective-permute-done | bytes 131104 | tf_op jit(solution)/shard_map/ppermute | solution.py:282
  9.4 0.9 copy-done
  10.4 0.9 copy-done.2
  11.3 6.9 %forward.1 = (f32[2,64,512]{2,1,0:T(8,128)S(1)}, f32[8,2,4,40,128]{4,3,2,1,0:T(8,128)S(1)}, f32[4,40,128]{2,1,0:T(8,128)S(1)}) custom-call(s32[1]{0:T(128)} %bitcast.where_ref, f32[2,64,512]{2,1,0:T(8,128)S(1)} %bitcast.4, f32[2,64,512]{2,1,0:T(8,128)S(1)} %collective-permute-done.clo_ref, f32[2,64,512]{2,1,0:T(8,128)S(1)} %collective-permute-done.1.chi_ref, ...), custom_call_target="tpu_custom_call" | custom-call | tf_op jit(solution)/shard_map/forward/pallas_call | solution.py:287
  18.2 23.6 %all_to_all.10.tau_ref = f32[8,2,4,40,128]{4,3,2,1,0:T(8,128)S(1)} all-to-all(f32[8,2,4,40,128]{4,3,2,1,0:T(8,128)S(1)} %get-tuple-element.13), channel_id=1, replica_groups={{0,8,16,24,32,40,48,56},{64,72,80,88,96,104,112,120},{128,136,144,152,1..., dimensions={0} | all-to-all | bytes 2621440 | tf_op jit(solution)/shard_map/all_to_all | solution.py:301
  41.8 0.7 broadcast_in_dim.7.corr_in
  42.5 0.7 collective-permute-start.4
  43.2 0.7 collective-permute-start.5
  43.8 0.7 collective-permute-start.6
  44.5 0.7 collective-permute-start.7
  45.2 0.7 collective-permute-start.8
  45.9 0.0 collective-permute-done.5.m1
  45.9 0.0 collective-permute-done.6.own
  45.9 0.0 collective-permute-done.8.p2
  45.9 0.7 collective-permute-start.10
  46.6 0.7 collective-permute-start.11
  47.3 0.7 collective-permute-start.12
  48.0 0.7 collective-permute-start.13
  48.6 0.7 collective-permute-start.9
  49.3 0.0 collective-permute-done.10.m1
  49.3 0.0 collective-permute-done.11.own
  49.3 0.0 collective-permute-done.13.p2
  49.3 0.0 collective-permute-done.9.m2
  49.4 0.0 copy-start.1
  49.4 0.0 copy-start.3
  49.4 1.4 %collective-permute-start.14 = (f32[2,4,8,128]{3,2,1,0:T(8,128)S(1)}, f32[2,4,8,128]{3,2,1,0:T(8,128)S(1)}, u32[]{:S(2)}, u32[]{:S(2)}) collective-permute-start(f32[2,4,8,128]{3,2,1,0:T(8,128)S(1)} %get-tuple-element.19), channel_id=1, source_target_pairs={{128,208},{129,209},{130,210},{131,211},{132,212},{133,213},{134,2... | collective-permute-start | bytes 98312 | tf_op jit(solution)/shard_map/ppermute | solution.py:332
  50.8 1.3 %collective-permute-start.15 = (f32[2,4,8,128]{3,2,1,0:T(8,128)S(1)}, f32[2,4,8,128]{3,2,1,0:T(8,128)S(1)}, u32[]{:S(2)}, u32[]{:S(2)}) collective-permute-start(f32[2,4,8,128]{3,2,1,0:T(8,128)S(1)} %get-tuple-element.19), channel_id=1, source_target_pairs={{128,200},{129,201},{130,202},{131,203},{132,204},{133,205},{134,2... | collective-permute-start | bytes 98312 | tf_op jit(solution)/shard_map/ppermute | solution.py:332
  52.1 1.3 %collective-permute-start.16 = (f32[2,4,8,128]{3,2,1,0:T(8,128)S(1)}, f32[2,4,8,128]{3,2,1,0:T(8,128)S(1)}, u32[]{:S(2)}, u32[]{:S(2)}) collective-permute-start(f32[2,4,8,128]{3,2,1,0:T(8,128)S(1)} %get-tuple-element.19), channel_id=1, source_target_pairs={{128,192},{129,193},{130,194},{131,195},{132,196},{133,197},{134,1... | collective-permute-start | bytes 98312 | tf_op jit(solution)/shard_map/ppermute | solution.py:332
  53.4 1.3 %collective-permute-start.17 = (f32[2,4,8,128]{3,2,1,0:T(8,128)S(1)}, f32[2,4,8,128]{3,2,1,0:T(8,128)S(1)}, u32[]{:S(2)}, u32[]{:S(2)}) collective-permute-start(f32[2,4,8,128]{3,2,1,0:T(8,128)S(1)} %get-tuple-element.19), channel_id=1, source_target_pairs={{128,255},{129,248},{130,249},{131,250},{132,251},{133,252},{134,2... | collective-permute-start | bytes 98312 | tf_op jit(solution)/shard_map/ppermute | solution.py:332
  54.7 1.3 %collective-permute-start.18 = (f32[2,4,8,128]{3,2,1,0:T(8,128)S(1)}, f32[2,4,8,128]{3,2,1,0:T(8,128)S(1)}, u32[]{:S(2)}, u32[]{:S(2)}) collective-permute-start(f32[2,4,8,128]{3,2,1,0:T(8,128)S(1)} %get-tuple-element.19), channel_id=1, source_target_pairs={{128,247},{129,240},{130,241},{131,242},{132,243},{133,244},{134,2... | collective-permute-start | bytes 98312 | tf_op jit(solution)/shard_map/ppermute | solution.py:332
  56.0 24.6 %collective-permute-done.14.m2 = f32[2,4,8,128]{3,2,1,0:T(8,128)S(1)} collective-permute-done((f32[2,4,8,128]{3,2,1,0:T(8,128)S(1)}, f32[2,4,8,128]{3,2,1,0:T(8,128)S(1)}, u32[]{:S(2)}, u32[]{:S(2)}) %collective-permute-start.14) | collective-permute-done | bytes 32800 | tf_op jit(solution)/shard_map/ppermute | solution.py:332
  80.7 1.2 %collective-permute-done.15.m1 = f32[2,4,8,128]{3,2,1,0:T(8,128)S(1)} collective-permute-done((f32[2,4,8,128]{3,2,1,0:T(8,128)S(1)}, f32[2,4,8,128]{3,2,1,0:T(8,128)S(1)}, u32[]{:S(2)}, u32[]{:S(2)}) %collective-permute-start.15) | collective-permute-done | bytes 32800 | tf_op jit(solution)/shard_map/ppermute | solution.py:332
  81.9 0.6 collective-permute-done.16.own
  82.5 1.6 %collective-permute-done.17.p1 = f32[2,4,8,128]{3,2,1,0:T(8,128)S(1)} collective-permute-done((f32[2,4,8,128]{3,2,1,0:T(8,128)S(1)}, f32[2,4,8,128]{3,2,1,0:T(8,128)S(1)}, u32[]{:S(2)}, u32[]{:S(2)}) %collective-permute-start.17) | collective-permute-done | bytes 32800 | tf_op jit(solution)/shard_map/ppermute | solution.py:332
  84.1 3.5 %chain3.1 = (f32[8,2,4,8,128]{4,3,2,1,0:T(8,128)}, f32[2,4,8,128]{3,2,1,0:T(8,128)}) custom-call(s32[1]{0:T(128)} %bitcast.where_ref, f32[8,2,4,40,128]{4,3,2,1,0:T(8,128)S(1)} %all_to_all.10.tau_ref, f32[4,40,128]{2,1,0:T(8,128)S(1)} %get-tuple-element.14.nwin_ref, ...), custom_call_target="tpu_custom_call", output_to_operand_aliasing={{0}: (8, {})} | custom-call | tf_op jit(solution)/shard_map/chain3/pallas_call | solution.py:309
  87.6 3.4 %all-to-all-start.1 = ((f32[8,2,4,8,128]{4,3,2,1,0:T(8,128)}), f32[8,2,4,8,128]{4,3,2,1,0:T(8,128)S(1)}, u32[]{:S(2)}, u32[]{:S(2)}) async-start(f32[8,2,4,8,128]{4,3,2,1,0:T(8,128)} %get-tuple-element.21), calls=%async_computation.1 | async-start | bytes 524288 | tf_op jit(solution)/shard_map/all_to_all | solution.py:334
  91.0 3.8 %collective-permute-start.21 = (f32[2,64,512]{2,1,0:T(8,128)S(1)}, f32[2,64,512]{2,1,0:T(8,128)S(1)}, u32[]{:S(2)}, u32[]{:S(2)}) collective-permute-start(f32[2,64,512]{2,1,0:T(8,128)S(1)} %get-tuple-element.22), channel_id=1, source_target_pairs={{0,8},{8,16},{16,24},{24,32},{32,40},{40,48},{48,56},{56,64},{64,7... | collective-permute-start | bytes 786440 | tf_op jit(solution)/shard_map/ppermute | solution.py:302
  94.8 4.8 %all-to-all-done.1.got_ref = f32[8,2,4,8,128]{4,3,2,1,0:T(8,128)S(1)} async-done(((f32[8,2,4,8,128]{4,3,2,1,0:T(8,128)}), f32[8,2,4,8,128]{4,3,2,1,0:T(8,128)S(1)}, u32[]{:S(2)}, u32[]{:S(2)}) %all-to-all-start.1) | async-done | bytes 262176 | tf_op jit(solution)/shard_map/all_to_all | solution.py:334
  99.6 0.0 collective-permute-start.19
  99.6 7.4 %collective-permute-start.20 = (f32[2,2,4,8,128]{4,3,2,1,0:T(8,128)S(1)}, f32[2,2,4,8,128]{4,3,2,1,0:T(8,128)S(1)}, u32[]{:S(2)}, u32[]{:S(2)}) collective-permute-start(f32[2,2,4,8,128]{4,3,2,1,0:T(8,128)S(1)} %get-tuple-element.23), channel_id=1, source_target_pairs={{1,0},{2,1},{3,2},{4,3},{5,4},{6,5},{7,6},{0,7},{9,8},{10,9},{11,1... | collective-permute-start | bytes 196616 | tf_op jit(solution)/shard_map/ppermute | solution.py:336
  107.0 0.0 collective-permute-done.21.handed_ref
  107.0 1.9 %collective-permute-done.19.lo_ref = f32[2,2,4,8,128]{4,3,2,1,0:T(8,128)S(1)} collective-permute-done((f32[2,2,4,8,128]{4,3,2,1,0:T(8,128)S(1)}, f32[2,2,4,8,128]{4,3,2,1,0:T(8,128)S(1)}, u32[]{:S(2)}, u32[]{:S(2)}) %collective-permute-start.19) | collective-permute-done | bytes 65568 | tf_op jit(solution)/shard_map/ppermute | solution.py:335
  109.0 0.0 collective-permute-done.20.hi_ref
  109.0 5.4 %final.1 = (f32[1,2,64,512]{3,2,1,0:T(8,128)}, f32[1,2,64,512]{3,2,1,0:T(8,128)}, f32[1,2,64,512]{3,2,1,0:T(8,128)}) custom-call(s32[1]{0:T(128)} %bitcast.where_ref, f32[8,2,4,8,128]{4,3,2,1,0:T(8,128)S(1)} %all-to-all-done.1.got_ref, f32[2,2,4,8,128]{4,3,2,1,0:T(8,128)S(1)} %collective-permute-done.19.lo_ref, ...), custom_call_target="tpu_custom_call" | custom-call | tf_op jit(solution)/shard_map/final/pallas_call | solution.py:339
  (16 shorter events, 0.1 us)
Async XLA Ops:
  0.6 8.8 %collective-permute-start = (f32[2,64,512]{2,1,0:T(8,128)}, f32[2,64,512]{2,1,0:T(8,128)S(1)}, u32[]{:S(2)}, u32[]{:S(2)}) collective-permute-start(f32[2,64,512]{2,1,0:T(8,128)} %bitcast.2), channel_id=1, source_target_pairs={{0,1},{1,2},{2,3},{3,4},{4,5},{5,6},{6,7},{7,0},{8,9},{9,10},{10,1... | collective-permute-start | bytes 786440 | tf_op jit(solution)/shard_map/ppermute | solution.py:280
  0.7 8.8 %collective-permute-start.1 = (f32[2,64,512]{2,1,0:T(8,128)}, f32[2,64,512]{2,1,0:T(8,128)S(1)}, u32[]{:S(2)}, u32[]{:S(2)}) collective-permute-start(f32[2,64,512]{2,1,0:T(8,128)} %bitcast.3), channel_id=1, source_target_pairs={{1,0},{2,1},{3,2},{4,3},{5,4},{6,5},{7,6},{0,7},{9,8},{10,9},{11,1... | collective-permute-start | bytes 786440 | tf_op jit(solution)/shard_map/ppermute | solution.py:281
  3.6 5.8 %collective-permute-start.2 = (f32[64,512]{1,0:T(8,128)}, f32[64,512]{1,0:T(8,128)S(1)}, u32[]{:S(2)}, u32[]{:S(2)}) collective-permute-start(f32[64,512]{1,0:T(8,128)} %n_ref.3), channel_id=1, source_target_pairs={{0,1},{1,2},{2,3},{3,4},{4,5},{5,6},{6,7},{7,0},{8,9},{9,10},{10,1... | collective-permute-start | bytes 393224 | tf_op jit(solution)/shard_map/ppermute | solution.py:282
  3.6 5.8 %collective-permute-start.3 = (f32[64,512]{1,0:T(8,128)}, f32[64,512]{1,0:T(8,128)S(1)}, u32[]{:S(2)}, u32[]{:S(2)}) collective-permute-start(f32[64,512]{1,0:T(8,128)} %n_ref.3), channel_id=1, source_target_pairs={{1,0},{2,1},{3,2},{4,3},{5,4},{6,5},{7,6},{0,7},{9,8},{10,9},{11,1... | collective-permute-start | bytes 393224 | tf_op jit(solution)/shard_map/ppermute | solution.py:283
  9.4 1.0 copy-start
  10.4 0.9 copy-start.2
  42.5 3.4 %collective-permute-start.4 = (f32[2,4,8,128]{3,2,1,0:T(8,128)S(1)}, f32[2,4,8,128]{3,2,1,0:T(8,128)S(1)}, u32[]{:S(2)}, u32[]{:S(2)}) collective-permute-start(f32[2,4,8,128]{3,2,1,0:T(8,128)S(1)} %get-tuple-element.15), channel_id=1, source_target_pairs={{0,80},{1,81},{2,82},{3,83},{4,84},{5,85},{6,86},{7,87},{8,88},{9,... | collective-permute-start | bytes 98312 | tf_op jit(solution)/shard_map/ppermute | solution.py:332
  43.2 2.7 %collective-permute-start.5 = (f32[2,4,8,128]{3,2,1,0:T(8,128)S(1)}, f32[2,4,8,128]{3,2,1,0:T(8,128)S(1)}, u32[]{:S(2)}, u32[]{:S(2)}) collective-permute-start(f32[2,4,8,128]{3,2,1,0:T(8,128)S(1)} %get-tuple-element.15), channel_id=1, source_target_pairs={{0,72},{1,73},{2,74},{3,75},{4,76},{5,77},{6,78},{7,79},{8,80},{9,... | collective-permute-start | bytes 98312 | tf_op jit(solution)/shard_map/ppermute | solution.py:332
  43.8 2.0 %collective-permute-start.6 = (f32[2,4,8,128]{3,2,1,0:T(8,128)S(1)}, f32[2,4,8,128]{3,2,1,0:T(8,128)S(1)}, u32[]{:S(2)}, u32[]{:S(2)}) collective-permute-start(f32[2,4,8,128]{3,2,1,0:T(8,128)S(1)} %get-tuple-element.15), channel_id=1, source_target_pairs={{0,64},{1,65},{2,66},{3,67},{4,68},{5,69},{6,70},{7,71},{8,72},{9,... | collective-permute-start | bytes 98312 | tf_op jit(solution)/shard_map/ppermute | solution.py:332
  44.5 1.4 %collective-permute-start.7 = (f32[2,4,8,128]{3,2,1,0:T(8,128)S(1)}, f32[2,4,8,128]{3,2,1,0:T(8,128)S(1)}, u32[]{:S(2)}, u32[]{:S(2)}) collective-permute-start(f32[2,4,8,128]{3,2,1,0:T(8,128)S(1)} %get-tuple-element.15), channel_id=1, source_target_pairs={{0,127},{1,120},{2,121},{3,122},{4,123},{5,124},{6,125},{7,126},{8... | collective-permute-start | bytes 98312 | tf_op jit(solution)/shard_map/ppermute | solution.py:332
  45.2 0.7 collective-permute-start.8
  45.9 3.4 %collective-permute-start.10 = (f32[2,4,8,128]{3,2,1,0:T(8,128)S(1)}, f32[2,4,8,128]{3,2,1,0:T(8,128)S(1)}, u32[]{:S(2)}, u32[]{:S(2)}) collective-permute-start(f32[2,4,8,128]{3,2,1,0:T(8,128)S(1)} %get-tuple-element.17), channel_id=1, source_target_pairs={{64,136},{65,137},{66,138},{67,139},{68,140},{69,141},{70,142},{71... | collective-permute-start | bytes 98312 | tf_op jit(solution)/shard_map/ppermute | solution.py:332
  46.6 2.7 %collective-permute-start.11 = (f32[2,4,8,128]{3,2,1,0:T(8,128)S(1)}, f32[2,4,8,128]{3,2,1,0:T(8,128)S(1)}, u32[]{:S(2)}, u32[]{:S(2)}) collective-permute-start(f32[2,4,8,128]{3,2,1,0:T(8,128)S(1)} %get-tuple-element.17), channel_id=1, source_target_pairs={{64,128},{65,129},{66,130},{67,131},{68,132},{69,133},{70,134},{71... | collective-permute-start | bytes 98312 | tf_op jit(solution)/shard_map/ppermute | solution.py:332
  47.3 2.0 %collective-permute-start.12 = (f32[2,4,8,128]{3,2,1,0:T(8,128)S(1)}, f32[2,4,8,128]{3,2,1,0:T(8,128)S(1)}, u32[]{:S(2)}, u32[]{:S(2)}) collective-permute-start(f32[2,4,8,128]{3,2,1,0:T(8,128)S(1)} %get-tuple-element.17), channel_id=1, source_target_pairs={{64,191},{65,184},{66,185},{67,186},{68,187},{69,188},{70,189},{71... | collective-permute-start | bytes 98312 | tf_op jit(solution)/shard_map/ppermute | solution.py:332
  48.0 1.4 %collective-permute-start.13 = (f32[2,4,8,128]{3,2,1,0:T(8,128)S(1)}, f32[2,4,8,128]{3,2,1,0:T(8,128)S(1)}, u32[]{:S(2)}, u32[]{:S(2)}) collective-permute-start(f32[2,4,8,128]{3,2,1,0:T(8,128)S(1)} %get-tuple-element.17), channel_id=1, source_target_pairs={{64,183},{65,176},{66,177},{67,178},{68,179},{69,180},{70,181},{71... | collective-permute-start | bytes 98312 | tf_op jit(solution)/shard_map/ppermute | solution.py:332
  48.6 0.7 collective-permute-start.9
  49.4 59.6 %copy-start.1 = (f32[1,2,64,512]{3,2,1,0:T(8,128)S(1)}, f32[1,2,64,512]{3,2,1,0:T(8,128)}, u32[]{:S(2)}) copy-start(f32[1,2,64,512]{3,2,1,0:T(8,128)} %param.2) | copy-start | bytes 786436
  49.4 59.6 %copy-start.3 = (f32[64,512]{1,0:T(8,128)S(1)}, f32[64,512]{1,0:T(8,128)}, u32[]{:S(2)}) copy-start(f32[64,512]{1,0:T(8,128)} %n_ref.3) | copy-start | bytes 393220
  49.4 31.3 %collective-permute-start.14 = (f32[2,4,8,128]{3,2,1,0:T(8,128)S(1)}, f32[2,4,8,128]{3,2,1,0:T(8,128)S(1)}, u32[]{:S(2)}, u32[]{:S(2)}) collective-permute-start(f32[2,4,8,128]{3,2,1,0:T(8,128)S(1)} %get-tuple-element.19), channel_id=1, source_target_pairs={{128,208},{129,209},{130,210},{131,211},{132,212},{133,213},{134,2... | collective-permute-start | bytes 98312 | tf_op jit(solution)/shard_map/ppermute | solution.py:332
  50.8 31.0 %collective-permute-start.15 = (f32[2,4,8,128]{3,2,1,0:T(8,128)S(1)}, f32[2,4,8,128]{3,2,1,0:T(8,128)S(1)}, u32[]{:S(2)}, u32[]{:S(2)}) collective-permute-start(f32[2,4,8,128]{3,2,1,0:T(8,128)S(1)} %get-tuple-element.19), channel_id=1, source_target_pairs={{128,200},{129,201},{130,202},{131,203},{132,204},{133,205},{134,2... | collective-permute-start | bytes 98312 | tf_op jit(solution)/shard_map/ppermute | solution.py:332
  52.1 30.4 %collective-permute-start.16 = (f32[2,4,8,128]{3,2,1,0:T(8,128)S(1)}, f32[2,4,8,128]{3,2,1,0:T(8,128)S(1)}, u32[]{:S(2)}, u32[]{:S(2)}) collective-permute-start(f32[2,4,8,128]{3,2,1,0:T(8,128)S(1)} %get-tuple-element.19), channel_id=1, source_target_pairs={{128,192},{129,193},{130,194},{131,195},{132,196},{133,197},{134,1... | collective-permute-start | bytes 98312 | tf_op jit(solution)/shard_map/ppermute | solution.py:332
  53.4 30.6 %collective-permute-start.17 = (f32[2,4,8,128]{3,2,1,0:T(8,128)S(1)}, f32[2,4,8,128]{3,2,1,0:T(8,128)S(1)}, u32[]{:S(2)}, u32[]{:S(2)}) collective-permute-start(f32[2,4,8,128]{3,2,1,0:T(8,128)S(1)} %get-tuple-element.19), channel_id=1, source_target_pairs={{128,255},{129,248},{130,249},{131,250},{132,251},{133,252},{134,2... | collective-permute-start | bytes 98312 | tf_op jit(solution)/shard_map/ppermute | solution.py:332
  54.7 29.3 %collective-permute-start.18 = (f32[2,4,8,128]{3,2,1,0:T(8,128)S(1)}, f32[2,4,8,128]{3,2,1,0:T(8,128)S(1)}, u32[]{:S(2)}, u32[]{:S(2)}) collective-permute-start(f32[2,4,8,128]{3,2,1,0:T(8,128)S(1)} %get-tuple-element.19), channel_id=1, source_target_pairs={{128,247},{129,240},{130,241},{131,242},{132,243},{133,244},{134,2... | collective-permute-start | bytes 98312 | tf_op jit(solution)/shard_map/ppermute | solution.py:332
  87.6 12.0 %all-to-all-start.1 = ((f32[8,2,4,8,128]{4,3,2,1,0:T(8,128)}), f32[8,2,4,8,128]{4,3,2,1,0:T(8,128)S(1)}, u32[]{:S(2)}, u32[]{:S(2)}) async-start(f32[8,2,4,8,128]{4,3,2,1,0:T(8,128)} %get-tuple-element.21), calls=%async_computation.1 | async-start | bytes 524288 | tf_op jit(solution)/shard_map/all_to_all | solution.py:334
  91.0 16.0 %collective-permute-start.21 = (f32[2,64,512]{2,1,0:T(8,128)S(1)}, f32[2,64,512]{2,1,0:T(8,128)S(1)}, u32[]{:S(2)}, u32[]{:S(2)}) collective-permute-start(f32[2,64,512]{2,1,0:T(8,128)S(1)} %get-tuple-element.22), channel_id=1, source_target_pairs={{0,8},{8,16},{16,24},{24,32},{32,40},{40,48},{48,56},{56,64},{64,7... | collective-permute-start | bytes 786440 | tf_op jit(solution)/shard_map/ppermute | solution.py:302
  99.6 9.4 %collective-permute-start.19 = (f32[2,2,4,8,128]{4,3,2,1,0:T(8,128)S(1)}, f32[2,2,4,8,128]{4,3,2,1,0:T(8,128)S(1)}, u32[]{:S(2)}, u32[]{:S(2)}) collective-permute-start(f32[2,2,4,8,128]{4,3,2,1,0:T(8,128)S(1)} %get-tuple-element.24), channel_id=1, source_target_pairs={{0,1},{1,2},{2,3},{3,4},{4,5},{5,6},{6,7},{7,0},{8,9},{9,10},{10,1... | collective-permute-start | bytes 196616 | tf_op jit(solution)/shard_map/ppermute | solution.py:335
  99.6 9.3 %collective-permute-start.20 = (f32[2,2,4,8,128]{4,3,2,1,0:T(8,128)S(1)}, f32[2,2,4,8,128]{4,3,2,1,0:T(8,128)S(1)}, u32[]{:S(2)}, u32[]{:S(2)}) collective-permute-start(f32[2,2,4,8,128]{4,3,2,1,0:T(8,128)S(1)} %get-tuple-element.23), channel_id=1, source_target_pairs={{1,0},{2,1},{3,2},{4,3},{5,4},{6,5},{7,6},{0,7},{9,8},{10,9},{11,1... | collective-permute-start | bytes 196616 | tf_op jit(solution)/shard_map/ppermute | solution.py:336

commit v2 on v1

v2 whole, which is shorter than its diff:
```python
import functools

import jax
import jax.numpy as jnp
from jax import lax
from jax.experimental import pallas as pl
from jax.experimental.pallas import tpu as pltpu
from jax.sharding import PartitionSpec as P

STEPS = 8
GROUP = 8
STRIP = 16
HALO = 16
EDGE = 32
WINDOW = STRIP + 2 * HALO
LANES = 128
SPLIT = 4
advect_scale = 0.1
coarse_size = 1.0
COARSE = 0.5 * advect_scale * coarse_size
FINE = COARSE / STEPS
f32 = jnp.float32


def shift_up(plane):
    return pltpu.roll(plane, 1, 0)


def shift_down(plane):
    return pltpu.roll(plane, plane.shape[0] - 1, 0)


def left_of(x):
    return pltpu.roll(x, 1, 1)


def right_of(x):
    return pltpu.roll(x, x.shape[1] - 1, 1)


def make_coefs(planes, size, coef):
    cx, cyp, cym, dd = coef
    n = len(planes)
    faces = []
    for i in range(n):
        below = planes[i + 1] if i + 1 < n else shift_down(planes[0])
        faces.append((0.5 * size) * (planes[i] + below))
    first = shift_up(faces[n - 1])
    cx[0] = first
    for i in range(n):
        cx[i + 1] = faces[i]
        nyp = (0.5 * size) * (planes[i] + right_of(planes[i]))
        nym = left_of(nyp)
        cyp[i] = nyp
        cym[i] = nym
        nxm = faces[i - 1] if i > 0 else first
        dd[i] = 1.0 - ((faces[i] + nxm) + (nyp + nym))


def euler(src, coef, n, emit):
    cx, cyp, cym, dd = coef
    above = [shift_up(src[c, n - 1]) for c in range(2)]
    here = [src[c, 0] for c in range(2)]
    first = here
    for i in range(n):
        if i + 1 < n:
            below = [src[c, i + 1] for c in range(2)]
        else:
            below = [shift_down(first[c]) for c in range(2)]
        wxp = cx[i + 1] - here[0]
        wxm = cx[i] + here[0]
        wyp = cyp[i] - here[1]
        wym = cym[i] + here[1]
        d = dd[i]
        res = []
        for c in range(2):
            f = here[c]
            res.append(
                (d * f + (wxp * below[c] + wxm * above[c]))
                + (wyp * right_of(f) + wym * left_of(f))
            )
        emit(i, res)
        above, here = here, below


def heun(src, mid, dst, coef, n, extra=None):
    def to_mid(i, res):
        for c in range(2):
            mid[c, i] = res[c]

    euler(src, coef, n, to_mid)

    def to_dst(i, res):
        for c in range(2):
            out = 0.5 * (src[c, i] + res[c])
            if extra is not None:
                out = out + extra(c, i)
            dst[c, i] = out

    euler(mid, coef, n, to_dst)


def plane(nat, i, n):
    return jnp.concatenate([nat[b, pl.ds(i, 8, stride=n), :] for b in range(nat.shape[0])], axis=1)


def put_plane(nat, i, n, value):
    for b in range(nat.shape[0]):
        nat[b, pl.ds(i, 8, stride=n), :] = value[:, b * LANES : (b + 1) * LANES]


def load_planes(nat, n):
    return [plane(nat, i, n) for i in range(n)]


def copies(pairs, sem):
    started = [pltpu.make_async_copy(a, b, sem.at[i]) for i, (a, b) in enumerate(pairs)]
    for copy in started:
        copy.start()
    return started


def edges_kernel(c_ref, n_ref, top_ref, bottom_ref, held, sem):
    rows = n_ref.shape[0]
    pairs, later = [], []
    for k, (out, start) in enumerate(((top_ref, 0), (bottom_ref, rows - EDGE))):
        pairs.append((c_ref.at[0, :, pl.ds(start, EDGE), :], held.at[k, pl.ds(0, 2)]))
        pairs.append((n_ref.at[pl.ds(start, EDGE), :], held.at[k, 2]))
        later += [(held.at[k, pl.ds(0, 2)], out.at[pl.ds(0, 2)]), (held.at[k, 2], out.at[2])]
    started = copies(pairs, sem)
    sent = []
    for i, copy in enumerate(started):
        copy.wait()
        sent += copies([later[i]], sem.at[pl.ds(4 + i, 1)])
    for copy in sent:
        copy.wait()


def load_kernel(c_ref, n_ref, out_ref, sem):
    pairs = [(c_ref.at[0], out_ref.at[pl.ds(0, 2)]), (n_ref, out_ref.at[2])]
    for copy in copies(pairs, sem):
        copy.wait()


def cut(b):
    return pl.ds(b * LANES, LANES)


def forward_kernel(where_ref, own_ref, lo_ref, hi_ref,
                   fwd_ref, tau_ref, nwin_ref,
                   nat, fnat, w, mid, tau, cf, cc, sem):
    n = 16
    blocks = nat.shape[1]
    rows = own_ref.shape[1]
    pairs = []
    for b in range(blocks):
        mine = pl.ds(EDGE, rows)
        pairs.append((own_ref.at[2, :, cut(b)], nat.at[2, b, mine, :]))
        pairs.append((lo_ref.at[2, :, cut(b)], nat.at[2, b, pl.ds(0, EDGE), :]))
        pairs.append((hi_ref.at[2, :, cut(b)], nat.at[2, b, pl.ds(EDGE + rows, EDGE), :]))
    for b in range(blocks):
        both = pl.ds(0, 2)
        pairs.append((own_ref.at[both, :, cut(b)], nat.at[both, b, mine, :]))
        pairs.append((lo_ref.at[both, :, cut(b)], nat.at[both, b, pl.ds(0, EDGE), :]))
        pairs.append((hi_ref.at[both, :, cut(b)], nat.at[both, b, pl.ds(EDGE + rows, EDGE), :]))
    started = copies(pairs, sem)
    for copy in started[: 3 * blocks]:
        copy.wait()
    position = where_ref[0]
    vnat = nat.at[2]
    start = pl.multiple_of(lax.rem(position, SPLIT) * STRIP + HALO, 8)
    nwin_ref[...] = nat[2, :, pl.ds(start, WINDOW), :]
    visc = load_planes(vnat, n)
    coef_c = [cc.at[i] for i in range(4)]
    coef_f = [cf.at[i] for i in range(4)]
    make_coefs(visc, coarse_size, coef_c)
    make_coefs(visc, coarse_size / STEPS, coef_f)
    for copy in started[3 * blocks :]:
        copy.wait()
    for c in range(2):
        for i in range(n):
            w[c, i] = COARSE * plane(nat.at[c], i, n)
    heun(w, mid, tau, coef_c, n)
    for c in range(2):
        for i in range(n):
            w[c, i] = w[c, i] * (FINE / COARSE)

    def step(_, carry):
        heun(w, mid, w, coef_f, n)
        return carry

    lax.fori_loop(0, STEPS, step, 0)
    keep = jnp.where(position == 0, 0.0, 1.0).astype(f32)
    for c in range(2):
        for i in range(n):
            end = w[c, i] * (COARSE / FINE)
            put_plane(nat.at[c], i, n, end - keep * tau[c, i])
            put_plane(fnat.at[c], i, n, end * (1.0 / COARSE))
    pairs = []
    for b in range(blocks):
        both = pl.ds(0, 2)
        pairs.append((fnat.at[both, b, pl.ds(EDGE, rows), :], fwd_ref.at[both, :, cut(b)]))
    started = copies(pairs, sem)
    for c in range(2):
        for p in range(GROUP):
            at = EDGE - HALO + (p % SPLIT) * STRIP
            tau_ref[p, c] = nat[c, :, at : at + WINDOW, :]
    for copy in started:
        copy.wait()


def chain_kernel(stage, stages, *refs):
    refs = list(refs)
    where_ref, tau_ref, nwin_ref = refs[:3]
    pieces = refs[3:6] if stage > 0 else None
    scratch = refs[-6:]
    nat, w, mid, cc, part, sem = scratch
    corr_ref, last_ref = refs[-8:-6]
    n = WINDOW // 8
    position = where_ref[0]
    planes = GROUP // SPLIT

    @pl.when(position // SPLIT == (stage + 1) * planes - 1)
    def _():
        coef = [cc.at[i] for i in range(4)]
        make_coefs(load_planes(nwin_ref, n), coarse_size, coef)

        def keep(t):
            for c in range(2):
                for i in range(n):
                    put_plane(nat.at[c], i, n, w[c, i])
                part[t, c] = nat[c, :, HALO : HALO + STRIP, :]

        def one(t):
            heun(w, mid, w, coef, n, lambda c, i: plane(tau_ref.at[t, c], i, n))
            keep(t + 1)

        if stage == 0:
            for c in range(2):
                part[0, c] = jnp.zeros_like(part[0, c])
                for i in range(n):
                    w[c, i] = plane(tau_ref.at[0, c], i, n)
            keep(1)
        else:
            for c in range(2):
                for k, ref in enumerate(pieces):
                    nat[c, :, k * STRIP : (k + 1) * STRIP, :] = ref[c]
                part[0, c] = pieces[1][c]
                for i in range(n):
                    w[c, i] = plane(nat.at[c], i, n)
            one(0)

        def step(t, carry):
            one(t)
            return carry

        lax.fori_loop(1, GROUP - 1, step, 0)
        copy = pltpu.make_async_copy(part.at[pl.ds(0, GROUP)], corr_ref, sem)
        copy.start()
        if stage + 1 < stages:
            one(GROUP - 1)
            last_ref[...] = part[GROUP]
        copy.wait()


def final_kernel(where_ref, got_ref, lo_ref, hi_ref, c_ref, clo_ref, chi_ref,
                 n_ref, handed_ref, handed2_ref,
                 corr_ref, adv_ref, defect_ref,
                 nat, vnat, anat, dbuf, w, mid, cf, sem):
    n = 12
    rows = n_ref.shape[0]
    blocks = nat.shape[1]
    position = where_ref[0]
    for b in range(blocks):
        vnat[b, 0:HALO, :] = clo_ref[2, EDGE - HALO :, b * LANES : (b + 1) * LANES]
        vnat[b, HALO : HALO + rows, :] = n_ref[:, b * LANES : (b + 1) * LANES]
        vnat[b, HALO + rows :, :] = chi_ref[2, 0:HALO, b * LANES : (b + 1) * LANES]
    coef = [cf.at[i] for i in range(4)]
    make_coefs(load_planes(vnat, n), coarse_size / STEPS, coef)

    @pl.when(position == 0)
    def _():
        for c in range(2):
            dbuf[c] = jnp.zeros_like(dbuf[c])
            for b in range(blocks):
                own = slice(b * LANES, (b + 1) * LANES)
                nat[c, b, 0:HALO, :] = clo_ref[c, EDGE - HALO :, own]
                nat[c, b, HALO : HALO + rows, :] = c_ref[0, c, :, own]
                nat[c, b, HALO + rows :, :] = chi_ref[c, 0:HALO, own]

    @pl.when(position != 0)
    def _():
        back = 1.0 / COARSE
        for c in range(2):
            dbuf[c] = (handed_ref[c] + handed2_ref[c]) - c_ref[0, c]
            nat[c, :, 0:HALO, :] = back * lo_ref[c]
            nat[c, :, HALO + rows :, :] = back * hi_ref[c]
            for q in range(SPLIT):
                at = HALO + q * STRIP
                nat[c, :, at : at + STRIP, :] = back * got_ref[GROUP - SPLIT + q, c]

    both = pl.ds(0, 2)
    mine = pl.ds(HALO, rows)
    pairs = [(dbuf, defect_ref.at[0])]
    for b in range(blocks):
        pairs.append((nat.at[both, b, mine, :], corr_ref.at[0, both, :, cut(b)]))
    started = copies(pairs, sem)
    for c in range(2):
        for i in range(n):
            w[c, i] = FINE * plane(nat.at[c], i, n)

    def step(_, carry):
        heun(w, mid, w, coef, n)
        return carry

    lax.fori_loop(0, STEPS, step, 0)
    for c in range(2):
        for i in range(n):
            put_plane(anat.at[c], i, n, w[c, i] * (1.0 / FINE))
    pairs = []
    for b in range(blocks):
        pairs.append((anat.at[both, b, mine, :], adv_ref.at[0, both, :, cut(b)]))
    started += copies(pairs, sem.at[pl.ds(1 + blocks, blocks)])
    for copy in started:
        copy.wait()


VMEM = pl.BlockSpec(memory_space=pltpu.VMEM)
SMEM = pl.BlockSpec(memory_space=pltpu.SMEM)
ANY = pl.BlockSpec(memory_space=pl.ANY)
HBM = pl.BlockSpec(memory_space=pltpu.HBM)
FULL = pltpu.CompilerParams(vmem_limit_bytes=63 * 1024 * 1024)
PARAMS = pltpu.CompilerParams(vmem_limit_bytes=48 * 1024 * 1024)


def shards(c_values, viscosity):
    _, _, rows, cols = c_values.shape
    blocks = cols // LANES
    ring = lax.axis_size("space")
    intervals = lax.axis_size("tm")
    stages = intervals // GROUP
    up = [(i, (i + 1) % ring) for i in range(ring)]
    down = [(b, a) for a, b in up]
    where = lax.axis_index("tm").reshape(1).astype(jnp.int32)
    shape = lambda *s: jax.ShapeDtypeStruct(s, f32)
    vm = lambda *s: pltpu.VMEM(s, f32)
    dma = lambda k: pltpu.SemaphoreType.DMA((k,))

    top, bottom = pl.pallas_call(
        edges_kernel,
        out_shape=(shape(3, EDGE, cols),) * 2,
        in_specs=[HBM] * 2,
        out_specs=(ANY,) * 2,
        scratch_shapes=[vm(2, 3, EDGE, cols), dma(8)],
        compiler_params=FULL,
        name="edges",
    )(c_values, viscosity)
    own = pl.pallas_call(
        load_kernel,
        out_shape=shape(3, rows, cols),
        in_specs=[ANY] * 2,
        out_specs=ANY,
        scratch_shapes=[dma(2)],
        compiler_params=PARAMS,
        cost_estimate=pl.CostEstimate(flops=0, bytes_accessed=6 * rows * cols * 4, transcendentals=0),
        name="load",
    )(c_values, viscosity)
    lo = lax.ppermute(bottom, "space", up)
    hi = lax.ppermute(top, "space", down)

    n = 16
    forward, tau, nwin = pl.pallas_call(
        forward_kernel,
        out_shape=(shape(2, rows, cols), shape(GROUP, 2, blocks, WINDOW, LANES), shape(blocks, WINDOW, LANES)),
        in_specs=[SMEM, ANY, ANY, ANY],
        out_specs=(HBM, VMEM, VMEM),
        scratch_shapes=[
            vm(3, blocks, 128, LANES), vm(2, blocks, 128, LANES),
            vm(2, n, 8, cols), vm(2, n, 8, cols), vm(2, n, 8, cols),
            vm(4, n + 1, 8, cols), vm(4, n + 1, 8, cols), dma(6 * blocks),
        ],
        compiler_params=PARAMS,
        name="forward",
    )(where, own, lo, hi)

    groups = [[g * GROUP + j for j in range(GROUP)] for g in range(stages)]
    taus = lax.all_to_all(tau, "tm", 0, 0, axis_index_groups=groups)

    strips = ring * SPLIT
    n = WINDOW // 8
    pieces, corr, handed = [], [], []
    for stage in range(stages):
        extra = {0: [forward], 1: handed, stages - 2: [forward], stages - 1: handed}[stage]
        carries = stage in (0, stages - 2)
        count = 3 + len(pieces)
        aliases = {count: 1} if stage > 0 else {}
        if carries:
            aliases[count + len(corr)] = 0
        kept = shape(2, rows, cols) if carries else shape(8, LANES)
        done = pl.pallas_call(
            functools.partial(chain_kernel, stage, stages),
            out_shape=(kept, shape(GROUP, 2, blocks, STRIP, LANES), shape(2, blocks, STRIP, LANES)),
            in_specs=[SMEM] + [VMEM] * (count - 1) + [ANY] * len(corr) + [HBM] * len(extra),
            out_specs=(HBM, ANY, VMEM),
            scratch_shapes=[
                vm(2, blocks, WINDOW, LANES), vm(2, n, 8, cols), vm(2, n, 8, cols), vm(4, n + 1, 8, cols),
                vm(GROUP + 1, 2, blocks, STRIP, LANES), pltpu.SemaphoreType.DMA,
            ],
            input_output_aliases=aliases,
            compiler_params=PARAMS,
            name="chain%d" % stage,
        )(where, taus, nwin, *pieces, *corr, *extra)
        corr, last = [done[1]], done[2]
        if carries:
            forward = done[0]
            chain = [g * GROUP + GROUP - 1 - q for g in range(2) for q in range(SPLIT)]
            pairs = [(i, i + 1) for i in range(intervals - 1) if (i in chain or i + 1 in chain) == (stage > 0)]
            handed = handed + [lax.ppermute(forward, "tm", pairs)]
        if stage + 1 < stages:
            pieces = []
            for delta in (1, 0, -1):
                pairs = []
                for strip in range(strips):
                    to = (strip + delta) % strips
                    source = stage * GROUP + GROUP - SPLIT + strip % SPLIT
                    target = (stage + 1) * GROUP + GROUP - SPLIT + to % SPLIT
                    pairs.append((source * ring + strip // SPLIT, target * ring + to // SPLIT))
                pieces.append(lax.ppermute(last, ("tm", "space"), pairs))

    got = lax.all_to_all(corr[0], "tm", 0, 0, axis_index_groups=groups)
    above = lax.ppermute(got[GROUP - 1], "space", up)
    below = lax.ppermute(got[GROUP - SPLIT], "space", down)

    n = 12
    return pl.pallas_call(
        final_kernel,
        out_shape=(shape(1, 2, rows, cols),) * 3,
        in_specs=[SMEM] + [VMEM] * 9,
        out_specs=(ANY,) * 3,
        scratch_shapes=[
            vm(2, blocks, 96, LANES), vm(blocks, 96, LANES), vm(2, blocks, 96, LANES), vm(2, rows, cols),
            vm(2, n, 8, cols), vm(2, n, 8, cols), vm(4, n + 1, 8, cols), dma(1 + 2 * blocks),
        ],
        compiler_params=PARAMS,
        name="final",
    )(where, got, above, below, c_values, lo, hi, viscosity, *handed)


def solution(mesh):
    return jax.shard_map(
        shards,
        mesh=mesh,
        in_specs=(P("tm", None, "space", None), P("space", None)),
        out_specs=(P("tm", None, "space", None),) * 3,
        check_vma=False,
    )
```

time: 116 us -> 105 us (0.905); the launches traced: 114 us -> 105 us
  blocking collectives: 23.6 us -> 61.6 us
  waiting for transfers between devices: 37.6 us -> 12.3 us
  starting transfers between devices: 33.8 us -> 12.3 us
    all_to_all x0 -> x1, blocking collectives: none -> 35.1 us  [shards(): got = lax.all_to_all(corr[0], 'tm', 0, 0, axis_index_groups=groups)]
    ppermute x15 -> x9, waiting for transfers between devices: 28.1 us -> 0.02 us  [shards(): pieces.append(lax.ppermute(last, ('tm', 'space'), pairs))]
    ppermute x7 -> x6, starting transfers between devices: 17.2 us -> 6.33 us  [the longest x1 2.94 us: shards(): hi = lax.ppermute(top, 'space', down)]
    ppermute x7 -> x6, waiting for transfers between devices: 4.79 us -> 12.2 us  [the longest x2 6.34 us: shards(): handed = handed + [lax.ppermute(forward, 'tm', pairs)]]
    ppermute x15 -> x9, starting transfers between devices: 13.2 us -> 5.98 us  [shards(): pieces.append(lax.ppermute(last, ('tm', 'space'), pairs))]
    all_to_all x1 -> x0, waiting for transfers between devices: 4.77 us -> none  [shards(): got = lax.all_to_all(corr, 'tm', 0, 0, axis_index_groups=groups)]
    all_to_all x1 -> x0, starting transfers between devices: 3.42 us -> none  [shards(): got = lax.all_to_all(corr, 'tm', 0, 0, axis_index_groups=groups)]
    all_to_all x1, blocking collectives: 23.6 us -> 26.5 us  [shards(): taus = lax.all_to_all(tau, 'tm', 0, 0, axis_index_groups=groups)]
  transfers between devices with their start and end apart: 23 -> 15, of which waited for: 7 -> 4; matrix products, arithmetic and copies ran while one was open for 0% -> 0% of each run, Pallas kernels for 0% -> 0%
where the time goes in v2:
time: 105 us
  blocking collectives  61.6 us (59%)
  Pallas kernels  15.7 us (15%)
  starting transfers between devices  12.3 us (12%)
  waiting for transfers between devices  12.3 us (12%)
  local copies, waits for them, and re-layouts  1.88 us (2%)
    all_to_all x1, blocking collectives, shards(): got = lax.all_to_all(corr[0], 'tm', 0, 0, axis_index_groups=groups)  35.1 us
    all_to_all x1, blocking collectives, shards(): taus = lax.all_to_all(tau, 'tm', 0, 0, axis_index_groups=groups)  26.5 us
    pallas_call x1, Pallas kernels, shards(): pl.pallas_call(forward_kernel, out_shape=(shape(2, rows, cols), shape(GRO...  7.53 us
    ppermute x2, waiting for transfers between devices, shards(): handed = handed + [lax.ppermute(forward, 'tm', pairs)]  6.34 us
    ppermute x9, starting transfers between devices, shards(): pieces.append(lax.ppermute(last, ('tm', 'space'), pairs))  5.98 us
    pallas_call x1, Pallas kernels, shards(): pl.pallas_call(final_kernel, out_shape=(shape(1, 2, rows, cols),) * 3, in...  5.52 us
    ppermute x1, waiting for transfers between devices, shards(): above = lax.ppermute(got[GROUP - 1], 'space', up)  3.01 us
    ppermute x1, starting transfers between devices, shards(): hi = lax.ppermute(top, 'space', down)  2.94 us
  transfers between devices with their start and end apart: 15, of which 4 were waited for; matrix products, arithmetic and copies ran while one was open for 0% of the time, Pallas kernels for 0%

profile of v2, /device:TPU:192, one launch (start us, length us, event | category | flops | bytes accessed | tf_op | source)
XLA Modules:
  0.0 104.6 jit_solution(11414913429443732981)
XLA Ops:
  0.6 1.7 %edges.1 = (f32[3,32,512]{2,1,0:T(8,128)}, f32[3,32,512]{2,1,0:T(8,128)}) custom-call(f32[1,2,64,512]{3,2,1,0:T(8,128)} %c_ref.5, f32[64,512]{1,0:T(8,128)} %n_ref.5), custom_call_target="tpu_custom_call" | custom-call | tf_op jit(solution)/shard_map/edges/pallas_call | solution.py:349
  2.4 0.0 collective-permute-start
  2.4 2.9 %collective-permute-start.1 = (f32[3,32,512]{2,1,0:T(8,128)}, f32[3,32,512]{2,1,0:T(8,128)S(1)}, u32[]{:S(2)}, u32[]{:S(2)}) collective-permute-start(f32[3,32,512]{2,1,0:T(8,128)} %get-tuple-element.18), channel_id=1, source_target_pairs={{1,0},{2,1},{3,2},{4,3},{5,4},{6,5},{7,6},{0,7},{9,8},{10,9},{11,1... | collective-permute-start | bytes 589832 | tf_op jit(solution)/shard_map/ppermute | solution.py:369
  5.3 0.0 copy-start
  5.3 0.9 copy-done
  6.3 0.0 copy-start.2
  6.3 0.9 copy-done.2
  7.2 0.2 load.1.own_ref
  7.4 1.5 %collective-permute-done.lo_ref.clo_ref = f32[3,32,512]{2,1,0:T(8,128)S(1)} collective-permute-done((f32[3,32,512]{2,1,0:T(8,128)}, f32[3,32,512]{2,1,0:T(8,128)S(1)}, u32[]{:S(2)}, u32[]{:S(2)}) %collective-permute-start) | collective-permute-done | bytes 196640 | tf_op jit(solution)/shard_map/ppermute | solution.py:368
  8.9 0.0 collective-permute-done.1.hi_ref.chi_ref
  8.9 7.5 %forward.1 = (f32[2,64,512]{2,1,0:T(8,128)S(1)}, f32[8,2,4,48,128]{4,3,2,1,0:T(8,128)S(1)}, f32[4,48,128]{2,1,0:T(8,128)S(1)}) custom-call(s32[1]{0:T(128)} %bitcast.where_ref.refs_0_, f32[3,64,512]{2,1,0:T(8,128)S(1)} %load.1.own_ref, f32[3,32,512]{2,1,0:T(8,128)S(1)} %collective-permute-done.lo_ref.clo_ref, ...), custom_call_target="tpu_custom_call" | custom-call | tf_op jit(solution)/shard_map/forward/pallas_call | solution.py:372
  16.4 26.5 %all_to_all.10.refs_1_ = f32[8,2,4,48,128]{4,3,2,1,0:T(8,128)S(1)} all-to-all(f32[8,2,4,48,128]{4,3,2,1,0:T(8,128)S(1)} %get-tuple-element.19), channel_id=1, replica_groups={{0,8,16,24,32,40,48,56},{64,72,80,88,96,104,112,120},{128,136,144,152,1..., dimensions={0} | all-to-all | bytes 3145728 | tf_op jit(solution)/shard_map/all_to_all | solution.py:387
  42.9 2.2 %collective-permute-start.5 = (f32[2,64,512]{2,1,0:T(8,128)S(1)}, f32[2,64,512]{2,1,0:T(8,128)S(1)}, u32[]{:S(2)}, u32[]{:S(2)}) collective-permute-start(f32[2,64,512]{2,1,0:T(8,128)S(1)} %get-tuple-element.24.refs_7_), channel_id=1, source_target_pairs={{0,8},{8,16},{16,24},{64,72},{72,80},{80,88},{128,136},{136,144},{... | collective-permute-start | bytes 786440 | tf_op jit(solution)/shard_map/ppermute | solution.py:418
  45.1 0.7 collective-permute-start.4
  45.8 0.7 collective-permute-start.3
  46.5 0.7 collective-permute-start.2
  47.2 0.0 collective-permute-done.4.refs_5_
  47.2 0.0 collective-permute-done.3.refs_4_
  47.2 0.0 collective-permute-done.2.refs_3_
  47.2 6.3 %collective-permute-done.5.refs_7_.handed_ref = f32[2,64,512]{2,1,0:T(8,128)S(1)} collective-permute-done((f32[2,64,512]{2,1,0:T(8,128)S(1)}, f32[2,64,512]{2,1,0:T(8,128)S(1)}, u32[]{:S(2)}, u32[]{:S(2)}) %collective-permute-start.5) | collective-permute-done | bytes 262176 | tf_op jit(solution)/shard_map/ppermute | solution.py:418
  53.5 0.7 collective-permute-start.8
  54.2 0.7 collective-permute-start.7
  54.9 0.7 collective-permute-start.6
  55.6 0.0 collective-permute-done.8.refs_5_
  55.6 0.0 collective-permute-done.7.refs_4_
  55.6 0.0 collective-permute-done.6.refs_3_
  55.6 0.7 collective-permute-start.12
  56.3 0.7 collective-permute-start.11
  57.0 0.7 collective-permute-start.10
  57.7 0.7 collective-permute-start.9
  58.3 0.0 collective-permute-done.11.refs_5_
  58.3 0.0 collective-permute-done.10.refs_4_
  58.3 0.0 collective-permute-done.9.refs_3_
  58.4 0.0 collective-permute-done.12.refs_8_.handed2_ref
  58.4 0.0 copy-start.1
  58.4 0.0 copy-start.3
  58.4 0.7 chain3.1
  59.1 35.1 %all_to_all.11.got_ref = f32[8,2,4,16,128]{4,3,2,1,0:T(8,128)S(1)} all-to-all(f32[8,2,4,16,128]{4,3,2,1,0:T(8,128)S(1)} %get-tuple-element.30), channel_id=1, replica_groups={{0,8,16,24,32,40,48,56},{64,72,80,88,96,104,112,120},{128,136,144,152,1..., dimensions={0} | all-to-all | bytes 1048576 | tf_op jit(solution)/shard_map/all_to_all | solution.py:430
  94.2 0.0 collective-permute-start.14
  94.2 0.5 collective-permute-start.13
  94.7 1.4 %collective-permute-done.14.hi_ref = f32[2,4,16,128]{3,2,1,0:T(8,128)S(1)} collective-permute-done((f32[2,4,16,128]{3,2,1,0:T(8,128)S(1)}, f32[2,4,16,128]{3,2,1,0:T(8,128)S(1)}, u32[]{:S(2)}, u32[]{:S(2)}) %collective-permute-start.14) | collective-permute-done | bytes 65568 | tf_op jit(solution)/shard_map/ppermute | solution.py:432
  96.1 3.0 %collective-permute-done.13.lo_ref = f32[2,4,16,128]{3,2,1,0:T(8,128)S(1)} collective-permute-done((f32[2,4,16,128]{3,2,1,0:T(8,128)S(1)}, f32[2,4,16,128]{3,2,1,0:T(8,128)S(1)}, u32[]{:S(2)}, u32[]{:S(2)}) %collective-permute-start.13) | collective-permute-done | bytes 65568 | tf_op jit(solution)/shard_map/ppermute | solution.py:431
  99.1 0.0 copy-done.1
  99.1 0.0 copy-done.3
  99.1 5.5 %final.1 = (f32[1,2,64,512]{3,2,1,0:T(8,128)}, f32[1,2,64,512]{3,2,1,0:T(8,128)}, f32[1,2,64,512]{3,2,1,0:T(8,128)}) custom-call(s32[1]{0:T(128)} %bitcast.where_ref.refs_0_, f32[8,2,4,16,128]{4,3,2,1,0:T(8,128)S(1)} %all_to_all.11.got_ref, f32[2,4,16,128]{3,2,1,0:T(8,128)S(1)} %collective-permute-done.13.lo_ref, ...), custom_call_target="tpu_custom_call" | custom-call | tf_op jit(solution)/shard_map/final/pallas_call | solution.py:435
  (4 shorter events, 0.1 us)
Async XLA Ops:
  2.4 6.5 %collective-permute-start = (f32[3,32,512]{2,1,0:T(8,128)}, f32[3,32,512]{2,1,0:T(8,128)S(1)}, u32[]{:S(2)}, u32[]{:S(2)}) collective-permute-start(f32[3,32,512]{2,1,0:T(8,128)} %get-tuple-element.17), channel_id=1, source_target_pairs={{0,1},{1,2},{2,3},{3,4},{4,5},{5,6},{6,7},{7,0},{8,9},{9,10},{10,1... | collective-permute-start | bytes 589832 | tf_op jit(solution)/shard_map/ppermute | solution.py:368
  2.4 6.5 %collective-permute-start.1 = (f32[3,32,512]{2,1,0:T(8,128)}, f32[3,32,512]{2,1,0:T(8,128)S(1)}, u32[]{:S(2)}, u32[]{:S(2)}) collective-permute-start(f32[3,32,512]{2,1,0:T(8,128)} %get-tuple-element.18), channel_id=1, source_target_pairs={{1,0},{2,1},{3,2},{4,3},{5,4},{6,5},{7,6},{0,7},{9,8},{10,9},{11,1... | collective-permute-start | bytes 589832 | tf_op jit(solution)/shard_map/ppermute | solution.py:369
  5.3 0.9 copy-start
  6.3 0.9 copy-start.2
  42.9 10.6 %collective-permute-start.5 = (f32[2,64,512]{2,1,0:T(8,128)S(1)}, f32[2,64,512]{2,1,0:T(8,128)S(1)}, u32[]{:S(2)}, u32[]{:S(2)}) collective-permute-start(f32[2,64,512]{2,1,0:T(8,128)S(1)} %get-tuple-element.24.refs_7_), channel_id=1, source_target_pairs={{0,8},{8,16},{16,24},{64,72},{72,80},{80,88},{128,136},{136,144},{... | collective-permute-start | bytes 786440 | tf_op jit(solution)/shard_map/ppermute | solution.py:418
  45.1 2.0 %collective-permute-start.4 = (f32[2,4,16,128]{3,2,1,0:T(8,128)S(1)}, f32[2,4,16,128]{3,2,1,0:T(8,128)S(1)}, u32[]{:S(2)}, u32[]{:S(2)}) collective-permute-start(f32[2,4,16,128]{3,2,1,0:T(8,128)S(1)} %get-tuple-element.22), channel_id=1, source_target_pairs={{32,127},{40,96},{48,104},{56,112},{33,120},{41,97},{49,105},{57,1... | collective-permute-start | bytes 196616 | tf_op jit(solution)/shard_map/ppermute | solution.py:428
  45.8 1.4 %collective-permute-start.3 = (f32[2,4,16,128]{3,2,1,0:T(8,128)S(1)}, f32[2,4,16,128]{3,2,1,0:T(8,128)S(1)}, u32[]{:S(2)}, u32[]{:S(2)}) collective-permute-start(f32[2,4,16,128]{3,2,1,0:T(8,128)S(1)} %get-tuple-element.22), channel_id=1, source_target_pairs={{32,96},{40,104},{48,112},{56,120},{33,97},{41,105},{49,113},{57,1... | collective-permute-start | bytes 196616 | tf_op jit(solution)/shard_map/ppermute | solution.py:428
  46.5 0.7 collective-permute-start.2
  53.5 2.0 %collective-permute-start.8 = (f32[2,4,16,128]{3,2,1,0:T(8,128)S(1)}, f32[2,4,16,128]{3,2,1,0:T(8,128)S(1)}, u32[]{:S(2)}, u32[]{:S(2)}) collective-permute-start(f32[2,4,16,128]{3,2,1,0:T(8,128)S(1)} %get-tuple-element.25), channel_id=1, source_target_pairs={{96,191},{104,160},{112,168},{120,176},{97,184},{105,161},{113,169... | collective-permute-start | bytes 196616 | tf_op jit(solution)/shard_map/ppermute | solution.py:428
  54.2 1.4 %collective-permute-start.7 = (f32[2,4,16,128]{3,2,1,0:T(8,128)S(1)}, f32[2,4,16,128]{3,2,1,0:T(8,128)S(1)}, u32[]{:S(2)}, u32[]{:S(2)}) collective-permute-start(f32[2,4,16,128]{3,2,1,0:T(8,128)S(1)} %get-tuple-element.25), channel_id=1, source_target_pairs={{96,160},{104,168},{112,176},{120,184},{97,161},{105,169},{113,177... | collective-permute-start | bytes 196616 | tf_op jit(solution)/shard_map/ppermute | solution.py:428
  54.9 0.7 collective-permute-start.6
  55.6 2.7 %collective-permute-start.12 = (f32[2,64,512]{2,1,0:T(8,128)S(1)}, f32[2,64,512]{2,1,0:T(8,128)S(1)}, u32[]{:S(2)}, u32[]{:S(2)}) collective-permute-start(f32[2,64,512]{2,1,0:T(8,128)S(1)} %get-tuple-element.29), channel_id=1, source_target_pairs={{24,32},{32,40},{40,48},{48,56},{56,64},{88,96},{96,104},{104,112}... | collective-permute-start | bytes 786440 | tf_op jit(solution)/shard_map/ppermute | solution.py:418
  56.3 2.0 %collective-permute-start.11 = (f32[2,4,16,128]{3,2,1,0:T(8,128)S(1)}, f32[2,4,16,128]{3,2,1,0:T(8,128)S(1)}, u32[]{:S(2)}, u32[]{:S(2)}) collective-permute-start(f32[2,4,16,128]{3,2,1,0:T(8,128)S(1)} %get-tuple-element.27), channel_id=1, source_target_pairs={{160,255},{168,224},{176,232},{184,240},{161,248},{169,225},{177,2... | collective-permute-start | bytes 196616 | tf_op jit(solution)/shard_map/ppermute | solution.py:428
  57.0 1.4 %collective-permute-start.10 = (f32[2,4,16,128]{3,2,1,0:T(8,128)S(1)}, f32[2,4,16,128]{3,2,1,0:T(8,128)S(1)}, u32[]{:S(2)}, u32[]{:S(2)}) collective-permute-start(f32[2,4,16,128]{3,2,1,0:T(8,128)S(1)} %get-tuple-element.27), channel_id=1, source_target_pairs={{160,224},{168,232},{176,240},{184,248},{161,225},{169,233},{177,2... | collective-permute-start | bytes 196616 | tf_op jit(solution)/shard_map/ppermute | solution.py:428
  57.7 0.7 collective-permute-start.9
  58.4 40.7 %copy-start.1 = (f32[1,2,64,512]{3,2,1,0:T(8,128)S(1)}, f32[1,2,64,512]{3,2,1,0:T(8,128)}, u32[]{:S(2)}) copy-start(f32[1,2,64,512]{3,2,1,0:T(8,128)} %c_ref.5) | copy-start | bytes 786436
  58.4 40.7 %copy-start.3 = (f32[64,512]{1,0:T(8,128)S(1)}, f32[64,512]{1,0:T(8,128)}, u32[]{:S(2)}) copy-start(f32[64,512]{1,0:T(8,128)} %n_ref.5) | copy-start | bytes 393220
  94.2 1.9 %collective-permute-start.14 = (f32[2,4,16,128]{3,2,1,0:T(8,128)S(1)}, f32[2,4,16,128]{3,2,1,0:T(8,128)S(1)}, u32[]{:S(2)}, u32[]{:S(2)}) collective-permute-start(f32[2,4,16,128]{3,2,1,0:T(8,128)S(1)} %get-tuple-element.31), channel_id=1, source_target_pairs={{1,0},{2,1},{3,2},{4,3},{5,4},{6,5},{7,6},{0,7},{9,8},{10,9},{11,1... | collective-permute-start | bytes 196616 | tf_op jit(solution)/shard_map/ppermute | solution.py:432
  94.2 4.9 %collective-permute-start.13 = (f32[2,4,16,128]{3,2,1,0:T(8,128)S(1)}, f32[2,4,16,128]{3,2,1,0:T(8,128)S(1)}, u32[]{:S(2)}, u32[]{:S(2)}) collective-permute-start(f32[2,4,16,128]{3,2,1,0:T(8,128)S(1)} %get-tuple-element.32), channel_id=1, source_target_pairs={{0,1},{1,2},{2,3},{3,4},{4,5},{5,6},{6,7},{7,0},{8,9},{9,10},{10,1... | collective-permute-start | bytes 196616 | tf_op jit(solution)/shard_map/ppermute | solution.py:431

commit v3 on v2

--- a/solution.py
+++ b/solution.py
@@ -13,6 +13,7 @@
 HALO = 16
 EDGE = 32
 WINDOW = STRIP + 2 * HALO
+INNER = 8
 LANES = 128
 SPLIT = 4
 advect_scale = 0.1
@@ -113,6 +114,11 @@
     return [plane(nat, i, n) for i in range(n)]
 
 
+def fill(nat, at, ref, start, count):
+    for b in range(nat.shape[0]):
+        nat[b, at : at + count, :] = ref[start : start + count, b * LANES : (b + 1) * LANES]
+
+
 def copies(pairs, sem):
     started = [pltpu.make_async_copy(a, b, sem.at[i]) for i, (a, b) in enumerate(pairs)]
     for copy in started:
@@ -147,25 +153,15 @@
 
 
 def forward_kernel(where_ref, own_ref, lo_ref, hi_ref,
-                   fwd_ref, tau_ref, nwin_ref,
+                   fwd_ref, nwin_ref, own_tau, near1, near2, near3, far0, far1, far2, far3,
                    nat, fnat, w, mid, tau, cf, cc, sem):
     n = 16
     blocks = nat.shape[1]
     rows = own_ref.shape[1]
-    pairs = []
-    for b in range(blocks):
-        mine = pl.ds(EDGE, rows)
-        pairs.append((own_ref.at[2, :, cut(b)], nat.at[2, b, mine, :]))
-        pairs.append((lo_ref.at[2, :, cut(b)], nat.at[2, b, pl.ds(0, EDGE), :]))
-        pairs.append((hi_ref.at[2, :, cut(b)], nat.at[2, b, pl.ds(EDGE + rows, EDGE), :]))
-    for b in range(blocks):
-        both = pl.ds(0, 2)
-        pairs.append((own_ref.at[both, :, cut(b)], nat.at[both, b, mine, :]))
-        pairs.append((lo_ref.at[both, :, cut(b)], nat.at[both, b, pl.ds(0, EDGE), :]))
-        pairs.append((hi_ref.at[both, :, cut(b)], nat.at[both, b, pl.ds(EDGE + rows, EDGE), :]))
-    started = copies(pairs, sem)
-    for copy in started[: 3 * blocks]:
-        copy.wait()
+    for c in (2, 0, 1):
+        fill(nat.at[c], 0, lo_ref.at[c], 0, EDGE)
+        fill(nat.at[c], EDGE, own_ref.at[c], 0, rows)
+        fill(nat.at[c], EDGE + rows, hi_ref.at[c], 0, EDGE)
     position = where_ref[0]
     vnat = nat.at[2]
     start = pl.multiple_of(lax.rem(position, SPLIT) * STRIP + HALO, 8)
@@ -174,9 +170,12 @@
     coef_c = [cc.at[i] for i in range(4)]
     coef_f = [cf.at[i] for i in range(4)]
     make_coefs(visc, coarse_size, coef_c)
-    make_coefs(visc, coarse_size / STEPS, coef_f)
-    for copy in started[3 * blocks :]:
-        copy.wait()
+    for i in range(n + 1):
+        cf[0, i] = cc[0, i] * (1.0 / STEPS)
+    for i in range(n):
+        cf[1, i] = cc[1, i] * (1.0 / STEPS)
+        cf[2, i] = cc[2, i] * (1.0 / STEPS)
+        cf[3, i] = cc[3, i] * (1.0 / STEPS) + (1.0 - 1.0 / STEPS)
     for c in range(2):
         for i in range(n):
             w[c, i] = COARSE * plane(nat.at[c], i, n)
@@ -201,66 +200,85 @@
         both = pl.ds(0, 2)
         pairs.append((fnat.at[both, b, pl.ds(EDGE, rows), :], fwd_ref.at[both, :, cut(b)]))
     started = copies(pairs, sem)
-    for c in range(2):
-        for p in range(GROUP):
-            at = EDGE - HALO + (p % SPLIT) * STRIP
-            tau_ref[p, c] = nat[c, :, at : at + WINDOW, :]
+    for k, ref in enumerate((own_tau, near1, near2, near3)):
+        first = lax.rem(position + k, SPLIT) * STRIP + (EDGE - HALO)
+        ref[...] = nat[0:2, :, pl.ds(pl.multiple_of(first, 8), WINDOW), :]
+    for k, ref in enumerate((far0, far1, far2, far3)):
+        first = lax.rem(position + k, SPLIT) * STRIP + (EDGE - INNER)
+        ref[...] = nat[0:2, :, pl.ds(pl.multiple_of(first, 8), STRIP + 2 * INNER), :]
     for copy in started:
         copy.wait()
 
 
-def chain_kernel(stage, stages, *refs):
+def prep_kernel(nwin_ref, cc_ref):
+    make_coefs(load_planes(nwin_ref, WINDOW // 8), coarse_size, [cc_ref.at[i] for i in range(4)])
+
+
+def chain_kernel(stage, stages, carried, *refs):
     refs = list(refs)
-    where_ref, tau_ref, nwin_ref = refs[:3]
-    pieces = refs[3:6] if stage > 0 else None
-    scratch = refs[-6:]
-    nat, w, mid, cc, part, sem = scratch
-    corr_ref, last_ref = refs[-8:-6]
+    where_ref, cc_ref = refs[:2]
+    nat, w, mid = refs[-3:]
+    corr_ref, last_ref = refs[-5:-3]
     n = WINDOW // 8
     position = where_ref[0]
     planes = GROUP // SPLIT
-
-    @pl.when(position // SPLIT == (stage + 1) * planes - 1)
+    rest = refs[2 + carried :]
+    if stage == 0:
+        tau_ref = refs[-6]
+        for k in range(SPLIT):
+            source = lax.rem(position + SPLIT - k, SPLIT)
+            tau_ref[source] = rest[k][...]
+            far = source + SPLIT
+            tau_ref[far, :, :, 0:INNER, :] = jnp.zeros_like(rest[0][:, :, 0:INNER, :])
+            tau_ref[far, :, :, WINDOW - INNER :, :] = jnp.zeros_like(rest[0][:, :, 0:INNER, :])
+            tau_ref[far, :, :, INNER : WINDOW - INNER, :] = rest[SPLIT + k][...]
+    else:
+        tau_ref = rest[0]
+        own, above, below, corr_in = rest[1:5]
+    active = position // SPLIT == stage * planes
+
+    @pl.when(active)
     def _():
-        coef = [cc.at[i] for i in range(4)]
-        make_coefs(load_planes(nwin_ref, n), coarse_size, coef)
-
-        def keep(t):
+        coef = [cc_ref.at[i] for i in range(4)]
+
+        def keep(out):
             for c in range(2):
                 for i in range(n):
                     put_plane(nat.at[c], i, n, w[c, i])
-                part[t, c] = nat[c, :, HALO : HALO + STRIP, :]
-
-        def one(t):
+                out[c] = nat[c, :, HALO : HALO + STRIP, :]
+
+        def one(t, out):
             heun(w, mid, w, coef, n, lambda c, i: plane(tau_ref.at[t, c], i, n))
-            keep(t + 1)
+            keep(out)
 
         if stage == 0:
             for c in range(2):
-                part[0, c] = jnp.zeros_like(part[0, c])
+                corr_ref[0, c] = jnp.zeros_like(corr_ref[0, c])
                 for i in range(n):
                     w[c, i] = plane(tau_ref.at[0, c], i, n)
-            keep(1)
+            keep(corr_ref.at[1])
         else:
             for c in range(2):
-                for k, ref in enumerate(pieces):
+                for k, ref in enumerate((above, own, below)):
                     nat[c, :, k * STRIP : (k + 1) * STRIP, :] = ref[c]
-                part[0, c] = pieces[1][c]
+                corr_ref[0, c] = own[c]
                 for i in range(n):
                     w[c, i] = plane(nat.at[c], i, n)
-            one(0)
+            one(0, corr_ref.at[1])
 
         def step(t, carry):
-            one(t)
+            one(t, corr_ref.at[t + 1])
             return carry
 
         lax.fori_loop(1, GROUP - 1, step, 0)
-        copy = pltpu.make_async_copy(part.at[pl.ds(0, GROUP)], corr_ref, sem)
-        copy.start()
         if stage + 1 < stages:
-            one(GROUP - 1)
-            last_ref[...] = part[GROUP]
-        copy.wait()
+            one(GROUP - 1, last_ref)
+
+    if stage > 0:
+
+        @pl.when(jnp.logical_not(active))
+        def _():
+            corr_ref[...] = corr_in[...]
 
 
 def final_kernel(where_ref, got_ref, lo_ref, hi_ref, c_ref, clo_ref, chi_ref,
@@ -271,10 +289,9 @@
     rows = n_ref.shape[0]
     blocks = nat.shape[1]
     position = where_ref[0]
-    for b in range(blocks):
-        vnat[b, 0:HALO, :] = clo_ref[2, EDGE - HALO :, b * LANES : (b + 1) * LANES]
-        vnat[b, HALO : HALO + rows, :] = n_ref[:, b * LANES : (b + 1) * LANES]
-        vnat[b, HALO + rows :, :] = chi_ref[2, 0:HALO, b * LANES : (b + 1) * LANES]
+    fill(vnat, 0, clo_ref.at[2], EDGE - HALO, HALO)
+    fill(vnat, HALO, n_ref, 0, rows)
+    fill(vnat, HALO + rows, chi_ref.at[2], 0, HALO)
     coef = [cf.at[i] for i in range(4)]
     make_coefs(load_planes(vnat, n), coarse_size / STEPS, coef)
 
@@ -297,7 +314,7 @@
             nat[c, :, HALO + rows :, :] = back * hi_ref[c]
             for q in range(SPLIT):
                 at = HALO + q * STRIP
-                nat[c, :, at : at + STRIP, :] = back * got_ref[GROUP - SPLIT + q, c]
+                nat[c, :, at : at + STRIP, :] = back * got_ref[q, c]
 
     both = pl.ds(0, 2)
     mine = pl.ds(HALO, rows)
@@ -369,67 +386,92 @@
     hi = lax.ppermute(top, "space", down)
 
     n = 16
-    forward, tau, nwin = pl.pallas_call(
+    window = shape(2, blocks, WINDOW, LANES)
+    inner = shape(2, blocks, STRIP + 2 * INNER, LANES)
+    forward, nwin, *sent = pl.pallas_call(
         forward_kernel,
-        out_shape=(shape(2, rows, cols), shape(GROUP, 2, blocks, WINDOW, LANES), shape(blocks, WINDOW, LANES)),
-        in_specs=[SMEM, ANY, ANY, ANY],
-        out_specs=(HBM, VMEM, VMEM),
+        out_shape=(shape(2, rows, cols), shape(blocks, WINDOW, LANES)) + (window,) * SPLIT + (inner,) * SPLIT,
+        in_specs=[SMEM, VMEM, VMEM, VMEM],
+        out_specs=(HBM,) + (VMEM,) * (1 + 2 * SPLIT),
         scratch_shapes=[
             vm(3, blocks, 128, LANES), vm(2, blocks, 128, LANES),
             vm(2, n, 8, cols), vm(2, n, 8, cols), vm(2, n, 8, cols),
-            vm(4, n + 1, 8, cols), vm(4, n + 1, 8, cols), dma(6 * blocks),
+            vm(4, n + 1, 8, cols), vm(4, n + 1, 8, cols), dma(blocks),
         ],
         compiler_params=PARAMS,
         name="forward",
     )(where, own, lo, hi)
 
+    n = WINDOW // 8
+    cc = pl.pallas_call(
+        prep_kernel,
+        out_shape=shape(4, n + 1, 8, cols),
+        in_specs=[VMEM],
+        out_specs=VMEM,
+        compiler_params=PARAMS,
+        name="prep",
+    )(nwin)
+
+    planes = range(0, intervals, SPLIT)
+    gathered = [sent[0]]
+    for k in range(1, SPLIT):
+        pairs = [(p + q, p + (q + k) % SPLIT) for p in planes for q in range(SPLIT)]
+        gathered.append(lax.ppermute(sent[k], "tm", pairs))
+    for k in range(SPLIT):
+        pairs = []
+        for p in range(0, intervals, GROUP):
+            for q in range(SPLIT):
+                a, b = p + SPLIT + q, p + (q + k) % SPLIT
+                pairs += [(a, b), (b, a)]
+        gathered.append(lax.ppermute(sent[SPLIT + k], "tm", pairs))
     groups = [[g * GROUP + j for j in range(GROUP)] for g in range(stages)]
-    taus = lax.all_to_all(tau, "tm", 0, 0, axis_index_groups=groups)
 
     strips = ring * SPLIT
-    n = WINDOW // 8
     pieces, corr, handed = [], [], []
     for stage in range(stages):
         extra = {0: [forward], 1: handed, stages - 2: [forward], stages - 1: handed}[stage]
         carries = stage in (0, stages - 2)
-        count = 3 + len(pieces)
-        aliases = {count: 1} if stage > 0 else {}
+        operands = [where, cc] + extra + (gathered if stage == 0 else [taus] + pieces + corr)
+        specs = [SMEM, VMEM] + [HBM] * len(extra) + [VMEM] * (len(operands) - 2 - len(extra))
+        shapes = [shape(2, rows, cols) if carries else shape(8, LANES)]
+        shapes += [shape(GROUP, 2, blocks, WINDOW, LANES)] if stage == 0 else []
+        shapes += [shape(GROUP, 2, blocks, STRIP, LANES), shape(2, blocks, STRIP, LANES)]
+        aliases = {len(operands) - 1: 1} if stage > 0 else {}
         if carries:
-            aliases[count + len(corr)] = 0
-        kept = shape(2, rows, cols) if carries else shape(8, LANES)
+            aliases[2] = 0
         done = pl.pallas_call(
-            functools.partial(chain_kernel, stage, stages),
-            out_shape=(kept, shape(GROUP, 2, blocks, STRIP, LANES), shape(2, blocks, STRIP, LANES)),
-            in_specs=[SMEM] + [VMEM] * (count - 1) + [ANY] * len(corr) + [HBM] * len(extra),
-            out_specs=(HBM, ANY, VMEM),
-            scratch_shapes=[
-                vm(2, blocks, WINDOW, LANES), vm(2, n, 8, cols), vm(2, n, 8, cols), vm(4, n + 1, 8, cols),
-                vm(GROUP + 1, 2, blocks, STRIP, LANES), pltpu.SemaphoreType.DMA,
-            ],
+            functools.partial(chain_kernel, stage, stages, len(extra)),
+            out_shape=tuple(shapes),
+            in_specs=specs,
+            out_specs=(HBM,) + (VMEM,) * (len(shapes) - 1),
+            scratch_shapes=[vm(2, blocks, WINDOW, LANES), vm(2, n, 8, cols), vm(2, n, 8, cols)],
             input_output_aliases=aliases,
             compiler_params=PARAMS,
             name="chain%d" % stage,
-        )(where, taus, nwin, *pieces, *corr, *extra)
-        corr, last = [done[1]], done[2]
+        )(*operands)
+        if stage == 0:
+            taus = done[1]
+        corr, last = [done[-2]], done[-1]
         if carries:
             forward = done[0]
-            chain = [g * GROUP + GROUP - 1 - q for g in range(2) for q in range(SPLIT)]
+            chain = [g * GROUP + q for g in range(2) for q in range(SPLIT)]
             pairs = [(i, i + 1) for i in range(intervals - 1) if (i in chain or i + 1 in chain) == (stage > 0)]
             handed = handed + [lax.ppermute(forward, "tm", pairs)]
         if stage + 1 < stages:
-            pieces = []
-            for delta in (1, 0, -1):
+            arrived = {}
+            for delta in (0, 1, -1):
                 pairs = []
                 for strip in range(strips):
                     to = (strip + delta) % strips
-                    source = stage * GROUP + GROUP - SPLIT + strip % SPLIT
-                    target = (stage + 1) * GROUP + GROUP - SPLIT + to % SPLIT
+                    source = stage * GROUP + strip % SPLIT
+                    target = (stage + 1) * GROUP + to % SPLIT
                     pairs.append((source * ring + strip // SPLIT, target * ring + to // SPLIT))
-                pieces.append(lax.ppermute(last, ("tm", "space"), pairs))
+                arrived[delta] = lax.ppermute(last, ("tm", "space"), pairs)
+            pieces = [arrived[0], arrived[1], arrived[-1]]
 
     got = lax.all_to_all(corr[0], "tm", 0, 0, axis_index_groups=groups)
-    above = lax.ppermute(got[GROUP - 1], "space", up)
-    below = lax.ppermute(got[GROUP - SPLIT], "space", down)
+    above = lax.ppermute(got[SPLIT - 1], "space", up)
+    below = lax.ppermute(got[0], "space", down)
 
     n = 12
     return pl.pallas_call(
@@ -438,7 +480,7 @@
         in_specs=[SMEM] + [VMEM] * 9,
         out_specs=(ANY,) * 3,
         scratch_shapes=[
-            vm(2, blocks, 96, LANES), vm(blocks, 96, LANES), vm(2, blocks, 96, LANES), vm(2, rows, cols),
+            vm(2, blocks, 8 * n, LANES), vm(blocks, 8 * n, LANES), vm(2, blocks, 8 * n, LANES), vm(2, rows, cols),
             vm(2, n, 8, cols), vm(2, n, 8, cols), vm(4, n + 1, 8, cols), dma(1 + 2 * blocks),
         ],
         compiler_params=PARAMS,

time: 105 us -> 102 us (0.971)
  blocking collectives: 61.6 us -> 13.1 us
  waiting for transfers between devices: 12.3 us -> 43.2 us
  starting transfers between devices: 12.3 us -> 25 us
  Pallas kernels: 15.7 us -> 17.7 us
    ppermute x11 -> x18, waiting for transfers between devices: 4.44 us -> 34.9 us  [the longest x9 18.6 us: shards(): arrived[delta] = lax.ppermute(last, ('tm', 'space'), pairs)]
    all_to_all x1 -> x0, blocking collectives: 26.5 us -> none  [shards(): taus = lax.all_to_all(tau, 'tm', 0, 0, axis_index_groups=groups)]
    all_to_all x1, blocking collectives: 35.1 us -> 13.1 us  [shards(): got = lax.all_to_all(corr[0], 'tm', 0, 0, axis_index_groups=groups)]
    ppermute x11 -> x18, starting transfers between devices: 6.5 us -> 19.2 us  [the longest x9 7.86 us: shards(): arrived[delta] = lax.ppermute(last, ('tm', 'space'), pairs)]
    pallas_call x5 -> x6, Pallas kernels: 8.23 us -> 10.3 us  [the longest x1 6.9 us: shards(): pl.pallas_call(forward_kernel, out_shape=(shape(2, rows, cols), shape(blo...]
  transfers between devices with their start and end apart: 15 -> 22, of which waited for: 4 -> 12; matrix products, arithmetic and copies ran while one was open for 0% -> 0% of each run, Pallas kernels for 0% -> 0%
where the time goes in v3:
time: 102 us
  waiting for transfers between devices  43.2 us (42%)
  starting transfers between devices  25 us (25%)
  Pallas kernels  17.7 us (17%)
  blocking collectives  13.1 us (13%)
  local copies, waits for them, and re-layouts  1.87 us (2%)
    ppermute x9, waiting for transfers between devices, shards(): arrived[delta] = lax.ppermute(last, ('tm', 'space'), pairs)  18.6 us
    all_to_all x1, blocking collectives, shards(): got = lax.all_to_all(corr[0], 'tm', 0, 0, axis_index_groups=groups)  13.1 us
    ppermute x9, starting transfers between devices, shards(): arrived[delta] = lax.ppermute(last, ('tm', 'space'), pairs)  7.86 us
    ppermute x4, starting transfers between devices, shards(): gathered.append(lax.ppermute(sent[SPLIT + k], 'tm', pairs))  7.56 us
    pallas_call x1, Pallas kernels, shards(): pl.pallas_call(forward_kernel, out_shape=(shape(2, rows, cols), shape(blo...  6.9 us
    ppermute x2, waiting for transfers between devices, shards(): handed = handed + [lax.ppermute(forward, 'tm', pairs)]  6.84 us
    ppermute x4, waiting for transfers between devices, shards(): gathered.append(lax.ppermute(sent[SPLIT + k], 'tm', pairs))  6.12 us
    ppermute x3, waiting for transfers between devices, shards(): gathered.append(lax.ppermute(sent[k], 'tm', pairs))  5.75 us
  transfers between devices with their start and end apart: 22, of which 12 were waited for; matrix products, arithmetic and copies ran while one was open for 0% of the time, Pallas kernels for 0%

profile of v3, /device:TPU:192, one launch (start us, length us, event | category | flops | bytes accessed | tf_op | source)
XLA Modules:
  0.0 101.8 jit_solution(18078243124947565326)
XLA Ops:
  0.6 1.7 %edges.1 = (f32[3,32,512]{2,1,0:T(8,128)}, f32[3,32,512]{2,1,0:T(8,128)}) custom-call(f32[1,2,64,512]{3,2,1,0:T(8,128)} %c_ref.5, f32[64,512]{1,0:T(8,128)} %n_ref.5), custom_call_target="tpu_custom_call" | custom-call | tf_op jit(solution)/shard_map/edges/pallas_call | solution.py:366
  2.4 0.0 collective-permute-start
  2.4 2.9 %collective-permute-start.1 = (f32[3,32,512]{2,1,0:T(8,128)}, f32[3,32,512]{2,1,0:T(8,128)S(1)}, u32[]{:S(2)}, u32[]{:S(2)}) collective-permute-start(f32[3,32,512]{2,1,0:T(8,128)} %get-tuple-element.26), channel_id=1, source_target_pairs={{1,0},{2,1},{3,2},{4,3},{5,4},{6,5},{7,6},{0,7},{9,8},{10,9},{11,1... | collective-permute-start | bytes 589832 | tf_op jit(solution)/shard_map/ppermute | solution.py:386
  5.3 0.9 copy-done
  6.3 0.9 copy-done.2
  7.2 0.2 load.1.own_ref
  7.4 1.5 %collective-permute-done.lo_ref.clo_ref = f32[3,32,512]{2,1,0:T(8,128)S(1)} collective-permute-done((f32[3,32,512]{2,1,0:T(8,128)}, f32[3,32,512]{2,1,0:T(8,128)S(1)}, u32[]{:S(2)}, u32[]{:S(2)}) %collective-permute-start) | collective-permute-done | bytes 196640 | tf_op jit(solution)/shard_map/ppermute | solution.py:385
  8.9 0.0 collective-permute-done.1.hi_ref.chi_ref
  8.9 6.9 %forward.1 = (f32[2,64,512]{2,1,0:T(8,128)S(1)}, f32[4,48,128]{2,1,0:T(8,128)S(1)}, f32[2,4,48,128]{3,2,1,0:T(8,128)S(1)}, f32[2,4,48,128]{3,2,1,0:T(8,128)S(1)}...) custom-call(s32[1]{0:T(128)} %bitcast.where_ref.refs_0_, ...), custom_call_target="tpu_custom_call" | custom-call | tf_op jit(solution)/shard_map/forward/pallas_call | solution.py:391
  15.8 1.1 %collective-permute-start.5 = (f32[2,4,32,128]{3,2,1,0:T(8,128)S(1)}, f32[2,4,32,128]{3,2,1,0:T(8,128)S(1)}, u32[]{:S(2)}, u32[]{:S(2)}) collective-permute-start(f32[2,4,32,128]{3,2,1,0:T(8,128)S(1)} %get-tuple-element.33), channel_id=1, source_target_pairs={{32,0},{0,32},{40,8},{8,40},{48,16},{16,48},{56,24},{24,56},{96,64... | collective-permute-start | bytes 393224 | tf_op jit(solution)/shard_map/ppermute | solution.py:426
  17.0 3.5 %collective-permute-start.6 = (f32[2,4,32,128]{3,2,1,0:T(8,128)S(1)}, f32[2,4,32,128]{3,2,1,0:T(8,128)S(1)}, u32[]{:S(2)}, u32[]{:S(2)}) collective-permute-start(f32[2,4,32,128]{3,2,1,0:T(8,128)S(1)} %get-tuple-element.34), channel_id=1, source_target_pairs={{32,8},{8,32},{40,16},{16,40},{48,24},{24,48},{56,0},{0,56},{96,72... | collective-permute-start | bytes 393224 | tf_op jit(solution)/shard_map/ppermute | solution.py:426
  20.4 0.0 collective-permute-start.2
  20.4 2.2 %collective-permute-start.3 = (f32[2,4,48,128]{3,2,1,0:T(8,128)S(1)}, f32[2,4,48,128]{3,2,1,0:T(8,128)S(1)}, u32[]{:S(2)}, u32[]{:S(2)}) collective-permute-start(f32[2,4,48,128]{3,2,1,0:T(8,128)S(1)} %get-tuple-element.31), channel_id=1, source_target_pairs={{0,16},{8,24},{16,0},{24,8},{32,48},{40,56},{48,32},{56,40},{64,80... | collective-permute-start | bytes 589832 | tf_op jit(solution)/shard_map/ppermute | solution.py:419
  22.6 1.1 %collective-permute-start.4 = (f32[2,4,48,128]{3,2,1,0:T(8,128)S(1)}, f32[2,4,48,128]{3,2,1,0:T(8,128)S(1)}, u32[]{:S(2)}, u32[]{:S(2)}) collective-permute-start(f32[2,4,48,128]{3,2,1,0:T(8,128)S(1)} %get-tuple-element.32), channel_id=1, source_target_pairs={{0,24},{8,0},{16,8},{24,16},{32,56},{40,32},{48,40},{56,48},{64,88... | collective-permute-start | bytes 589832 | tf_op jit(solution)/shard_map/ppermute | solution.py:419
  23.7 2.2 %collective-permute-start.7 = (f32[2,4,32,128]{3,2,1,0:T(8,128)S(1)}, f32[2,4,32,128]{3,2,1,0:T(8,128)S(1)}, u32[]{:S(2)}, u32[]{:S(2)}) collective-permute-start(f32[2,4,32,128]{3,2,1,0:T(8,128)S(1)} %get-tuple-element.35), channel_id=1, source_target_pairs={{32,16},{16,32},{40,24},{24,40},{48,0},{0,48},{56,8},{8,56},{96,80... | collective-permute-start | bytes 393224 | tf_op jit(solution)/shard_map/ppermute | solution.py:426
  25.9 1.2 %collective-permute-done.6.refs_8_ = f32[2,4,32,128]{3,2,1,0:T(8,128)S(1)} collective-permute-done((f32[2,4,32,128]{3,2,1,0:T(8,128)S(1)}, f32[2,4,32,128]{3,2,1,0:T(8,128)S(1)}, u32[]{:S(2)}, u32[]{:S(2)}) %collective-permute-start.6) | collective-permute-done | bytes 131104 | tf_op jit(solution)/shard_map/ppermute | solution.py:426
  27.1 0.7 collective-permute-start.8
  27.8 0.2 prep.1.refs_1_
  28.0 4.2 %collective-permute-done.7.refs_9_ = f32[2,4,32,128]{3,2,1,0:T(8,128)S(1)} collective-permute-done((f32[2,4,32,128]{3,2,1,0:T(8,128)S(1)}, f32[2,4,32,128]{3,2,1,0:T(8,128)S(1)}, u32[]{:S(2)}, u32[]{:S(2)}) %collective-permute-start.7) | collective-permute-done | bytes 131104 | tf_op jit(solution)/shard_map/ppermute | solution.py:426
  32.2 0.7 collective-permute-done.8.refs_10_
  32.9 4.9 %collective-permute-done.2.refs_4_ = f32[2,4,48,128]{3,2,1,0:T(8,128)S(1)} collective-permute-done((f32[2,4,48,128]{3,2,1,0:T(8,128)S(1)}, f32[2,4,48,128]{3,2,1,0:T(8,128)S(1)}, u32[]{:S(2)}, u32[]{:S(2)}) %collective-permute-start.2) | collective-permute-done | bytes 196640 | tf_op jit(solution)/shard_map/ppermute | solution.py:419
  37.9 0.0 collective-permute-done.3.refs_5_
  37.9 0.8 collective-permute-done.4.refs_6_
  38.7 0.1 chain0.1
  38.8 2.1 %collective-permute-start.9 = (f32[2,64,512]{2,1,0:T(8,128)S(1)}, f32[2,64,512]{2,1,0:T(8,128)S(1)}, u32[]{:S(2)}, u32[]{:S(2)}) collective-permute-start(f32[2,64,512]{2,1,0:T(8,128)S(1)} %get-tuple-element.37.refs_2_), channel_id=1, source_target_pairs={{32,40},{40,48},{48,56},{96,104},{104,112},{112,120},{120,128},{12... | collective-permute-start | bytes 786440 | tf_op jit(solution)/shard_map/ppermute | solution.py:459
  41.0 0.7 collective-permute-start.12
  41.6 0.7 collective-permute-start.11
  42.3 0.7 collective-permute-start.10
  43.0 6.8 %collective-permute-done.9.refs_2_.handed_ref = f32[2,64,512]{2,1,0:T(8,128)S(1)} collective-permute-done((f32[2,64,512]{2,1,0:T(8,128)S(1)}, f32[2,64,512]{2,1,0:T(8,128)S(1)}, u32[]{:S(2)}, u32[]{:S(2)}) %collective-permute-start.9) | collective-permute-done | bytes 262176 | tf_op jit(solution)/shard_map/ppermute | solution.py:459
  49.8 0.1 chain1.1
  49.9 0.7 collective-permute-start.15
  50.6 0.7 collective-permute-start.14
  51.3 0.7 collective-permute-start.13
  52.0 0.1 chain2.1
  52.1 0.7 collective-permute-start.16
  52.7 1.3 %collective-permute-start.19 = (f32[2,4,16,128]{3,2,1,0:T(8,128)S(1)}, f32[2,4,16,128]{3,2,1,0:T(8,128)S(1)}, u32[]{:S(2)}, u32[]{:S(2)}) collective-permute-start(f32[2,4,16,128]{3,2,1,0:T(8,128)S(1)} %get-tuple-element.44), channel_id=1, source_target_pairs={{128,223},{136,192},{144,200},{152,208},{129,216},{137,193},{145,2... | collective-permute-start | bytes 196616 | tf_op jit(solution)/shard_map/ppermute | solution.py:469
  54.0 1.3 %collective-permute-start.18 = (f32[2,4,16,128]{3,2,1,0:T(8,128)S(1)}, f32[2,4,16,128]{3,2,1,0:T(8,128)S(1)}, u32[]{:S(2)}, u32[]{:S(2)}) collective-permute-start(f32[2,4,16,128]{3,2,1,0:T(8,128)S(1)} %get-tuple-element.44), channel_id=1, source_target_pairs={{128,200},{136,208},{144,216},{152,193},{129,201},{137,209},{145,2... | collective-permute-start | bytes 196616 | tf_op jit(solution)/shard_map/ppermute | solution.py:469
  55.3 1.3 %collective-permute-start.17 = (f32[2,4,16,128]{3,2,1,0:T(8,128)S(1)}, f32[2,4,16,128]{3,2,1,0:T(8,128)S(1)}, u32[]{:S(2)}, u32[]{:S(2)}) collective-permute-start(f32[2,4,16,128]{3,2,1,0:T(8,128)S(1)} %get-tuple-element.44), channel_id=1, source_target_pairs={{128,192},{136,200},{144,208},{152,216},{129,193},{137,201},{145,2... | collective-permute-start | bytes 196616 | tf_op jit(solution)/shard_map/ppermute | solution.py:469
  56.6 14.5 %collective-permute-done.19.refs_7_ = f32[2,4,16,128]{3,2,1,0:T(8,128)S(1)} collective-permute-done((f32[2,4,16,128]{3,2,1,0:T(8,128)S(1)}, f32[2,4,16,128]{3,2,1,0:T(8,128)S(1)}, u32[]{:S(2)}, u32[]{:S(2)}) %collective-permute-start.19) | collective-permute-done | bytes 65568 | tf_op jit(solution)/shard_map/ppermute | solution.py:469
  71.2 3.3 %collective-permute-done.18.refs_6_ = f32[2,4,16,128]{3,2,1,0:T(8,128)S(1)} collective-permute-done((f32[2,4,16,128]{3,2,1,0:T(8,128)S(1)}, f32[2,4,16,128]{3,2,1,0:T(8,128)S(1)}, u32[]{:S(2)}, u32[]{:S(2)}) %collective-permute-start.18) | collective-permute-done | bytes 65568 | tf_op jit(solution)/shard_map/ppermute | solution.py:469
  74.5 0.7 collective-permute-done.17.refs_5_
  75.2 2.9 %chain3.1 = (f32[8,128]{1,0:T(8,128)}, f32[8,2,4,16,128]{4,3,2,1,0:T(8,128)S(1)}, f32[2,4,16,128]{3,2,1,0:T(8,128)}) custom-call(s32[1]{0:T(128)} %bitcast.where_ref.refs_0_, f32[4,7,8,512]{3,2,1,0:T(8,128)S(1)} %prep.1.refs_1_, f32[2,64,512]{2,1,0:T(8,128)S(1)} %collective-permute-done.9.refs_2_.handed_ref, ...), custom_call_target="tpu_custom_call", output_to_operand_aliasing={{1}: (8, {})} | custom-call | tf_op jit(solution)/shard_map/chain3/pallas_call | solution.py:442
  78.2 13.1 %all_to_all.5.got_ref = f32[8,2,4,16,128]{4,3,2,1,0:T(8,128)S(1)} all-to-all(f32[8,2,4,16,128]{4,3,2,1,0:T(8,128)S(1)} %get-tuple-element.46), channel_id=1, replica_groups={{0,8,16,24,32,40,48,56},{64,72,80,88,96,104,112,120},{128,136,144,152,1..., dimensions={0} | all-to-all | bytes 1048576 | tf_op jit(solution)/shard_map/all_to_all | solution.py:472
  91.3 0.0 collective-permute-start.21
  91.4 0.5 collective-permute-start.20
  91.9 1.4 %collective-permute-done.21.hi_ref = f32[2,4,16,128]{3,2,1,0:T(8,128)S(1)} collective-permute-done((f32[2,4,16,128]{3,2,1,0:T(8,128)S(1)}, f32[2,4,16,128]{3,2,1,0:T(8,128)S(1)}, u32[]{:S(2)}, u32[]{:S(2)}) %collective-permute-start.21) | collective-permute-done | bytes 65568 | tf_op jit(solution)/shard_map/ppermute | solution.py:474
  93.3 3.0 %collective-permute-done.20.lo_ref = f32[2,4,16,128]{3,2,1,0:T(8,128)S(1)} collective-permute-done((f32[2,4,16,128]{3,2,1,0:T(8,128)S(1)}, f32[2,4,16,128]{3,2,1,0:T(8,128)S(1)}, u32[]{:S(2)}, u32[]{:S(2)}) %collective-permute-start.20) | collective-permute-done | bytes 65568 | tf_op jit(solution)/shard_map/ppermute | solution.py:473
  96.3 5.5 %final.1 = (f32[1,2,64,512]{3,2,1,0:T(8,128)}, f32[1,2,64,512]{3,2,1,0:T(8,128)}, f32[1,2,64,512]{3,2,1,0:T(8,128)}) custom-call(s32[1]{0:T(128)} %bitcast.where_ref.refs_0_, f32[8,2,4,16,128]{4,3,2,1,0:T(8,128)S(1)} %all_to_all.5.got_ref, f32[2,4,16,128]{3,2,1,0:T(8,128)S(1)} %collective-permute-done.20.lo_ref, ...), custom_call_target="tpu_custom_call" | custom-call | tf_op jit(solution)/shard_map/final/pallas_call | solution.py:477
  (15 shorter events, 0.0 us)
Async XLA Ops:
  2.4 6.5 %collective-permute-start = (f32[3,32,512]{2,1,0:T(8,128)}, f32[3,32,512]{2,1,0:T(8,128)S(1)}, u32[]{:S(2)}, u32[]{:S(2)}) collective-permute-start(f32[3,32,512]{2,1,0:T(8,128)} %get-tuple-element.25), channel_id=1, source_target_pairs={{0,1},{1,2},{2,3},{3,4},{4,5},{5,6},{6,7},{7,0},{8,9},{9,10},{10,1... | collective-permute-start | bytes 589832 | tf_op jit(solution)/shard_map/ppermute | solution.py:385
  2.4 6.5 %collective-permute-start.1 = (f32[3,32,512]{2,1,0:T(8,128)}, f32[3,32,512]{2,1,0:T(8,128)S(1)}, u32[]{:S(2)}, u32[]{:S(2)}) collective-permute-start(f32[3,32,512]{2,1,0:T(8,128)} %get-tuple-element.26), channel_id=1, source_target_pairs={{1,0},{2,1},{3,2},{4,3},{5,4},{6,5},{7,6},{0,7},{9,8},{10,9},{11,1... | collective-permute-start | bytes 589832 | tf_op jit(solution)/shard_map/ppermute | solution.py:386
  5.3 0.9 copy-start
  6.3 0.9 copy-start.2
  15.8 7.9 %collective-permute-start.5 = (f32[2,4,32,128]{3,2,1,0:T(8,128)S(1)}, f32[2,4,32,128]{3,2,1,0:T(8,128)S(1)}, u32[]{:S(2)}, u32[]{:S(2)}) collective-permute-start(f32[2,4,32,128]{3,2,1,0:T(8,128)S(1)} %get-tuple-element.33), channel_id=1, source_target_pairs={{32,0},{0,32},{40,8},{8,40},{48,16},{16,48},{56,24},{24,56},{96,64... | collective-permute-start | bytes 393224 | tf_op jit(solution)/shard_map/ppermute | solution.py:426
  17.0 10.1 %collective-permute-start.6 = (f32[2,4,32,128]{3,2,1,0:T(8,128)S(1)}, f32[2,4,32,128]{3,2,1,0:T(8,128)S(1)}, u32[]{:S(2)}, u32[]{:S(2)}) collective-permute-start(f32[2,4,32,128]{3,2,1,0:T(8,128)S(1)} %get-tuple-element.34), channel_id=1, source_target_pairs={{32,8},{8,32},{40,16},{16,40},{48,24},{24,48},{56,0},{0,56},{96,72... | collective-permute-start | bytes 393224 | tf_op jit(solution)/shard_map/ppermute | solution.py:426
  20.4 17.4 %collective-permute-start.2 = (f32[2,4,48,128]{3,2,1,0:T(8,128)S(1)}, f32[2,4,48,128]{3,2,1,0:T(8,128)S(1)}, u32[]{:S(2)}, u32[]{:S(2)}) collective-permute-start(f32[2,4,48,128]{3,2,1,0:T(8,128)S(1)} %get-tuple-element.30), channel_id=1, source_target_pairs={{0,8},{8,16},{16,24},{24,0},{32,40},{40,48},{48,56},{56,32},{64,72... | collective-permute-start | bytes 589832 | tf_op jit(solution)/shard_map/ppermute | solution.py:419
  20.4 17.4 %collective-permute-start.3 = (f32[2,4,48,128]{3,2,1,0:T(8,128)S(1)}, f32[2,4,48,128]{3,2,1,0:T(8,128)S(1)}, u32[]{:S(2)}, u32[]{:S(2)}) collective-permute-start(f32[2,4,48,128]{3,2,1,0:T(8,128)S(1)} %get-tuple-element.31), channel_id=1, source_target_pairs={{0,16},{8,24},{16,0},{24,8},{32,48},{40,56},{48,32},{56,40},{64,80... | collective-permute-start | bytes 589832 | tf_op jit(solution)/shard_map/ppermute | solution.py:419
  22.6 16.1 %collective-permute-start.4 = (f32[2,4,48,128]{3,2,1,0:T(8,128)S(1)}, f32[2,4,48,128]{3,2,1,0:T(8,128)S(1)}, u32[]{:S(2)}, u32[]{:S(2)}) collective-permute-start(f32[2,4,48,128]{3,2,1,0:T(8,128)S(1)} %get-tuple-element.32), channel_id=1, source_target_pairs={{0,24},{8,0},{16,8},{24,16},{32,56},{40,32},{48,40},{56,48},{64,88... | collective-permute-start | bytes 589832 | tf_op jit(solution)/shard_map/ppermute | solution.py:419
  23.7 8.5 %collective-permute-start.7 = (f32[2,4,32,128]{3,2,1,0:T(8,128)S(1)}, f32[2,4,32,128]{3,2,1,0:T(8,128)S(1)}, u32[]{:S(2)}, u32[]{:S(2)}) collective-permute-start(f32[2,4,32,128]{3,2,1,0:T(8,128)S(1)} %get-tuple-element.35), channel_id=1, source_target_pairs={{32,16},{16,32},{40,24},{24,40},{48,0},{0,48},{56,8},{8,56},{96,80... | collective-permute-start | bytes 393224 | tf_op jit(solution)/shard_map/ppermute | solution.py:426
  27.1 5.9 %collective-permute-start.8 = (f32[2,4,32,128]{3,2,1,0:T(8,128)S(1)}, f32[2,4,32,128]{3,2,1,0:T(8,128)S(1)}, u32[]{:S(2)}, u32[]{:S(2)}) collective-permute-start(f32[2,4,32,128]{3,2,1,0:T(8,128)S(1)} %get-tuple-element.36), channel_id=1, source_target_pairs={{32,24},{24,32},{40,0},{0,40},{48,8},{8,48},{56,16},{16,56},{96,88... | collective-permute-start | bytes 393224 | tf_op jit(solution)/shard_map/ppermute | solution.py:426
  38.8 11.0 %collective-permute-start.9 = (f32[2,64,512]{2,1,0:T(8,128)S(1)}, f32[2,64,512]{2,1,0:T(8,128)S(1)}, u32[]{:S(2)}, u32[]{:S(2)}) collective-permute-start(f32[2,64,512]{2,1,0:T(8,128)S(1)} %get-tuple-element.37.refs_2_), channel_id=1, source_target_pairs={{32,40},{40,48},{48,56},{96,104},{104,112},{112,120},{120,128},{12... | collective-permute-start | bytes 786440 | tf_op jit(solution)/shard_map/ppermute | solution.py:459
  41.0 2.0 %collective-permute-start.12 = (f32[2,4,16,128]{3,2,1,0:T(8,128)S(1)}, f32[2,4,16,128]{3,2,1,0:T(8,128)S(1)}, u32[]{:S(2)}, u32[]{:S(2)}) collective-permute-start(f32[2,4,16,128]{3,2,1,0:T(8,128)S(1)} %get-tuple-element.39), channel_id=1, source_target_pairs={{0,95},{8,64},{16,72},{24,80},{1,88},{9,65},{17,73},{25,81},{2,89}... | collective-permute-start | bytes 196616 | tf_op jit(solution)/shard_map/ppermute | solution.py:469
  41.6 1.4 %collective-permute-start.11 = (f32[2,4,16,128]{3,2,1,0:T(8,128)S(1)}, f32[2,4,16,128]{3,2,1,0:T(8,128)S(1)}, u32[]{:S(2)}, u32[]{:S(2)}) collective-permute-start(f32[2,4,16,128]{3,2,1,0:T(8,128)S(1)} %get-tuple-element.39), channel_id=1, source_target_pairs={{0,72},{8,80},{16,88},{24,65},{1,73},{9,81},{17,89},{25,66},{2,74}... | collective-permute-start | bytes 196616 | tf_op jit(solution)/shard_map/ppermute | solution.py:469
  42.3 0.7 collective-permute-start.10
  49.9 2.0 %collective-permute-start.15 = (f32[2,4,16,128]{3,2,1,0:T(8,128)S(1)}, f32[2,4,16,128]{3,2,1,0:T(8,128)S(1)}, u32[]{:S(2)}, u32[]{:S(2)}) collective-permute-start(f32[2,4,16,128]{3,2,1,0:T(8,128)S(1)} %get-tuple-element.41), channel_id=1, source_target_pairs={{64,159},{72,128},{80,136},{88,144},{65,152},{73,129},{81,137},{89... | collective-permute-start | bytes 196616 | tf_op jit(solution)/shard_map/ppermute | solution.py:469
  50.6 1.4 %collective-permute-start.14 = (f32[2,4,16,128]{3,2,1,0:T(8,128)S(1)}, f32[2,4,16,128]{3,2,1,0:T(8,128)S(1)}, u32[]{:S(2)}, u32[]{:S(2)}) collective-permute-start(f32[2,4,16,128]{3,2,1,0:T(8,128)S(1)} %get-tuple-element.41), channel_id=1, source_target_pairs={{64,136},{72,144},{80,152},{88,129},{65,137},{73,145},{81,153},{89... | collective-permute-start | bytes 196616 | tf_op jit(solution)/shard_map/ppermute | solution.py:469
  51.3 0.7 collective-permute-start.13
  52.1 23.2 %collective-permute-start.16 = (f32[2,64,512]{2,1,0:T(8,128)S(1)}, f32[2,64,512]{2,1,0:T(8,128)S(1)}, u32[]{:S(2)}, u32[]{:S(2)}) collective-permute-start(f32[2,64,512]{2,1,0:T(8,128)S(1)} %get-tuple-element.43), channel_id=1, source_target_pairs={{0,8},{8,16},{16,24},{24,32},{56,64},{64,72},{72,80},{80,88},{88,9... | collective-permute-start | bytes 786440 | tf_op jit(solution)/shard_map/ppermute | solution.py:459
  52.7 18.4 %collective-permute-start.19 = (f32[2,4,16,128]{3,2,1,0:T(8,128)S(1)}, f32[2,4,16,128]{3,2,1,0:T(8,128)S(1)}, u32[]{:S(2)}, u32[]{:S(2)}) collective-permute-start(f32[2,4,16,128]{3,2,1,0:T(8,128)S(1)} %get-tuple-element.44), channel_id=1, source_target_pairs={{128,223},{136,192},{144,200},{152,208},{129,216},{137,193},{145,2... | collective-permute-start | bytes 196616 | tf_op jit(solution)/shard_map/ppermute | solution.py:469
  54.0 20.5 %collective-permute-start.18 = (f32[2,4,16,128]{3,2,1,0:T(8,128)S(1)}, f32[2,4,16,128]{3,2,1,0:T(8,128)S(1)}, u32[]{:S(2)}, u32[]{:S(2)}) collective-permute-start(f32[2,4,16,128]{3,2,1,0:T(8,128)S(1)} %get-tuple-element.44), channel_id=1, source_target_pairs={{128,200},{136,208},{144,216},{152,193},{129,201},{137,209},{145,2... | collective-permute-start | bytes 196616 | tf_op jit(solution)/shard_map/ppermute | solution.py:469
  55.3 19.9 %collective-permute-start.17 = (f32[2,4,16,128]{3,2,1,0:T(8,128)S(1)}, f32[2,4,16,128]{3,2,1,0:T(8,128)S(1)}, u32[]{:S(2)}, u32[]{:S(2)}) collective-permute-start(f32[2,4,16,128]{3,2,1,0:T(8,128)S(1)} %get-tuple-element.44), channel_id=1, source_target_pairs={{128,192},{136,200},{144,208},{152,216},{129,193},{137,201},{145,2... | collective-permute-start | bytes 196616 | tf_op jit(solution)/shard_map/ppermute | solution.py:469
  75.2 21.0 %copy-start.1 = (f32[1,2,64,512]{3,2,1,0:T(8,128)S(1)}, f32[1,2,64,512]{3,2,1,0:T(8,128)}, u32[]{:S(2)}) copy-start(f32[1,2,64,512]{3,2,1,0:T(8,128)} %c_ref.5) | copy-start | bytes 786436
  75.2 21.0 %copy-start.3 = (f32[64,512]{1,0:T(8,128)S(1)}, f32[64,512]{1,0:T(8,128)}, u32[]{:S(2)}) copy-start(f32[64,512]{1,0:T(8,128)} %n_ref.5) | copy-start | bytes 393220
  91.3 1.9 %collective-permute-start.21 = (f32[2,4,16,128]{3,2,1,0:T(8,128)S(1)}, f32[2,4,16,128]{3,2,1,0:T(8,128)S(1)}, u32[]{:S(2)}, u32[]{:S(2)}) collective-permute-start(f32[2,4,16,128]{3,2,1,0:T(8,128)S(1)} %get-tuple-element.47), channel_id=1, source_target_pairs={{1,0},{2,1},{3,2},{4,3},{5,4},{6,5},{7,6},{0,7},{9,8},{10,9},{11,1... | collective-permute-start | bytes 196616 | tf_op jit(solution)/shard_map/ppermute | solution.py:474
  91.4 4.9 %collective-permute-start.20 = (f32[2,4,16,128]{3,2,1,0:T(8,128)S(1)}, f32[2,4,16,128]{3,2,1,0:T(8,128)S(1)}, u32[]{:S(2)}, u32[]{:S(2)}) collective-permute-start(f32[2,4,16,128]{3,2,1,0:T(8,128)S(1)} %get-tuple-element.48), channel_id=1, source_target_pairs={{0,1},{1,2},{2,3},{3,4},{4,5},{5,6},{6,7},{7,0},{8,9},{9,10},{10,1... | collective-permute-start | bytes 196616 | tf_op jit(solution)/shard_map/ppermute | solution.py:473

commit v4 on v3

--- a/solution.py
+++ b/solution.py
@@ -14,6 +14,8 @@
 EDGE = 32
 WINDOW = STRIP + 2 * HALO
 INNER = 8
+TIGHT = STRIP + 2 * INNER
+FINAL = 96
 LANES = 128
 SPLIT = 4
 advect_scale = 0.1
@@ -101,8 +103,10 @@
     euler(mid, coef, n, to_dst)
 
 
-def plane(nat, i, n):
-    return jnp.concatenate([nat[b, pl.ds(i, 8, stride=n), :] for b in range(nat.shape[0])], axis=1)
+def plane(nat, i, n, first=0):
+    return jnp.concatenate(
+        [nat[b, pl.ds(first + i, 8, stride=n), :] for b in range(nat.shape[0])], axis=1
+    )
 
 
 def put_plane(nat, i, n, value):
@@ -110,8 +114,8 @@
         nat[b, pl.ds(i, 8, stride=n), :] = value[:, b * LANES : (b + 1) * LANES]
 
 
-def load_planes(nat, n):
-    return [plane(nat, i, n) for i in range(n)]
+def load_planes(nat, n, first=0):
+    return [plane(nat, i, n, first) for i in range(n)]
 
 
 def fill(nat, at, ref, start, count):
@@ -205,41 +209,43 @@
         ref[...] = nat[0:2, :, pl.ds(pl.multiple_of(first, 8), WINDOW), :]
     for k, ref in enumerate((far0, far1, far2, far3)):
         first = lax.rem(position + k, SPLIT) * STRIP + (EDGE - INNER)
-        ref[...] = nat[0:2, :, pl.ds(pl.multiple_of(first, 8), STRIP + 2 * INNER), :]
+        ref[...] = nat[0:2, :, pl.ds(pl.multiple_of(first, 8), TIGHT), :]
     for copy in started:
         copy.wait()
 
 
-def prep_kernel(nwin_ref, cc_ref):
-    make_coefs(load_planes(nwin_ref, WINDOW // 8), coarse_size, [cc_ref.at[i] for i in range(4)])
+def prep_kernel(nwin_ref, wide_ref, tight_ref):
+    wide = [wide_ref.at[i] for i in range(4)]
+    tight = [tight_ref.at[i] for i in range(4)]
+    make_coefs(load_planes(nwin_ref, WINDOW // 8), coarse_size, wide)
+    make_coefs(load_planes(nwin_ref, TIGHT // 8, HALO - INNER), coarse_size, tight)
 
 
 def chain_kernel(stage, stages, carried, *refs):
     refs = list(refs)
-    where_ref, cc_ref = refs[:2]
-    nat, w, mid = refs[-3:]
-    corr_ref, last_ref = refs[-5:-3]
-    n = WINDOW // 8
+    where_ref, wide_ref, tight_ref = refs[:3]
+    nat, w, mid, nat_t, w_t, mid_t = refs[-6:]
+    if stage + 1 < stages:
+        last_ref = refs.pop(-7)
+    corr_ref = refs[-7]
+    n, n_t = WINDOW // 8, TIGHT // 8
     position = where_ref[0]
     planes = GROUP // SPLIT
-    rest = refs[2 + carried :]
+    rest = refs[3 + carried :]
     if stage == 0:
-        tau_ref = refs[-6]
+        near_ref, far_ref = refs[-9:-7]
         for k in range(SPLIT):
             source = lax.rem(position + SPLIT - k, SPLIT)
-            tau_ref[source] = rest[k][...]
-            far = source + SPLIT
-            tau_ref[far, :, :, 0:INNER, :] = jnp.zeros_like(rest[0][:, :, 0:INNER, :])
-            tau_ref[far, :, :, WINDOW - INNER :, :] = jnp.zeros_like(rest[0][:, :, 0:INNER, :])
-            tau_ref[far, :, :, INNER : WINDOW - INNER, :] = rest[SPLIT + k][...]
+            near_ref[source] = rest[k][...]
+            far_ref[source] = rest[SPLIT + k][...]
     else:
-        tau_ref = rest[0]
-        own, above, below, corr_in = rest[1:5]
+        near_ref, far_ref, own, pair, other, corr_in = rest[:6]
     active = position // SPLIT == stage * planes
 
     @pl.when(active)
     def _():
-        coef = [cc_ref.at[i] for i in range(4)]
+        wide = [wide_ref.at[i] for i in range(4)]
+        tight = [tight_ref.at[i] for i in range(4)]
 
         def keep(out):
             for c in range(2):
@@ -248,19 +254,33 @@
                 out[c] = nat[c, :, HALO : HALO + STRIP, :]
 
         def one(t, out):
-            heun(w, mid, w, coef, n, lambda c, i: plane(tau_ref.at[t, c], i, n))
+            heun(w, mid, w, wide, n, lambda c, i: plane(near_ref.at[t, c], i, n))
             keep(out)
+
+        def one_tight(t, out):
+            heun(w_t, mid_t, w_t, tight, n_t, lambda c, i: plane(far_ref.at[t - SPLIT, c], i, n_t))
+            for c in range(2):
+                for i in range(n_t):
+                    put_plane(nat_t.at[c], i, n_t, w_t[c, i])
+                out[c] = nat_t[c, :, INNER : INNER + STRIP, :]
 
         if stage == 0:
             for c in range(2):
                 corr_ref[0, c] = jnp.zeros_like(corr_ref[0, c])
                 for i in range(n):
-                    w[c, i] = plane(tau_ref.at[0, c], i, n)
+                    w[c, i] = plane(near_ref.at[0, c], i, n)
             keep(corr_ref.at[1])
         else:
+            even = lax.rem(position, 2) == 0
+            for choice, refs_in_order in ((even, (other, own, pair)), (jnp.logical_not(even), (pair, own, other))):
+
+                @pl.when(choice)
+                def _():
+                    for c in range(2):
+                        for k, ref in enumerate(refs_in_order):
+                            nat[c, :, k * STRIP : (k + 1) * STRIP, :] = ref[c]
+
             for c in range(2):
-                for k, ref in enumerate((above, own, below)):
-                    nat[c, :, k * STRIP : (k + 1) * STRIP, :] = ref[c]
                 corr_ref[0, c] = own[c]
                 for i in range(n):
                     w[c, i] = plane(nat.at[c], i, n)
@@ -270,9 +290,17 @@
             one(t, corr_ref.at[t + 1])
             return carry
 
-        lax.fori_loop(1, GROUP - 1, step, 0)
+        def step_tight(t, carry):
+            one_tight(t, corr_ref.at[t + 1])
+            return carry
+
+        lax.fori_loop(1, SPLIT, step, 0)
+        for c in range(2):
+            for i in range(n_t):
+                w_t[c, i] = plane(nat.at[c], i, n_t, HALO - INNER)
+        lax.fori_loop(SPLIT, GROUP - 1, step_tight, 0)
         if stage + 1 < stages:
-            one(GROUP - 1, last_ref)
+            one_tight(GROUP - 1, last_ref)
 
     if stage > 0:
 
@@ -281,48 +309,67 @@
             corr_ref[...] = corr_in[...]
 
 
-def final_kernel(where_ref, got_ref, lo_ref, hi_ref, c_ref, clo_ref, chi_ref,
-                 n_ref, handed_ref, handed2_ref,
-                 corr_ref, adv_ref, defect_ref,
-                 nat, vnat, anat, dbuf, w, mid, cf, sem):
-    n = 12
+def ready_kernel(where_ref, got_ref, c_ref, clo_ref, chi_ref, n_ref, handed_ref, handed2_ref,
+                 corr_ref, defect_ref, own_ref, cf_ref,
+                 vnat, dbuf, sem):
+    n = FINAL // 8
     rows = n_ref.shape[0]
-    blocks = nat.shape[1]
+    blocks = vnat.shape[0]
     position = where_ref[0]
+
+    @pl.when(position == 0)
+    def _():
+        for c in range(2):
+            dbuf[c] = jnp.zeros_like(dbuf[c])
+            fill(own_ref.at[c], 0, c_ref.at[0, c], 0, rows)
+
+    @pl.when(position != 0)
+    def _():
+        back = 1.0 / COARSE
+        for c in range(2):
+            dbuf[c] = (handed_ref[c] + handed2_ref[c]) - c_ref[0, c]
+            for q in range(SPLIT):
+                own_ref[c, :, q * STRIP : (q + 1) * STRIP, :] = back * got_ref[q, c]
+
+    both = pl.ds(0, 2)
+    pairs = [(dbuf, defect_ref.at[0])]
+    for b in range(blocks):
+        pairs.append((own_ref.at[both, b], corr_ref.at[0, both, :, cut(b)]))
+    started = copies(pairs, sem)
     fill(vnat, 0, clo_ref.at[2], EDGE - HALO, HALO)
     fill(vnat, HALO, n_ref, 0, rows)
     fill(vnat, HALO + rows, chi_ref.at[2], 0, HALO)
-    coef = [cf.at[i] for i in range(4)]
-    make_coefs(load_planes(vnat, n), coarse_size / STEPS, coef)
+    make_coefs(load_planes(vnat, n), coarse_size / STEPS, [cf_ref.at[i] for i in range(4)])
+    for copy in started:
+        copy.wait()
+
+
+def final_kernel(where_ref, own_ref, lo_ref, hi_ref, clo_ref, chi_ref, cf_ref,
+                 adv_ref,
+                 nat, anat, w, mid, sem):
+    n = FINAL // 8
+    rows = own_ref.shape[2]
+    blocks = nat.shape[1]
+    position = where_ref[0]
+    coef = [cf_ref.at[i] for i in range(4)]
 
     @pl.when(position == 0)
     def _():
         for c in range(2):
-            dbuf[c] = jnp.zeros_like(dbuf[c])
-            for b in range(blocks):
-                own = slice(b * LANES, (b + 1) * LANES)
-                nat[c, b, 0:HALO, :] = clo_ref[c, EDGE - HALO :, own]
-                nat[c, b, HALO : HALO + rows, :] = c_ref[0, c, :, own]
-                nat[c, b, HALO + rows :, :] = chi_ref[c, 0:HALO, own]
+            fill(nat.at[c], 0, clo_ref.at[c], EDGE - HALO, HALO)
+            fill(nat.at[c], HALO + rows, chi_ref.at[c], 0, HALO)
 
     @pl.when(position != 0)
     def _():
         back = 1.0 / COARSE
         for c in range(2):
-            dbuf[c] = (handed_ref[c] + handed2_ref[c]) - c_ref[0, c]
             nat[c, :, 0:HALO, :] = back * lo_ref[c]
             nat[c, :, HALO + rows :, :] = back * hi_ref[c]
-            for q in range(SPLIT):
-                at = HALO + q * STRIP
-                nat[c, :, at : at + STRIP, :] = back * got_ref[q, c]
 
     both = pl.ds(0, 2)
     mine = pl.ds(HALO, rows)
-    pairs = [(dbuf, defect_ref.at[0])]
-    for b in range(blocks):
-        pairs.append((nat.at[both, b, mine, :], corr_ref.at[0, both, :, cut(b)]))
-    started = copies(pairs, sem)
     for c in range(2):
+        nat[c, :, HALO : HALO + rows, :] = own_ref[c]
         for i in range(n):
             w[c, i] = FINE * plane(nat.at[c], i, n)
 
@@ -331,13 +378,14 @@
         return carry
 
     lax.fori_loop(0, STEPS, step, 0)
-    for c in range(2):
-        for i in range(n):
-            put_plane(anat.at[c], i, n, w[c, i] * (1.0 / FINE))
-    pairs = []
+    started = []
     for b in range(blocks):
-        pairs.append((anat.at[both, b, mine, :], adv_ref.at[0, both, :, cut(b)]))
-    started += copies(pairs, sem.at[pl.ds(1 + blocks, blocks)])
+        for c in range(2):
+            for i in range(n):
+                part = w[c, i, :, b * LANES : (b + 1) * LANES]
+                anat[c, b, pl.ds(i, 8, stride=n), :] = part * (1.0 / FINE)
+        pair = (anat.at[both, b, mine, :], adv_ref.at[0, both, :, cut(b)])
+        started += copies([pair], sem.at[pl.ds(b, 1)])
     for copy in started:
         copy.wait()
 
@@ -387,7 +435,7 @@
 
     n = 16
     window = shape(2, blocks, WINDOW, LANES)
-    inner = shape(2, blocks, STRIP + 2 * INNER, LANES)
+    inner = shape(2, blocks, TIGHT, LANES)
     forward, nwin, *sent = pl.pallas_call(
         forward_kernel,
         out_shape=(shape(2, rows, cols), shape(blocks, WINDOW, LANES)) + (window,) * SPLIT + (inner,) * SPLIT,
@@ -402,12 +450,12 @@
         name="forward",
     )(where, own, lo, hi)
 
-    n = WINDOW // 8
-    cc = pl.pallas_call(
+    n, n_t = WINDOW // 8, TIGHT // 8
+    coefs = pl.pallas_call(
         prep_kernel,
-        out_shape=shape(4, n + 1, 8, cols),
+        out_shape=(shape(4, n + 1, 8, cols), shape(4, n_t + 1, 8, cols)),
         in_specs=[VMEM],
-        out_specs=VMEM,
+        out_specs=(VMEM, VMEM),
         compiler_params=PARAMS,
         name="prep",
     )(nwin)
@@ -427,65 +475,81 @@
     groups = [[g * GROUP + j for j in range(GROUP)] for g in range(stages)]
 
     strips = ring * SPLIT
-    pieces, corr, handed = [], [], []
+    pieces, handed = [], []
     for stage in range(stages):
-        extra = {0: [forward], 1: handed, stages - 2: [forward], stages - 1: handed}[stage]
         carries = stage in (0, stages - 2)
-        operands = [where, cc] + extra + (gathered if stage == 0 else [taus] + pieces + corr)
-        specs = [SMEM, VMEM] + [HBM] * len(extra) + [VMEM] * (len(operands) - 2 - len(extra))
+        extra = ([forward] if carries else []) + (handed if stage >= stages - 2 else [])
+        operands = [where, *coefs] + extra + (gathered if stage == 0 else [*taus, *pieces, corr])
+        specs = [SMEM, VMEM, VMEM] + [HBM] * len(extra) + [VMEM] * (len(operands) - 3 - len(extra))
         shapes = [shape(2, rows, cols) if carries else shape(8, LANES)]
-        shapes += [shape(GROUP, 2, blocks, WINDOW, LANES)] if stage == 0 else []
-        shapes += [shape(GROUP, 2, blocks, STRIP, LANES), shape(2, blocks, STRIP, LANES)]
+        if stage == 0:
+            shapes += [shape(SPLIT, 2, blocks, WINDOW, LANES), shape(SPLIT, 2, blocks, TIGHT, LANES)]
+        shapes += [shape(GROUP, 2, blocks, STRIP, LANES)]
+        shapes += [shape(2, blocks, STRIP, LANES)] if stage + 1 < stages else []
         aliases = {len(operands) - 1: 1} if stage > 0 else {}
         if carries:
-            aliases[2] = 0
+            aliases[3] = 0
         done = pl.pallas_call(
             functools.partial(chain_kernel, stage, stages, len(extra)),
             out_shape=tuple(shapes),
             in_specs=specs,
             out_specs=(HBM,) + (VMEM,) * (len(shapes) - 1),
-            scratch_shapes=[vm(2, blocks, WINDOW, LANES), vm(2, n, 8, cols), vm(2, n, 8, cols)],
+            scratch_shapes=[
+                vm(2, blocks, WINDOW, LANES), vm(2, n, 8, cols), vm(2, n, 8, cols),
+                vm(2, blocks, TIGHT, LANES), vm(2, n_t, 8, cols), vm(2, n_t, 8, cols),
+            ],
             input_output_aliases=aliases,
             compiler_params=PARAMS,
             name="chain%d" % stage,
         )(*operands)
         if stage == 0:
-            taus = done[1]
-        corr, last = [done[-2]], done[-1]
+            taus = done[1:3]
+        corr, last = done[-2:] if stage + 1 < stages else (done[-1], None)
         if carries:
             forward = done[0]
             chain = [g * GROUP + q for g in range(2) for q in range(SPLIT)]
             pairs = [(i, i + 1) for i in range(intervals - 1) if (i in chain or i + 1 in chain) == (stage > 0)]
             handed = handed + [lax.ppermute(forward, "tm", pairs)]
         if stage + 1 < stages:
-            arrived = {}
-            for delta in (0, 1, -1):
+            pieces = []
+            moves = (lambda q: q, lambda q: q + 1 - 2 * (q % 2), lambda q: (q - 1 + 2 * (q % 2)) % strips)
+            for move in moves:
                 pairs = []
                 for strip in range(strips):
-                    to = (strip + delta) % strips
+                    to = move(strip)
                     source = stage * GROUP + strip % SPLIT
                     target = (stage + 1) * GROUP + to % SPLIT
                     pairs.append((source * ring + strip // SPLIT, target * ring + to // SPLIT))
-                arrived[delta] = lax.ppermute(last, ("tm", "space"), pairs)
-            pieces = [arrived[0], arrived[1], arrived[-1]]
-
-    got = lax.all_to_all(corr[0], "tm", 0, 0, axis_index_groups=groups)
+                pieces.append(lax.ppermute(last, ("tm", "space"), pairs))
+
+    got = lax.all_to_all(corr, "tm", 0, 0, axis_index_groups=groups)
     above = lax.ppermute(got[SPLIT - 1], "space", up)
     below = lax.ppermute(got[0], "space", down)
 
-    n = 12
-    return pl.pallas_call(
+    n = FINAL // 8
+    corrected, defect, mine, cf = pl.pallas_call(
+        ready_kernel,
+        out_shape=(shape(1, 2, rows, cols),) * 2 + (shape(2, blocks, rows, LANES), shape(4, n + 1, 8, cols)),
+        in_specs=[SMEM] + [VMEM] * 7,
+        out_specs=(ANY, ANY, VMEM, VMEM),
+        scratch_shapes=[vm(blocks, FINAL, LANES), vm(2, rows, cols), dma(1 + blocks)],
+        compiler_params=PARAMS,
+        cost_estimate=pl.CostEstimate(flops=10**6, bytes_accessed=2**21, transcendentals=0),
+        name="ready",
+    )(where, got, c_values, lo, hi, viscosity, *handed)
+    advanced = pl.pallas_call(
         final_kernel,
-        out_shape=(shape(1, 2, rows, cols),) * 3,
-        in_specs=[SMEM] + [VMEM] * 9,
-        out_specs=(ANY,) * 3,
+        out_shape=shape(1, 2, rows, cols),
+        in_specs=[SMEM] + [VMEM] * 6,
+        out_specs=ANY,
         scratch_shapes=[
-            vm(2, blocks, 8 * n, LANES), vm(blocks, 8 * n, LANES), vm(2, blocks, 8 * n, LANES), vm(2, rows, cols),
-            vm(2, n, 8, cols), vm(2, n, 8, cols), vm(4, n + 1, 8, cols), dma(1 + 2 * blocks),
+            vm(2, blocks, FINAL, LANES), vm(2, blocks, FINAL, LANES),
+            vm(2, n, 8, cols), vm(2, n, 8, cols), dma(blocks),
         ],
         compiler_params=PARAMS,
         name="final",
-    )(where, got, above, below, c_values, lo, hi, viscosity, *handed)
+    )(where, mine, above, below, lo, hi, cf)
+    return corrected, advanced, defect
 
 
 def solution(mesh):

time: 102 us -> 96.8 us (0.949)
  waiting for transfers between devices: 43.2 us -> 40.9 us
  local copies, waits for them, and re-layouts: 1.87 us -> 0.02 us
  blocking collectives: 13.1 us -> 11.7 us
    ppermute x2, waiting for transfers between devices: 6.84 us -> 4.7 us  [shards(): handed = handed + [lax.ppermute(forward, 'tm', pairs)]]
    unnamed x8 -> x4, local copies, waits for them, and re-layouts: 1.86 us -> 0.01 us
    ppermute x1, waiting for transfers between devices: 1.49 us -> 3.34 us  [shards(): lo = lax.ppermute(bottom, 'space', up)]
    ppermute x9, waiting for transfers between devices: 18.6 us -> 16.9 us  [shards(): pieces.append(lax.ppermute(last, ('tm', 'space'), pairs))]
    all_to_all x1, blocking collectives: 13.1 us -> 11.7 us  [shards(): got = lax.all_to_all(corr, 'tm', 0, 0, axis_index_groups=groups)]
    pallas_call x2 -> x3, Pallas kernels: 5.71 us -> 6.75 us  [the longest x1 5.69 us: shards(): pl.pallas_call(final_kernel, out_shape=shape(1, 2, rows, cols), in_specs=...]
  transfers between devices with their start and end apart: 22 -> 22, of which waited for: 12 -> 11; matrix products, arithmetic and copies ran while one was open for 0% -> 0% of each run, Pallas kernels for 0% -> 1%
where the time goes in v4:
time: 96.8 us; the launch traced here: 96.5 us
  waiting for transfers between devices  40.9 us (42%)
  starting transfers between devices  25.1 us (26%)
  Pallas kernels  17.9 us (18%)
  blocking collectives  11.7 us (12%)
    ppermute x9, waiting for transfers between devices, shards(): pieces.append(lax.ppermute(last, ('tm', 'space'), pairs))  16.9 us
    all_to_all x1, blocking collectives, shards(): got = lax.all_to_all(corr, 'tm', 0, 0, axis_index_groups=groups)  11.7 us
    ppermute x9, starting transfers between devices, shards(): pieces.append(lax.ppermute(last, ('tm', 'space'), pairs))  7.86 us
    ppermute x4, starting transfers between devices, shards(): gathered.append(lax.ppermute(sent[SPLIT + k], 'tm', pairs))  7.56 us
    pallas_call x1, Pallas kernels, shards(): pl.pallas_call(forward_kernel, out_shape=(shape(2, rows, cols), shape(blo...  6.9 us
    ppermute x4, waiting for transfers between devices, shards(): gathered.append(lax.ppermute(sent[SPLIT + k], 'tm', pairs))  6.1 us
    ppermute x3, waiting for transfers between devices, shards(): gathered.append(lax.ppermute(sent[k], 'tm', pairs))  5.75 us
    pallas_call x1, Pallas kernels, shards(): pl.pallas_call(final_kernel, out_shape=shape(1, 2, rows, cols), in_specs=...  5.69 us
  transfers between devices with their start and end apart: 22, of which 11 were waited for; matrix products, arithmetic and copies ran while one was open for 0% of the time, Pallas kernels for 1%

profile of v4, /device:TPU:192, one launch (start us, length us, event | category | flops | bytes accessed | tf_op | source)
XLA Modules:
  0.0 96.5 jit_solution(5248522237743963751)
XLA Ops:
  0.6 1.8 %edges.1 = (f32[3,32,512]{2,1,0:T(8,128)}, f32[3,32,512]{2,1,0:T(8,128)}) custom-call(f32[1,2,64,512]{3,2,1,0:T(8,128)} %c_ref.5, f32[64,512]{1,0:T(8,128)} %n_ref.5), custom_call_target="tpu_custom_call" | custom-call | tf_op jit(solution)/shard_map/edges/pallas_call | solution.py:414
  2.4 0.0 collective-permute-start
  2.5 2.9 %collective-permute-start.1 = (f32[3,32,512]{2,1,0:T(8,128)}, f32[3,32,512]{2,1,0:T(8,128)S(1)}, u32[]{:S(2)}, u32[]{:S(2)}) collective-permute-start(f32[3,32,512]{2,1,0:T(8,128)} %get-tuple-element.33), channel_id=1, source_target_pairs={{1,0},{2,1},{3,2},{4,3},{5,4},{6,5},{7,6},{0,7},{9,8},{10,9},{11,1... | collective-permute-start | bytes 589832 | tf_op jit(solution)/shard_map/ppermute | solution.py:434
  5.4 0.2 load.1.own_ref
  5.6 3.3 %collective-permute-done.lo_ref.clo_ref = f32[3,32,512]{2,1,0:T(8,128)S(1)} collective-permute-done((f32[3,32,512]{2,1,0:T(8,128)}, f32[3,32,512]{2,1,0:T(8,128)S(1)}, u32[]{:S(2)}, u32[]{:S(2)}) %collective-permute-start) | collective-permute-done | bytes 196640 | tf_op jit(solution)/shard_map/ppermute | solution.py:433
  9.0 6.9 %forward.1 = (f32[2,64,512]{2,1,0:T(8,128)S(1)}, f32[4,48,128]{2,1,0:T(8,128)S(1)}, f32[2,4,48,128]{3,2,1,0:T(8,128)S(1)}, f32[2,4,48,128]{3,2,1,0:T(8,128)S(1)}...) custom-call(s32[1]{0:T(128)} %bitcast.where_ref.refs_0_, ...), custom_call_target="tpu_custom_call" | custom-call | tf_op jit(solution)/shard_map/forward/pallas_call | solution.py:439
  15.9 1.1 %collective-permute-start.5 = (f32[2,4,32,128]{3,2,1,0:T(8,128)S(1)}, f32[2,4,32,128]{3,2,1,0:T(8,128)S(1)}, u32[]{:S(2)}, u32[]{:S(2)}) collective-permute-start(f32[2,4,32,128]{3,2,1,0:T(8,128)S(1)} %get-tuple-element.42), channel_id=1, source_target_pairs={{32,0},{0,32},{40,8},{8,40},{48,16},{16,48},{56,24},{24,56},{96,64... | collective-permute-start | bytes 393224 | tf_op jit(solution)/shard_map/ppermute | solution.py:474
  17.0 3.5 %collective-permute-start.6 = (f32[2,4,32,128]{3,2,1,0:T(8,128)S(1)}, f32[2,4,32,128]{3,2,1,0:T(8,128)S(1)}, u32[]{:S(2)}, u32[]{:S(2)}) collective-permute-start(f32[2,4,32,128]{3,2,1,0:T(8,128)S(1)} %get-tuple-element.43), channel_id=1, source_target_pairs={{32,8},{8,32},{40,16},{16,40},{48,24},{24,48},{56,0},{0,56},{96,72... | collective-permute-start | bytes 393224 | tf_op jit(solution)/shard_map/ppermute | solution.py:474
  20.5 0.0 collective-permute-start.2
  20.5 2.2 %collective-permute-start.3 = (f32[2,4,48,128]{3,2,1,0:T(8,128)S(1)}, f32[2,4,48,128]{3,2,1,0:T(8,128)S(1)}, u32[]{:S(2)}, u32[]{:S(2)}) collective-permute-start(f32[2,4,48,128]{3,2,1,0:T(8,128)S(1)} %get-tuple-element.40), channel_id=1, source_target_pairs={{0,16},{8,24},{16,0},{24,8},{32,48},{40,56},{48,32},{56,40},{64,80... | collective-permute-start | bytes 589832 | tf_op jit(solution)/shard_map/ppermute | solution.py:467
  22.7 1.1 %collective-permute-start.4 = (f32[2,4,48,128]{3,2,1,0:T(8,128)S(1)}, f32[2,4,48,128]{3,2,1,0:T(8,128)S(1)}, u32[]{:S(2)}, u32[]{:S(2)}) collective-permute-start(f32[2,4,48,128]{3,2,1,0:T(8,128)S(1)} %get-tuple-element.41), channel_id=1, source_target_pairs={{0,24},{8,0},{16,8},{24,16},{32,56},{40,32},{48,40},{56,48},{64,88... | collective-permute-start | bytes 589832 | tf_op jit(solution)/shard_map/ppermute | solution.py:467
  23.7 0.0 collective-permute-done.5.refs_8_
  23.7 2.2 %collective-permute-start.7 = (f32[2,4,32,128]{3,2,1,0:T(8,128)S(1)}, f32[2,4,32,128]{3,2,1,0:T(8,128)S(1)}, u32[]{:S(2)}, u32[]{:S(2)}) collective-permute-start(f32[2,4,32,128]{3,2,1,0:T(8,128)S(1)} %get-tuple-element.44), channel_id=1, source_target_pairs={{32,16},{16,32},{40,24},{24,40},{48,0},{0,48},{56,8},{8,56},{96,80... | collective-permute-start | bytes 393224 | tf_op jit(solution)/shard_map/ppermute | solution.py:474
  26.0 1.2 %collective-permute-done.6.refs_9_ = f32[2,4,32,128]{3,2,1,0:T(8,128)S(1)} collective-permute-done((f32[2,4,32,128]{3,2,1,0:T(8,128)S(1)}, f32[2,4,32,128]{3,2,1,0:T(8,128)S(1)}, u32[]{:S(2)}, u32[]{:S(2)}) %collective-permute-start.6) | collective-permute-done | bytes 131104 | tf_op jit(solution)/shard_map/ppermute | solution.py:474
  27.1 0.7 collective-permute-start.8
  27.9 0.2 prep.1
  28.1 4.2 %collective-permute-done.7.refs_10_ = f32[2,4,32,128]{3,2,1,0:T(8,128)S(1)} collective-permute-done((f32[2,4,32,128]{3,2,1,0:T(8,128)S(1)}, f32[2,4,32,128]{3,2,1,0:T(8,128)S(1)}, u32[]{:S(2)}, u32[]{:S(2)}) %collective-permute-start.7) | collective-permute-done | bytes 131104 | tf_op jit(solution)/shard_map/ppermute | solution.py:474
  32.3 0.7 collective-permute-done.8.refs_11_
  33.0 4.9 %collective-permute-done.2.refs_5_ = f32[2,4,48,128]{3,2,1,0:T(8,128)S(1)} collective-permute-done((f32[2,4,48,128]{3,2,1,0:T(8,128)S(1)}, f32[2,4,48,128]{3,2,1,0:T(8,128)S(1)}, u32[]{:S(2)}, u32[]{:S(2)}) %collective-permute-start.2) | collective-permute-done | bytes 196640 | tf_op jit(solution)/shard_map/ppermute | solution.py:467
  37.9 0.0 collective-permute-done.3.refs_6_
  37.9 0.8 collective-permute-done.4.refs_7_
  38.8 0.1 chain0.1
  38.8 2.1 %collective-permute-start.9 = (f32[2,64,512]{2,1,0:T(8,128)S(1)}, f32[2,64,512]{2,1,0:T(8,128)S(1)}, u32[]{:S(2)}, u32[]{:S(2)}) collective-permute-start(f32[2,64,512]{2,1,0:T(8,128)S(1)} %get-tuple-element.46.refs_3_), channel_id=1, source_target_pairs={{32,40},{40,48},{48,56},{96,104},{104,112},{112,120},{120,128},{12... | collective-permute-start | bytes 786440 | tf_op jit(solution)/shard_map/ppermute | solution.py:512
  41.0 0.7 collective-permute-start.12
  41.7 0.7 collective-permute-start.11
  42.4 0.7 collective-permute-start.10
  43.0 0.0 collective-permute-done.11.refs_6_
  43.0 0.0 collective-permute-done.10.refs_5_
  43.1 0.1 chain1.1
  43.1 0.7 collective-permute-start.15
  43.8 0.7 collective-permute-start.14
  44.5 0.7 collective-permute-start.13
  45.2 0.0 collective-permute-done.14.refs_8_
  45.2 4.7 %collective-permute-done.9.refs_4_.refs_3_.handed_ref = f32[2,64,512]{2,1,0:T(8,128)S(1)} collective-permute-done((f32[2,64,512]{2,1,0:T(8,128)S(1)}, f32[2,64,512]{2,1,0:T(8,128)S(1)}, u32[]{:S(2)}, u32[]{:S(2)}) %collective-permute-start.9) | collective-permute-done | bytes 262176 | tf_op jit(solution)/shard_map/ppermute | solution.py:512
  49.9 0.1 chain2.1
  50.0 0.7 collective-permute-start.16
  50.7 1.3 %collective-permute-start.19 = (f32[2,4,16,128]{3,2,1,0:T(8,128)S(1)}, f32[2,4,16,128]{3,2,1,0:T(8,128)S(1)}, u32[]{:S(2)}, u32[]{:S(2)}) collective-permute-start(f32[2,4,16,128]{3,2,1,0:T(8,128)S(1)} %get-tuple-element.54), channel_id=1, source_target_pairs={{128,223},{136,208},{144,200},{152,193},{129,216},{137,209},{145,2... | collective-permute-start | bytes 196616 | tf_op jit(solution)/shard_map/ppermute | solution.py:523
  52.0 1.3 %collective-permute-start.18 = (f32[2,4,16,128]{3,2,1,0:T(8,128)S(1)}, f32[2,4,16,128]{3,2,1,0:T(8,128)S(1)}, u32[]{:S(2)}, u32[]{:S(2)}) collective-permute-start(f32[2,4,16,128]{3,2,1,0:T(8,128)S(1)} %get-tuple-element.54), channel_id=1, source_target_pairs={{128,200},{136,192},{144,216},{152,208},{129,201},{137,193},{145,2... | collective-permute-start | bytes 196616 | tf_op jit(solution)/shard_map/ppermute | solution.py:523
  53.3 1.3 %collective-permute-start.17 = (f32[2,4,16,128]{3,2,1,0:T(8,128)S(1)}, f32[2,4,16,128]{3,2,1,0:T(8,128)S(1)}, u32[]{:S(2)}, u32[]{:S(2)}) collective-permute-start(f32[2,4,16,128]{3,2,1,0:T(8,128)S(1)} %get-tuple-element.54), channel_id=1, source_target_pairs={{128,192},{136,200},{144,208},{152,216},{129,193},{137,201},{145,2... | collective-permute-start | bytes 196616 | tf_op jit(solution)/shard_map/ppermute | solution.py:523
  54.6 15.9 %collective-permute-done.19.refs_9_ = f32[2,4,16,128]{3,2,1,0:T(8,128)S(1)} collective-permute-done((f32[2,4,16,128]{3,2,1,0:T(8,128)S(1)}, f32[2,4,16,128]{3,2,1,0:T(8,128)S(1)}, u32[]{:S(2)}, u32[]{:S(2)}) %collective-permute-start.19) | collective-permute-done | bytes 65568 | tf_op jit(solution)/shard_map/ppermute | solution.py:523
  70.4 1.1 %collective-permute-done.17.refs_7_ = f32[2,4,16,128]{3,2,1,0:T(8,128)S(1)} collective-permute-done((f32[2,4,16,128]{3,2,1,0:T(8,128)S(1)}, f32[2,4,16,128]{3,2,1,0:T(8,128)S(1)}, u32[]{:S(2)}, u32[]{:S(2)}) %collective-permute-start.17) | collective-permute-done | bytes 65568 | tf_op jit(solution)/shard_map/ppermute | solution.py:523
  71.5 2.0 %chain3.1 = (f32[8,128]{1,0:T(8,128)}, f32[8,2,4,16,128]{4,3,2,1,0:T(8,128)S(1)}) custom-call(s32[1]{0:T(128)} %bitcast.where_ref.refs_0_, f32[4,7,8,512]{3,2,1,0:T(8,128)S(1)} %get-tuple-element.35.refs_1_, f32[4,5,8,512]{3,2,1,0:T(8,128)S(1)} %get-tuple-element.36.refs_2_, ...), custom_call_target="tpu_custom_call", output_to_operand_aliasing={{1}: (10, {})} | custom-call | tf_op jit(solution)/shard_map/chain3/pallas_call | solution.py:492
  73.5 11.7 %all_to_all.5.got_ref = f32[8,2,4,16,128]{4,3,2,1,0:T(8,128)S(1)} all-to-all(f32[8,2,4,16,128]{4,3,2,1,0:T(8,128)S(1)} %get-tuple-element.56), channel_id=1, replica_groups={{0,8,16,24,32,40,48,56},{64,72,80,88,96,104,112,120},{128,136,144,152,1..., dimensions={0} | all-to-all | bytes 1048576 | tf_op jit(solution)/shard_map/all_to_all | solution.py:525
  85.2 0.6 collective-permute-start.21
  85.9 0.9 ready.1
  86.8 1.0 %collective-permute-done.21.hi_ref = f32[2,4,16,128]{3,2,1,0:T(8,128)S(1)} collective-permute-done((f32[2,4,16,128]{3,2,1,0:T(8,128)S(1)}, f32[2,4,16,128]{3,2,1,0:T(8,128)S(1)}, u32[]{:S(2)}, u32[]{:S(2)}) %collective-permute-start.21) | collective-permute-done | bytes 65568 | tf_op jit(solution)/shard_map/ppermute | solution.py:527
  87.8 3.0 %collective-permute-done.20.lo_ref = f32[2,4,16,128]{3,2,1,0:T(8,128)S(1)} collective-permute-done((f32[2,4,16,128]{3,2,1,0:T(8,128)S(1)}, f32[2,4,16,128]{3,2,1,0:T(8,128)S(1)}, u32[]{:S(2)}, u32[]{:S(2)}) %collective-permute-start.20) | collective-permute-done | bytes 65568 | tf_op jit(solution)/shard_map/ppermute | solution.py:526
  90.8 5.7 %final.1 = f32[1,2,64,512]{3,2,1,0:T(8,128)} custom-call(s32[1]{0:T(128)} %bitcast.where_ref.refs_0_, f32[2,4,64,128]{3,2,1,0:T(8,128)S(1)} %get-tuple-element.58.own_ref, f32[2,4,16,128]{3,2,1,0:T(8,128)S(1)} %collective-permute-done.20.lo_ref, f32[2,4,16,128]{3,2,1,0:T(8,128)S(1)} %collective-permute-done.21.hi_ref, ...), custom_call_target="tpu_custom_call" | custom-call | tf_op jit(solution)/shard_map/final/pallas_call | solution.py:540
  (12 shorter events, 0.0 us)
Async XLA Ops:
  0.6 4.8 %copy-start.1 = (f32[64,512]{1,0:T(8,128)S(1)}, f32[64,512]{1,0:T(8,128)}, u32[]{:S(2)}) copy-start(f32[64,512]{1,0:T(8,128)} %n_ref.5) | copy-start | bytes 393220
  0.6 4.8 %copy-start = (f32[1,2,64,512]{3,2,1,0:T(8,128)S(1)}, f32[1,2,64,512]{3,2,1,0:T(8,128)}, u32[]{:S(2)}) copy-start(f32[1,2,64,512]{3,2,1,0:T(8,128)} %c_ref.5) | copy-start | bytes 786436
  2.4 6.5 %collective-permute-start = (f32[3,32,512]{2,1,0:T(8,128)}, f32[3,32,512]{2,1,0:T(8,128)S(1)}, u32[]{:S(2)}, u32[]{:S(2)}) collective-permute-start(f32[3,32,512]{2,1,0:T(8,128)} %get-tuple-element.32), channel_id=1, source_target_pairs={{0,1},{1,2},{2,3},{3,4},{4,5},{5,6},{6,7},{7,0},{8,9},{9,10},{10,1... | collective-permute-start | bytes 589832 | tf_op jit(solution)/shard_map/ppermute | solution.py:433
  2.5 6.5 %collective-permute-start.1 = (f32[3,32,512]{2,1,0:T(8,128)}, f32[3,32,512]{2,1,0:T(8,128)S(1)}, u32[]{:S(2)}, u32[]{:S(2)}) collective-permute-start(f32[3,32,512]{2,1,0:T(8,128)} %get-tuple-element.33), channel_id=1, source_target_pairs={{1,0},{2,1},{3,2},{4,3},{5,4},{6,5},{7,6},{0,7},{9,8},{10,9},{11,1... | collective-permute-start | bytes 589832 | tf_op jit(solution)/shard_map/ppermute | solution.py:434
  15.9 7.9 %collective-permute-start.5 = (f32[2,4,32,128]{3,2,1,0:T(8,128)S(1)}, f32[2,4,32,128]{3,2,1,0:T(8,128)S(1)}, u32[]{:S(2)}, u32[]{:S(2)}) collective-permute-start(f32[2,4,32,128]{3,2,1,0:T(8,128)S(1)} %get-tuple-element.42), channel_id=1, source_target_pairs={{32,0},{0,32},{40,8},{8,40},{48,16},{16,48},{56,24},{24,56},{96,64... | collective-permute-start | bytes 393224 | tf_op jit(solution)/shard_map/ppermute | solution.py:474
  17.0 10.1 %collective-permute-start.6 = (f32[2,4,32,128]{3,2,1,0:T(8,128)S(1)}, f32[2,4,32,128]{3,2,1,0:T(8,128)S(1)}, u32[]{:S(2)}, u32[]{:S(2)}) collective-permute-start(f32[2,4,32,128]{3,2,1,0:T(8,128)S(1)} %get-tuple-element.43), channel_id=1, source_target_pairs={{32,8},{8,32},{40,16},{16,40},{48,24},{24,48},{56,0},{0,56},{96,72... | collective-permute-start | bytes 393224 | tf_op jit(solution)/shard_map/ppermute | solution.py:474
  20.5 17.4 %collective-permute-start.2 = (f32[2,4,48,128]{3,2,1,0:T(8,128)S(1)}, f32[2,4,48,128]{3,2,1,0:T(8,128)S(1)}, u32[]{:S(2)}, u32[]{:S(2)}) collective-permute-start(f32[2,4,48,128]{3,2,1,0:T(8,128)S(1)} %get-tuple-element.39), channel_id=1, source_target_pairs={{0,8},{8,16},{16,24},{24,0},{32,40},{40,48},{48,56},{56,32},{64,72... | collective-permute-start | bytes 589832 | tf_op jit(solution)/shard_map/ppermute | solution.py:467
  20.5 17.4 %collective-permute-start.3 = (f32[2,4,48,128]{3,2,1,0:T(8,128)S(1)}, f32[2,4,48,128]{3,2,1,0:T(8,128)S(1)}, u32[]{:S(2)}, u32[]{:S(2)}) collective-permute-start(f32[2,4,48,128]{3,2,1,0:T(8,128)S(1)} %get-tuple-element.40), channel_id=1, source_target_pairs={{0,16},{8,24},{16,0},{24,8},{32,48},{40,56},{48,32},{56,40},{64,80... | collective-permute-start | bytes 589832 | tf_op jit(solution)/shard_map/ppermute | solution.py:467
  22.7 16.1 %collective-permute-start.4 = (f32[2,4,48,128]{3,2,1,0:T(8,128)S(1)}, f32[2,4,48,128]{3,2,1,0:T(8,128)S(1)}, u32[]{:S(2)}, u32[]{:S(2)}) collective-permute-start(f32[2,4,48,128]{3,2,1,0:T(8,128)S(1)} %get-tuple-element.41), channel_id=1, source_target_pairs={{0,24},{8,0},{16,8},{24,16},{32,56},{40,32},{48,40},{56,48},{64,88... | collective-permute-start | bytes 589832 | tf_op jit(solution)/shard_map/ppermute | solution.py:467
  23.7 8.5 %collective-permute-start.7 = (f32[2,4,32,128]{3,2,1,0:T(8,128)S(1)}, f32[2,4,32,128]{3,2,1,0:T(8,128)S(1)}, u32[]{:S(2)}, u32[]{:S(2)}) collective-permute-start(f32[2,4,32,128]{3,2,1,0:T(8,128)S(1)} %get-tuple-element.44), channel_id=1, source_target_pairs={{32,16},{16,32},{40,24},{24,40},{48,0},{0,48},{56,8},{8,56},{96,80... | collective-permute-start | bytes 393224 | tf_op jit(solution)/shard_map/ppermute | solution.py:474
  27.1 5.9 %collective-permute-start.8 = (f32[2,4,32,128]{3,2,1,0:T(8,128)S(1)}, f32[2,4,32,128]{3,2,1,0:T(8,128)S(1)}, u32[]{:S(2)}, u32[]{:S(2)}) collective-permute-start(f32[2,4,32,128]{3,2,1,0:T(8,128)S(1)} %get-tuple-element.45), channel_id=1, source_target_pairs={{32,24},{24,32},{40,0},{0,40},{48,8},{8,48},{56,16},{16,56},{96,88... | collective-permute-start | bytes 393224 | tf_op jit(solution)/shard_map/ppermute | solution.py:474
  38.8 11.0 %collective-permute-start.9 = (f32[2,64,512]{2,1,0:T(8,128)S(1)}, f32[2,64,512]{2,1,0:T(8,128)S(1)}, u32[]{:S(2)}, u32[]{:S(2)}) collective-permute-start(f32[2,64,512]{2,1,0:T(8,128)S(1)} %get-tuple-element.46.refs_3_), channel_id=1, source_target_pairs={{32,40},{40,48},{48,56},{96,104},{104,112},{112,120},{120,128},{12... | collective-permute-start | bytes 786440 | tf_op jit(solution)/shard_map/ppermute | solution.py:512
  41.0 2.0 %collective-permute-start.12 = (f32[2,4,16,128]{3,2,1,0:T(8,128)S(1)}, f32[2,4,16,128]{3,2,1,0:T(8,128)S(1)}, u32[]{:S(2)}, u32[]{:S(2)}) collective-permute-start(f32[2,4,16,128]{3,2,1,0:T(8,128)S(1)} %get-tuple-element.49), channel_id=1, source_target_pairs={{0,95},{8,80},{16,72},{24,65},{1,88},{9,81},{17,73},{25,66},{2,89}... | collective-permute-start | bytes 196616 | tf_op jit(solution)/shard_map/ppermute | solution.py:523
  41.7 1.4 %collective-permute-start.11 = (f32[2,4,16,128]{3,2,1,0:T(8,128)S(1)}, f32[2,4,16,128]{3,2,1,0:T(8,128)S(1)}, u32[]{:S(2)}, u32[]{:S(2)}) collective-permute-start(f32[2,4,16,128]{3,2,1,0:T(8,128)S(1)} %get-tuple-element.49), channel_id=1, source_target_pairs={{0,72},{8,64},{16,88},{24,80},{1,73},{9,65},{17,89},{25,81},{2,74}... | collective-permute-start | bytes 196616 | tf_op jit(solution)/shard_map/ppermute | solution.py:523
  42.4 0.7 collective-permute-start.10
  43.1 2.0 %collective-permute-start.15 = (f32[2,4,16,128]{3,2,1,0:T(8,128)S(1)}, f32[2,4,16,128]{3,2,1,0:T(8,128)S(1)}, u32[]{:S(2)}, u32[]{:S(2)}) collective-permute-start(f32[2,4,16,128]{3,2,1,0:T(8,128)S(1)} %get-tuple-element.51), channel_id=1, source_target_pairs={{64,159},{72,144},{80,136},{88,129},{65,152},{73,145},{81,137},{89... | collective-permute-start | bytes 196616 | tf_op jit(solution)/shard_map/ppermute | solution.py:523
  43.8 1.4 %collective-permute-start.14 = (f32[2,4,16,128]{3,2,1,0:T(8,128)S(1)}, f32[2,4,16,128]{3,2,1,0:T(8,128)S(1)}, u32[]{:S(2)}, u32[]{:S(2)}) collective-permute-start(f32[2,4,16,128]{3,2,1,0:T(8,128)S(1)} %get-tuple-element.51), channel_id=1, source_target_pairs={{64,136},{72,128},{80,152},{88,144},{65,137},{73,129},{81,153},{89... | collective-permute-start | bytes 196616 | tf_op jit(solution)/shard_map/ppermute | solution.py:523
  44.5 0.7 collective-permute-start.13
  50.0 21.5 %collective-permute-start.16 = (f32[2,64,512]{2,1,0:T(8,128)S(1)}, f32[2,64,512]{2,1,0:T(8,128)S(1)}, u32[]{:S(2)}, u32[]{:S(2)}) collective-permute-start(f32[2,64,512]{2,1,0:T(8,128)S(1)} %get-tuple-element.53), channel_id=1, source_target_pairs={{0,8},{8,16},{16,24},{24,32},{56,64},{64,72},{72,80},{80,88},{88,9... | collective-permute-start | bytes 786440 | tf_op jit(solution)/shard_map/ppermute | solution.py:512
  50.7 19.8 %collective-permute-start.19 = (f32[2,4,16,128]{3,2,1,0:T(8,128)S(1)}, f32[2,4,16,128]{3,2,1,0:T(8,128)S(1)}, u32[]{:S(2)}, u32[]{:S(2)}) collective-permute-start(f32[2,4,16,128]{3,2,1,0:T(8,128)S(1)} %get-tuple-element.54), channel_id=1, source_target_pairs={{128,223},{136,208},{144,200},{152,193},{129,216},{137,209},{145,2... | collective-permute-start | bytes 196616 | tf_op jit(solution)/shard_map/ppermute | solution.py:523
  52.0 18.5 %collective-permute-start.18 = (f32[2,4,16,128]{3,2,1,0:T(8,128)S(1)}, f32[2,4,16,128]{3,2,1,0:T(8,128)S(1)}, u32[]{:S(2)}, u32[]{:S(2)}) collective-permute-start(f32[2,4,16,128]{3,2,1,0:T(8,128)S(1)} %get-tuple-element.54), channel_id=1, source_target_pairs={{128,200},{136,192},{144,216},{152,208},{129,201},{137,193},{145,2... | collective-permute-start | bytes 196616 | tf_op jit(solution)/shard_map/ppermute | solution.py:523
  53.3 18.2 %collective-permute-start.17 = (f32[2,4,16,128]{3,2,1,0:T(8,128)S(1)}, f32[2,4,16,128]{3,2,1,0:T(8,128)S(1)}, u32[]{:S(2)}, u32[]{:S(2)}) collective-permute-start(f32[2,4,16,128]{3,2,1,0:T(8,128)S(1)} %get-tuple-element.54), channel_id=1, source_target_pairs={{128,192},{136,200},{144,208},{152,216},{129,193},{137,201},{145,2... | collective-permute-start | bytes 196616 | tf_op jit(solution)/shard_map/ppermute | solution.py:523
  85.2 2.5 %collective-permute-start.21 = (f32[2,4,16,128]{3,2,1,0:T(8,128)S(1)}, f32[2,4,16,128]{3,2,1,0:T(8,128)S(1)}, u32[]{:S(2)}, u32[]{:S(2)}) collective-permute-start(f32[2,4,16,128]{3,2,1,0:T(8,128)S(1)} %get-tuple-element.61), channel_id=1, source_target_pairs={{1,0},{2,1},{3,2},{4,3},{5,4},{6,5},{7,6},{0,7},{9,8},{10,9},{11,1... | collective-permute-start | bytes 196616 | tf_op jit(solution)/shard_map/ppermute | solution.py:527
  85.9 4.9 %collective-permute-start.20 = (f32[2,4,16,128]{3,2,1,0:T(8,128)S(1)}, f32[2,4,16,128]{3,2,1,0:T(8,128)S(1)}, u32[]{:S(2)}, u32[]{:S(2)}) collective-permute-start(f32[2,4,16,128]{3,2,1,0:T(8,128)S(1)} %get-tuple-element.62), channel_id=1, source_target_pairs={{0,1},{1,2},{2,3},{3,4},{4,5},{5,6},{6,7},{7,0},{8,9},{9,10},{10,1... | collective-permute-start | bytes 196616 | tf_op jit(solution)/shard_map/ppermute | solution.py:526

commit v5 on v4

--- a/solution.py
+++ b/solution.py
@@ -157,7 +157,7 @@
 
 
 def forward_kernel(where_ref, own_ref, lo_ref, hi_ref,
-                   fwd_ref, nwin_ref, own_tau, near1, near2, near3, far0, far1, far2, far3,
+                   fwd_ref, nwin_ref, own_tau, far0, far1, far2, far3,
                    nat, fnat, w, mid, tau, cf, cc, sem):
     n = 16
     blocks = nat.shape[1]
@@ -204,9 +204,9 @@
         both = pl.ds(0, 2)
         pairs.append((fnat.at[both, b, pl.ds(EDGE, rows), :], fwd_ref.at[both, :, cut(b)]))
     started = copies(pairs, sem)
-    for k, ref in enumerate((own_tau, near1, near2, near3)):
-        first = lax.rem(position + k, SPLIT) * STRIP + (EDGE - HALO)
-        ref[...] = nat[0:2, :, pl.ds(pl.multiple_of(first, 8), WINDOW), :]
+    for k in range(SPLIT):
+        first = k * STRIP + (EDGE - HALO)
+        own_tau[k] = nat[0:2, :, first : first + WINDOW, :]
     for k, ref in enumerate((far0, far1, far2, far3)):
         first = lax.rem(position + k, SPLIT) * STRIP + (EDGE - INNER)
         ref[...] = nat[0:2, :, pl.ds(pl.multiple_of(first, 8), TIGHT), :]
@@ -233,11 +233,10 @@
     planes = GROUP // SPLIT
     rest = refs[3 + carried :]
     if stage == 0:
-        near_ref, far_ref = refs[-9:-7]
+        near_ref, far_ref = rest[0], refs[-8]
         for k in range(SPLIT):
             source = lax.rem(position + SPLIT - k, SPLIT)
-            near_ref[source] = rest[k][...]
-            far_ref[source] = rest[SPLIT + k][...]
+            far_ref[source] = rest[1 + k][...]
     else:
         near_ref, far_ref, own, pair, other, corr_in = rest[:6]
     active = position // SPLIT == stage * planes
@@ -434,13 +433,13 @@
     hi = lax.ppermute(top, "space", down)
 
     n = 16
-    window = shape(2, blocks, WINDOW, LANES)
+    window = shape(SPLIT, 2, blocks, WINDOW, LANES)
     inner = shape(2, blocks, TIGHT, LANES)
     forward, nwin, *sent = pl.pallas_call(
         forward_kernel,
-        out_shape=(shape(2, rows, cols), shape(blocks, WINDOW, LANES)) + (window,) * SPLIT + (inner,) * SPLIT,
+        out_shape=(shape(2, rows, cols), shape(blocks, WINDOW, LANES)) + (window,) + (inner,) * SPLIT,
         in_specs=[SMEM, VMEM, VMEM, VMEM],
-        out_specs=(HBM,) + (VMEM,) * (1 + 2 * SPLIT),
+        out_specs=(HBM,) + (VMEM,) * (2 + SPLIT),
         scratch_shapes=[
             vm(3, blocks, 128, LANES), vm(2, blocks, 128, LANES),
             vm(2, n, 8, cols), vm(2, n, 8, cols), vm(2, n, 8, cols),
@@ -462,16 +461,16 @@
 
     planes = range(0, intervals, SPLIT)
     gathered = [sent[0]]
-    for k in range(1, SPLIT):
-        pairs = [(p + q, p + (q + k) % SPLIT) for p in planes for q in range(SPLIT)]
-        gathered.append(lax.ppermute(sent[k], "tm", pairs))
+    four = [[p + q for q in range(SPLIT)] for p in planes]
+    near = lax.all_to_all(sent[0], "tm", 0, 0, axis_index_groups=four)
+    gathered = [near]
     for k in range(SPLIT):
         pairs = []
         for p in range(0, intervals, GROUP):
             for q in range(SPLIT):
                 a, b = p + SPLIT + q, p + (q + k) % SPLIT
                 pairs += [(a, b), (b, a)]
-        gathered.append(lax.ppermute(sent[SPLIT + k], "tm", pairs))
+        gathered.append(lax.ppermute(sent[1 + k], "tm", pairs))
     groups = [[g * GROUP + j for j in range(GROUP)] for g in range(stages)]
 
     strips = ring * SPLIT
@@ -483,7 +482,7 @@
         specs = [SMEM, VMEM, VMEM] + [HBM] * len(extra) + [VMEM] * (len(operands) - 3 - len(extra))
         shapes = [shape(2, rows, cols) if carries else shape(8, LANES)]
         if stage == 0:
-            shapes += [shape(SPLIT, 2, blocks, WINDOW, LANES), shape(SPLIT, 2, blocks, TIGHT, LANES)]
+            shapes += [shape(SPLIT, 2, blocks, TIGHT, LANES)]
         shapes += [shape(GROUP, 2, blocks, STRIP, LANES)]
         shapes += [shape(2, blocks, STRIP, LANES)] if stage + 1 < stages else []
         aliases = {len(operands) - 1: 1} if stage > 0 else {}
@@ -503,7 +502,7 @@
             name="chain%d" % stage,
         )(*operands)
         if stage == 0:
-            taus = done[1:3]
+            taus = [near, done[1]]
         corr, last = done[-2:] if stage + 1 < stages else (done[-1], None)
         if carries:
             forward = done[0]

time: 96.8 us -> 95.6 us (0.988)
  waiting for transfers between devices: 40.9 us -> 37.4 us
  starting transfers between devices: 25.1 us -> 26.3 us
    all_to_all x0 -> x1, starting transfers between devices: none -> 4.5 us  [shards(): near = lax.all_to_all(sent[0], 'tm', 0, 0, axis_index_groups=four)]
    ppermute x7 -> x4, waiting for transfers between devices: 11.8 us -> 7.89 us  [shards(): gathered.append(lax.ppermute(sent[1 + k], 'tm', pairs))]
    ppermute x7 -> x4, starting transfers between devices: 10.8 us -> 7.31 us  [shards(): gathered.append(lax.ppermute(sent[1 + k], 'tm', pairs))]
    all_to_all x0 -> x1, waiting for transfers between devices: none -> 3.03 us  [shards(): near = lax.all_to_all(sent[0], 'tm', 0, 0, axis_index_groups=four)]
    ppermute x9, waiting for transfers between devices: 16.9 us -> 14.4 us  [shards(): pieces.append(lax.ppermute(last, ('tm', 'space'), pairs))]
    pallas_call x1, Pallas kernels: 6.9 us -> 7.91 us  [shards(): pl.pallas_call(forward_kernel, out_shape=(shape(2, rows, cols), shape(blo...]
  transfers between devices with their start and end apart: 22 -> 20, of which waited for: 11 -> 10; matrix products, arithmetic and copies ran while one was open for 0% -> 0% of each run, Pallas kernels for 1% -> 1%
where the time goes in v5:
time: 95.6 us; the launch traced here: 95.2 us
  waiting for transfers between devices  37.4 us (39%)
  starting transfers between devices  26.3 us (28%)
  Pallas kernels  18.8 us (20%)
  blocking collectives  11.9 us (12%)
    ppermute x9, waiting for transfers between devices, shards(): pieces.append(lax.ppermute(last, ('tm', 'space'), pairs))  14.4 us
    all_to_all x1, blocking collectives, shards(): got = lax.all_to_all(corr, 'tm', 0, 0, axis_index_groups=groups)  11.9 us
    pallas_call x1, Pallas kernels, shards(): pl.pallas_call(forward_kernel, out_shape=(shape(2, rows, cols), shape(blo...  7.91 us
    ppermute x4, waiting for transfers between devices, shards(): gathered.append(lax.ppermute(sent[1 + k], 'tm', pairs))  7.89 us
    ppermute x9, starting transfers between devices, shards(): pieces.append(lax.ppermute(last, ('tm', 'space'), pairs))  7.86 us
    ppermute x4, starting transfers between devices, shards(): gathered.append(lax.ppermute(sent[1 + k], 'tm', pairs))  7.31 us
    pallas_call x1, Pallas kernels, shards(): pl.pallas_call(final_kernel, out_shape=shape(1, 2, rows, cols), in_specs=...  5.69 us
    ppermute x2, waiting for transfers between devices, shards(): handed = handed + [lax.ppermute(forward, 'tm', pairs)]  4.79 us
  transfers between devices with their start and end apart: 20, of which 10 were waited for; matrix products, arithmetic and copies ran while one was open for 0% of the time, Pallas kernels for 1%

profile of v5, /device:TPU:192, one launch (start us, length us, event | category | flops | bytes accessed | tf_op | source)
XLA Modules:
  0.0 95.2 jit_solution(12794037601219051668)
XLA Ops:
  0.6 1.8 %edges.1 = (f32[3,32,512]{2,1,0:T(8,128)}, f32[3,32,512]{2,1,0:T(8,128)}) custom-call(f32[1,2,64,512]{3,2,1,0:T(8,128)} %c_ref.5, f32[64,512]{1,0:T(8,128)} %n_ref.5), custom_call_target="tpu_custom_call" | custom-call | tf_op jit(solution)/shard_map/edges/pallas_call | solution.py:413
  2.4 0.0 collective-permute-start
  2.5 2.9 %collective-permute-start.1 = (f32[3,32,512]{2,1,0:T(8,128)}, f32[3,32,512]{2,1,0:T(8,128)S(1)}, u32[]{:S(2)}, u32[]{:S(2)}) collective-permute-start(f32[3,32,512]{2,1,0:T(8,128)} %get-tuple-element.29), channel_id=1, source_target_pairs={{1,0},{2,1},{3,2},{4,3},{5,4},{6,5},{7,6},{0,7},{9,8},{10,9},{11,1... | collective-permute-start | bytes 589832 | tf_op jit(solution)/shard_map/ppermute | solution.py:433
  5.4 0.2 load.1.own_ref
  5.6 3.3 %collective-permute-done.lo_ref.clo_ref = f32[3,32,512]{2,1,0:T(8,128)S(1)} collective-permute-done((f32[3,32,512]{2,1,0:T(8,128)}, f32[3,32,512]{2,1,0:T(8,128)S(1)}, u32[]{:S(2)}, u32[]{:S(2)}) %collective-permute-start) | collective-permute-done | bytes 196640 | tf_op jit(solution)/shard_map/ppermute | solution.py:432
  9.0 0.0 collective-permute-done.1.hi_ref.chi_ref
  9.0 7.9 %forward.1 = (f32[2,64,512]{2,1,0:T(8,128)S(1)}, f32[4,48,128]{2,1,0:T(8,128)S(1)}, f32[4,2,4,48,128]{4,3,2,1,0:T(8,128)}, f32[2,4,32,128]{3,2,1,0:T(8,128)}, f3...) custom-call(s32[1]{0:T(128)} %bitcast.where_ref.refs_0_, ...), custom_call_target="tpu_custom_call" | custom-call | tf_op jit(solution)/shard_map/forward/pallas_call | solution.py:438
  16.9 4.5 %all-to-all-start = ((f32[4,2,4,48,128]{4,3,2,1,0:T(8,128)}), f32[4,2,4,48,128]{4,3,2,1,0:T(8,128)S(1)}, u32[]{:S(2)}, u32[]{:S(2)}) async-start(f32[4,2,4,48,128]{4,3,2,1,0:T(8,128)} %get-tuple-element.34), calls=%async_computation | async-start | bytes 1572864 | tf_op jit(solution)/shard_map/all_to_all | solution.py:465
  21.4 1.0 %collective-permute-start.2 = (f32[2,4,32,128]{3,2,1,0:T(8,128)}, f32[2,4,32,128]{3,2,1,0:T(8,128)S(1)}, u32[]{:S(2)}, u32[]{:S(2)}) collective-permute-start(f32[2,4,32,128]{3,2,1,0:T(8,128)} %get-tuple-element.35), channel_id=1, source_target_pairs={{32,0},{0,32},{40,8},{8,40},{48,16},{16,48},{56,24},{24,56},{96,64... | collective-permute-start | bytes 393224 | tf_op jit(solution)/shard_map/ppermute | solution.py:473
  22.4 3.7 %collective-permute-start.3 = (f32[2,4,32,128]{3,2,1,0:T(8,128)}, f32[2,4,32,128]{3,2,1,0:T(8,128)S(1)}, u32[]{:S(2)}, u32[]{:S(2)}) collective-permute-start(f32[2,4,32,128]{3,2,1,0:T(8,128)} %get-tuple-element.36), channel_id=1, source_target_pairs={{32,8},{8,32},{40,16},{16,40},{48,24},{24,48},{56,0},{0,56},{96,72... | collective-permute-start | bytes 393224 | tf_op jit(solution)/shard_map/ppermute | solution.py:473
  26.1 1.9 %collective-permute-start.4 = (f32[2,4,32,128]{3,2,1,0:T(8,128)}, f32[2,4,32,128]{3,2,1,0:T(8,128)S(1)}, u32[]{:S(2)}, u32[]{:S(2)}) collective-permute-start(f32[2,4,32,128]{3,2,1,0:T(8,128)} %get-tuple-element.37), channel_id=1, source_target_pairs={{32,16},{16,32},{40,24},{24,40},{48,0},{0,48},{56,8},{8,56},{96,80... | collective-permute-start | bytes 393224 | tf_op jit(solution)/shard_map/ppermute | solution.py:473
  28.0 0.7 collective-permute-start.5
  28.7 0.2 prep.1
  28.9 0.0 collective-permute-done.2.refs_5_
  28.9 4.6 %collective-permute-done.3.refs_6_ = f32[2,4,32,128]{3,2,1,0:T(8,128)S(1)} collective-permute-done((f32[2,4,32,128]{3,2,1,0:T(8,128)}, f32[2,4,32,128]{3,2,1,0:T(8,128)S(1)}, u32[]{:S(2)}, u32[]{:S(2)}) %collective-permute-start.3) | collective-permute-done | bytes 131104 | tf_op jit(solution)/shard_map/ppermute | solution.py:473
  33.6 3.1 %collective-permute-done.4.refs_7_ = f32[2,4,32,128]{3,2,1,0:T(8,128)S(1)} collective-permute-done((f32[2,4,32,128]{3,2,1,0:T(8,128)}, f32[2,4,32,128]{3,2,1,0:T(8,128)S(1)}, u32[]{:S(2)}, u32[]{:S(2)}) %collective-permute-start.4) | collective-permute-done | bytes 131104 | tf_op jit(solution)/shard_map/ppermute | solution.py:473
  36.6 0.2 collective-permute-done.5.refs_8_
  36.8 3.0 %all-to-all-done.refs_4_.refs_3_.refs_5_ = f32[4,2,4,48,128]{4,3,2,1,0:T(8,128)S(1)} async-done(((f32[4,2,4,48,128]{4,3,2,1,0:T(8,128)}), f32[4,2,4,48,128]{4,3,2,1,0:T(8,128)S(1)}, u32[]{:S(2)}, u32[]{:S(2)}) %all-to-all-start) | async-done | bytes 786464 | tf_op jit(solution)/shard_map/all_to_all | solution.py:465
  39.9 2.5 %collective-permute-start.6 = (f32[2,64,512]{2,1,0:T(8,128)S(1)}, f32[2,64,512]{2,1,0:T(8,128)S(1)}, u32[]{:S(2)}, u32[]{:S(2)}) collective-permute-start(f32[2,64,512]{2,1,0:T(8,128)S(1)} %get-tuple-element.39.refs_3_), channel_id=1, source_target_pairs={{32,40},{40,48},{48,56},{96,104},{104,112},{112,120},{120,128},{12... | collective-permute-start | bytes 786440 | tf_op jit(solution)/shard_map/ppermute | solution.py:511
  42.4 0.7 collective-permute-start.9
  43.0 0.7 collective-permute-start.8
  43.7 0.7 collective-permute-start.7
  44.4 0.0 collective-permute-done.9.refs_7_
  44.4 0.0 collective-permute-done.8.refs_6_
  44.4 0.0 collective-permute-done.7.refs_5_
  44.4 0.1 chain1.1
  44.5 0.7 collective-permute-start.12
  45.2 0.7 collective-permute-start.11
  45.8 0.7 collective-permute-start.10
  46.5 0.0 collective-permute-done.12.refs_9_
  46.5 0.0 collective-permute-done.10.refs_7_
  46.6 4.8 %collective-permute-done.6.refs_4_.refs_3_.handed_ref = f32[2,64,512]{2,1,0:T(8,128)S(1)} collective-permute-done((f32[2,64,512]{2,1,0:T(8,128)S(1)}, f32[2,64,512]{2,1,0:T(8,128)S(1)}, u32[]{:S(2)}, u32[]{:S(2)}) %collective-permute-start.6) | collective-permute-done | bytes 262176 | tf_op jit(solution)/shard_map/ppermute | solution.py:511
  51.3 0.1 chain2.1
  51.4 0.7 collective-permute-start.13
  52.1 1.3 %collective-permute-start.16 = (f32[2,4,16,128]{3,2,1,0:T(8,128)S(1)}, f32[2,4,16,128]{3,2,1,0:T(8,128)S(1)}, u32[]{:S(2)}, u32[]{:S(2)}) collective-permute-start(f32[2,4,16,128]{3,2,1,0:T(8,128)S(1)} %get-tuple-element.46), channel_id=1, source_target_pairs={{128,223},{136,208},{144,200},{152,193},{129,216},{137,209},{145,2... | collective-permute-start | bytes 196616 | tf_op jit(solution)/shard_map/ppermute | solution.py:522
  53.4 1.3 %collective-permute-start.15 = (f32[2,4,16,128]{3,2,1,0:T(8,128)S(1)}, f32[2,4,16,128]{3,2,1,0:T(8,128)S(1)}, u32[]{:S(2)}, u32[]{:S(2)}) collective-permute-start(f32[2,4,16,128]{3,2,1,0:T(8,128)S(1)} %get-tuple-element.46), channel_id=1, source_target_pairs={{128,200},{136,192},{144,216},{152,208},{129,201},{137,193},{145,2... | collective-permute-start | bytes 196616 | tf_op jit(solution)/shard_map/ppermute | solution.py:522
  54.7 1.3 %collective-permute-start.14 = (f32[2,4,16,128]{3,2,1,0:T(8,128)S(1)}, f32[2,4,16,128]{3,2,1,0:T(8,128)S(1)}, u32[]{:S(2)}, u32[]{:S(2)}) collective-permute-start(f32[2,4,16,128]{3,2,1,0:T(8,128)S(1)} %get-tuple-element.46), channel_id=1, source_target_pairs={{128,192},{136,200},{144,208},{152,216},{129,193},{137,201},{145,2... | collective-permute-start | bytes 196616 | tf_op jit(solution)/shard_map/ppermute | solution.py:522
  56.0 13.5 %collective-permute-done.16.refs_9_ = f32[2,4,16,128]{3,2,1,0:T(8,128)S(1)} collective-permute-done((f32[2,4,16,128]{3,2,1,0:T(8,128)S(1)}, f32[2,4,16,128]{3,2,1,0:T(8,128)S(1)}, u32[]{:S(2)}, u32[]{:S(2)}) %collective-permute-start.16) | collective-permute-done | bytes 65568 | tf_op jit(solution)/shard_map/ppermute | solution.py:522
  69.5 0.9 collective-permute-done.14.refs_7_
  70.4 0.0 collective-permute-done.13.refs_4_.handed2_ref
  70.4 1.9 %chain3.1 = (f32[8,128]{1,0:T(8,128)}, f32[8,2,4,16,128]{4,3,2,1,0:T(8,128)S(1)}) custom-call(s32[1]{0:T(128)} %bitcast.where_ref.refs_0_, f32[4,7,8,512]{3,2,1,0:T(8,128)S(1)} %get-tuple-element.31.refs_1_, f32[4,5,8,512]{3,2,1,0:T(8,128)S(1)} %get-tuple-element.32.refs_2_, ...), custom_call_target="tpu_custom_call", output_to_operand_aliasing={{1}: (10, {})} | custom-call | tf_op jit(solution)/shard_map/chain3/pallas_call | solution.py:491
  72.3 11.9 %all_to_all.10.got_ref = f32[8,2,4,16,128]{4,3,2,1,0:T(8,128)S(1)} all-to-all(f32[8,2,4,16,128]{4,3,2,1,0:T(8,128)S(1)} %get-tuple-element.48), channel_id=1, replica_groups={{0,8,16,24,32,40,48,56},{64,72,80,88,96,104,112,120},{128,136,144,152,1..., dimensions={0} | all-to-all | bytes 1048576 | tf_op jit(solution)/shard_map/all_to_all | solution.py:524
  84.3 0.4 collective-permute-start.18
  84.6 0.1 collective-permute-start.17
  84.8 0.9 ready.1
  85.7 0.9 collective-permute-done.18.hi_ref
  86.5 3.0 %collective-permute-done.17.lo_ref = f32[2,4,16,128]{3,2,1,0:T(8,128)S(1)} collective-permute-done((f32[2,4,16,128]{3,2,1,0:T(8,128)S(1)}, f32[2,4,16,128]{3,2,1,0:T(8,128)S(1)}, u32[]{:S(2)}, u32[]{:S(2)}) %collective-permute-start.17) | collective-permute-done | bytes 65568 | tf_op jit(solution)/shard_map/ppermute | solution.py:525
  89.5 5.7 %final.1 = f32[1,2,64,512]{3,2,1,0:T(8,128)} custom-call(s32[1]{0:T(128)} %bitcast.where_ref.refs_0_, f32[2,4,64,128]{3,2,1,0:T(8,128)S(1)} %get-tuple-element.50.own_ref, f32[2,4,16,128]{3,2,1,0:T(8,128)S(1)} %collective-permute-done.17.lo_ref, f32[2,4,16,128]{3,2,1,0:T(8,128)S(1)} %collective-permute-done.18.hi_ref, ...), custom_call_target="tpu_custom_call" | custom-call | tf_op jit(solution)/shard_map/final/pallas_call | solution.py:539
  (8 shorter events, 0.1 us)
Async XLA Ops:
  0.6 4.8 %copy-start.1 = (f32[64,512]{1,0:T(8,128)S(1)}, f32[64,512]{1,0:T(8,128)}, u32[]{:S(2)}) copy-start(f32[64,512]{1,0:T(8,128)} %n_ref.5) | copy-start | bytes 393220
  0.6 4.8 %copy-start = (f32[1,2,64,512]{3,2,1,0:T(8,128)S(1)}, f32[1,2,64,512]{3,2,1,0:T(8,128)}, u32[]{:S(2)}) copy-start(f32[1,2,64,512]{3,2,1,0:T(8,128)} %c_ref.5) | copy-start | bytes 786436
  2.4 6.5 %collective-permute-start = (f32[3,32,512]{2,1,0:T(8,128)}, f32[3,32,512]{2,1,0:T(8,128)S(1)}, u32[]{:S(2)}, u32[]{:S(2)}) collective-permute-start(f32[3,32,512]{2,1,0:T(8,128)} %get-tuple-element.28), channel_id=1, source_target_pairs={{0,1},{1,2},{2,3},{3,4},{4,5},{5,6},{6,7},{7,0},{8,9},{9,10},{10,1... | collective-permute-start | bytes 589832 | tf_op jit(solution)/shard_map/ppermute | solution.py:432
  2.5 6.5 %collective-permute-start.1 = (f32[3,32,512]{2,1,0:T(8,128)}, f32[3,32,512]{2,1,0:T(8,128)S(1)}, u32[]{:S(2)}, u32[]{:S(2)}) collective-permute-start(f32[3,32,512]{2,1,0:T(8,128)} %get-tuple-element.29), channel_id=1, source_target_pairs={{1,0},{2,1},{3,2},{4,3},{5,4},{6,5},{7,6},{0,7},{9,8},{10,9},{11,1... | collective-permute-start | bytes 589832 | tf_op jit(solution)/shard_map/ppermute | solution.py:433
  16.9 22.9 %all-to-all-start = ((f32[4,2,4,48,128]{4,3,2,1,0:T(8,128)}), f32[4,2,4,48,128]{4,3,2,1,0:T(8,128)S(1)}, u32[]{:S(2)}, u32[]{:S(2)}) async-start(f32[4,2,4,48,128]{4,3,2,1,0:T(8,128)} %get-tuple-element.34), calls=%async_computation | async-start | bytes 1572864 | tf_op jit(solution)/shard_map/all_to_all | solution.py:465
  21.4 7.5 %collective-permute-start.2 = (f32[2,4,32,128]{3,2,1,0:T(8,128)}, f32[2,4,32,128]{3,2,1,0:T(8,128)S(1)}, u32[]{:S(2)}, u32[]{:S(2)}) collective-permute-start(f32[2,4,32,128]{3,2,1,0:T(8,128)} %get-tuple-element.35), channel_id=1, source_target_pairs={{32,0},{0,32},{40,8},{8,40},{48,16},{16,48},{56,24},{24,56},{96,64... | collective-permute-start | bytes 393224 | tf_op jit(solution)/shard_map/ppermute | solution.py:473
  22.4 11.1 %collective-permute-start.3 = (f32[2,4,32,128]{3,2,1,0:T(8,128)}, f32[2,4,32,128]{3,2,1,0:T(8,128)S(1)}, u32[]{:S(2)}, u32[]{:S(2)}) collective-permute-start(f32[2,4,32,128]{3,2,1,0:T(8,128)} %get-tuple-element.36), channel_id=1, source_target_pairs={{32,8},{8,32},{40,16},{16,40},{48,24},{24,48},{56,0},{0,56},{96,72... | collective-permute-start | bytes 393224 | tf_op jit(solution)/shard_map/ppermute | solution.py:473
  26.1 10.5 %collective-permute-start.4 = (f32[2,4,32,128]{3,2,1,0:T(8,128)}, f32[2,4,32,128]{3,2,1,0:T(8,128)S(1)}, u32[]{:S(2)}, u32[]{:S(2)}) collective-permute-start(f32[2,4,32,128]{3,2,1,0:T(8,128)} %get-tuple-element.37), channel_id=1, source_target_pairs={{32,16},{16,32},{40,24},{24,40},{48,0},{0,48},{56,8},{8,56},{96,80... | collective-permute-start | bytes 393224 | tf_op jit(solution)/shard_map/ppermute | solution.py:473
  28.0 8.8 %collective-permute-start.5 = (f32[2,4,32,128]{3,2,1,0:T(8,128)S(1)}, f32[2,4,32,128]{3,2,1,0:T(8,128)S(1)}, u32[]{:S(2)}, u32[]{:S(2)}) collective-permute-start(f32[2,4,32,128]{3,2,1,0:T(8,128)S(1)} %get-tuple-element.38), channel_id=1, source_target_pairs={{32,24},{24,32},{40,0},{0,40},{48,8},{8,48},{56,16},{16,56},{96,88... | collective-permute-start | bytes 393224 | tf_op jit(solution)/shard_map/ppermute | solution.py:473
  39.9 11.5 %collective-permute-start.6 = (f32[2,64,512]{2,1,0:T(8,128)S(1)}, f32[2,64,512]{2,1,0:T(8,128)S(1)}, u32[]{:S(2)}, u32[]{:S(2)}) collective-permute-start(f32[2,64,512]{2,1,0:T(8,128)S(1)} %get-tuple-element.39.refs_3_), channel_id=1, source_target_pairs={{32,40},{40,48},{48,56},{96,104},{104,112},{112,120},{120,128},{12... | collective-permute-start | bytes 786440 | tf_op jit(solution)/shard_map/ppermute | solution.py:511
  42.4 2.0 %collective-permute-start.9 = (f32[2,4,16,128]{3,2,1,0:T(8,128)S(1)}, f32[2,4,16,128]{3,2,1,0:T(8,128)S(1)}, u32[]{:S(2)}, u32[]{:S(2)}) collective-permute-start(f32[2,4,16,128]{3,2,1,0:T(8,128)S(1)} %get-tuple-element.41), channel_id=1, source_target_pairs={{0,95},{8,80},{16,72},{24,65},{1,88},{9,81},{17,73},{25,66},{2,89}... | collective-permute-start | bytes 196616 | tf_op jit(solution)/shard_map/ppermute | solution.py:522
  43.0 1.4 %collective-permute-start.8 = (f32[2,4,16,128]{3,2,1,0:T(8,128)S(1)}, f32[2,4,16,128]{3,2,1,0:T(8,128)S(1)}, u32[]{:S(2)}, u32[]{:S(2)}) collective-permute-start(f32[2,4,16,128]{3,2,1,0:T(8,128)S(1)} %get-tuple-element.41), channel_id=1, source_target_pairs={{0,72},{8,64},{16,88},{24,80},{1,73},{9,65},{17,89},{25,81},{2,74}... | collective-permute-start | bytes 196616 | tf_op jit(solution)/shard_map/ppermute | solution.py:522
  43.7 0.7 collective-permute-start.7
  44.5 2.0 %collective-permute-start.12 = (f32[2,4,16,128]{3,2,1,0:T(8,128)S(1)}, f32[2,4,16,128]{3,2,1,0:T(8,128)S(1)}, u32[]{:S(2)}, u32[]{:S(2)}) collective-permute-start(f32[2,4,16,128]{3,2,1,0:T(8,128)S(1)} %get-tuple-element.43), channel_id=1, source_target_pairs={{64,159},{72,144},{80,136},{88,129},{65,152},{73,145},{81,137},{89... | collective-permute-start | bytes 196616 | tf_op jit(solution)/shard_map/ppermute | solution.py:522
  45.2 1.4 %collective-permute-start.11 = (f32[2,4,16,128]{3,2,1,0:T(8,128)S(1)}, f32[2,4,16,128]{3,2,1,0:T(8,128)S(1)}, u32[]{:S(2)}, u32[]{:S(2)}) collective-permute-start(f32[2,4,16,128]{3,2,1,0:T(8,128)S(1)} %get-tuple-element.43), channel_id=1, source_target_pairs={{64,136},{72,128},{80,152},{88,144},{65,137},{73,129},{81,153},{89... | collective-permute-start | bytes 196616 | tf_op jit(solution)/shard_map/ppermute | solution.py:522
  45.8 0.7 collective-permute-start.10
  51.4 19.0 %collective-permute-start.13 = (f32[2,64,512]{2,1,0:T(8,128)S(1)}, f32[2,64,512]{2,1,0:T(8,128)S(1)}, u32[]{:S(2)}, u32[]{:S(2)}) collective-permute-start(f32[2,64,512]{2,1,0:T(8,128)S(1)} %get-tuple-element.45), channel_id=1, source_target_pairs={{0,8},{8,16},{16,24},{24,32},{56,64},{64,72},{72,80},{80,88},{88,9... | collective-permute-start | bytes 786440 | tf_op jit(solution)/shard_map/ppermute | solution.py:511
  52.1 17.4 %collective-permute-start.16 = (f32[2,4,16,128]{3,2,1,0:T(8,128)S(1)}, f32[2,4,16,128]{3,2,1,0:T(8,128)S(1)}, u32[]{:S(2)}, u32[]{:S(2)}) collective-permute-start(f32[2,4,16,128]{3,2,1,0:T(8,128)S(1)} %get-tuple-element.46), channel_id=1, source_target_pairs={{128,223},{136,208},{144,200},{152,193},{129,216},{137,209},{145,2... | collective-permute-start | bytes 196616 | tf_op jit(solution)/shard_map/ppermute | solution.py:522
  53.4 16.1 %collective-permute-start.15 = (f32[2,4,16,128]{3,2,1,0:T(8,128)S(1)}, f32[2,4,16,128]{3,2,1,0:T(8,128)S(1)}, u32[]{:S(2)}, u32[]{:S(2)}) collective-permute-start(f32[2,4,16,128]{3,2,1,0:T(8,128)S(1)} %get-tuple-element.46), channel_id=1, source_target_pairs={{128,200},{136,192},{144,216},{152,208},{129,201},{137,193},{145,2... | collective-permute-start | bytes 196616 | tf_op jit(solution)/shard_map/ppermute | solution.py:522
  54.7 15.7 %collective-permute-start.14 = (f32[2,4,16,128]{3,2,1,0:T(8,128)S(1)}, f32[2,4,16,128]{3,2,1,0:T(8,128)S(1)}, u32[]{:S(2)}, u32[]{:S(2)}) collective-permute-start(f32[2,4,16,128]{3,2,1,0:T(8,128)S(1)} %get-tuple-element.46), channel_id=1, source_target_pairs={{128,192},{136,200},{144,208},{152,216},{129,193},{137,201},{145,2... | collective-permute-start | bytes 196616 | tf_op jit(solution)/shard_map/ppermute | solution.py:522
  84.3 2.3 %collective-permute-start.18 = (f32[2,4,16,128]{3,2,1,0:T(8,128)S(1)}, f32[2,4,16,128]{3,2,1,0:T(8,128)S(1)}, u32[]{:S(2)}, u32[]{:S(2)}) collective-permute-start(f32[2,4,16,128]{3,2,1,0:T(8,128)S(1)} %get-tuple-element.53), channel_id=1, source_target_pairs={{1,0},{2,1},{3,2},{4,3},{5,4},{6,5},{7,6},{0,7},{9,8},{10,9},{11,1... | collective-permute-start | bytes 196616 | tf_op jit(solution)/shard_map/ppermute | solution.py:526
  84.6 4.9 %collective-permute-start.17 = (f32[2,4,16,128]{3,2,1,0:T(8,128)S(1)}, f32[2,4,16,128]{3,2,1,0:T(8,128)S(1)}, u32[]{:S(2)}, u32[]{:S(2)}) collective-permute-start(f32[2,4,16,128]{3,2,1,0:T(8,128)S(1)} %get-tuple-element.54), channel_id=1, source_target_pairs={{0,1},{1,2},{2,3},{3,4},{4,5},{5,6},{6,7},{7,0},{8,9},{9,10},{10,1... | collective-permute-start | bytes 196616 | tf_op jit(solution)/shard_map/ppermute | solution.py:525

commit v6 on v5

--- a/solution.py
+++ b/solution.py
@@ -192,7 +192,7 @@
         heun(w, mid, w, coef_f, n)
         return carry
 
-    lax.fori_loop(0, STEPS, step, 0)
+    lax.fori_loop(0, STEPS, step, 0, unroll=2)
     keep = jnp.where(position == 0, 0.0, 1.0).astype(f32)
     for c in range(2):
         for i in range(n):
@@ -293,11 +293,11 @@
             one_tight(t, corr_ref.at[t + 1])
             return carry
 
-        lax.fori_loop(1, SPLIT, step, 0)
+        lax.fori_loop(1, SPLIT, step, 0, unroll=True)
         for c in range(2):
             for i in range(n_t):
                 w_t[c, i] = plane(nat.at[c], i, n_t, HALO - INNER)
-        lax.fori_loop(SPLIT, GROUP - 1, step_tight, 0)
+        lax.fori_loop(SPLIT, GROUP - 1, step_tight, 0, unroll=True)
         if stage + 1 < stages:
             one_tight(GROUP - 1, last_ref)
 
@@ -376,7 +376,7 @@
         heun(w, mid, w, coef, n)
         return carry
 
-    lax.fori_loop(0, STEPS, step, 0)
+    lax.fori_loop(0, STEPS, step, 0, unroll=2)
     started = []
     for b in range(blocks):
         for c in range(2):
@@ -476,8 +476,8 @@
     strips = ring * SPLIT
     pieces, handed = [], []
     for stage in range(stages):
-        carries = stage in (0, stages - 2)
-        extra = ([forward] if carries else []) + (handed if stage >= stages - 2 else [])
+        carries = stage in (1, stages - 2)
+        extra = ([forward] if carries else []) + (handed if stage == stages - 1 else [])
         operands = [where, *coefs] + extra + (gathered if stage == 0 else [*taus, *pieces, corr])
         specs = [SMEM, VMEM, VMEM] + [HBM] * len(extra) + [VMEM] * (len(operands) - 3 - len(extra))
         shapes = [shape(2, rows, cols) if carries else shape(8, LANES)]
@@ -507,7 +507,7 @@
         if carries:
             forward = done[0]
             chain = [g * GROUP + q for g in range(2) for q in range(SPLIT)]
-            pairs = [(i, i + 1) for i in range(intervals - 1) if (i in chain or i + 1 in chain) == (stage > 0)]
+            pairs = [(i, i + 1) for i in range(intervals - 1) if (i in chain or i + 1 in chain) == (stage == stages - 2)]
             handed = handed + [lax.ppermute(forward, "tm", pairs)]
         if stage + 1 < stages:
             pieces = []

time: 95.6 us -> 93.8 us (0.981)
    ppermute x9, waiting for transfers between devices: 14.4 us -> 11.5 us  [shards(): pieces.append(lax.ppermute(last, ('tm', 'space'), pairs))]
    ppermute x2, waiting for transfers between devices: 4.79 us -> 6.93 us  [shards(): handed = handed + [lax.ppermute(forward, 'tm', pairs)]]
where the time goes in v6:
time: 93.8 us; the launch traced here: 93.5 us
  waiting for transfers between devices  36.5 us (39%)
  starting transfers between devices  26.3 us (28%)
  Pallas kernels  17.9 us (19%)
  blocking collectives  11.9 us (13%)
    all_to_all x1, blocking collectives, shards(): got = lax.all_to_all(corr, 'tm', 0, 0, axis_index_groups=groups)  11.9 us
    ppermute x9, waiting for transfers between devices, shards(): pieces.append(lax.ppermute(last, ('tm', 'space'), pairs))  11.5 us
    ppermute x4, waiting for transfers between devices, shards(): gathered.append(lax.ppermute(sent[1 + k], 'tm', pairs))  7.89 us
    ppermute x9, starting transfers between devices, shards(): pieces.append(lax.ppermute(last, ('tm', 'space'), pairs))  7.86 us
    pallas_call x1, Pallas kernels, shards(): pl.pallas_call(forward_kernel, out_shape=(shape(2, rows, cols), shape(blo...  7.71 us
    ppermute x4, starting transfers between devices, shards(): gathered.append(lax.ppermute(sent[1 + k], 'tm', pairs))  7.31 us
    ppermute x2, waiting for transfers between devices, shards(): handed = handed + [lax.ppermute(forward, 'tm', pairs)]  6.93 us
    pallas_call x1, Pallas kernels, shards(): pl.pallas_call(final_kernel, out_shape=shape(1, 2, rows, cols), in_specs=...  5.35 us
  transfers between devices with their start and end apart: 20, of which 10 were waited for; matrix products, arithmetic and copies ran while one was open for 0% of the time, Pallas kernels for 1%

profile of v6, /device:TPU:192, one launch (start us, length us, event | category | flops | bytes accessed | tf_op | source)
XLA Modules:
  0.0 93.5 jit_solution(7226402125445868845)
XLA Ops:
  0.6 1.8 %edges.1 = (f32[3,32,512]{2,1,0:T(8,128)}, f32[3,32,512]{2,1,0:T(8,128)}) custom-call(f32[1,2,64,512]{3,2,1,0:T(8,128)} %c_ref.5, f32[64,512]{1,0:T(8,128)} %n_ref.5), custom_call_target="tpu_custom_call" | custom-call | tf_op jit(solution)/shard_map/edges/pallas_call | solution.py:413
  2.4 0.0 collective-permute-start
  2.5 2.9 %collective-permute-start.1 = (f32[3,32,512]{2,1,0:T(8,128)}, f32[3,32,512]{2,1,0:T(8,128)S(1)}, u32[]{:S(2)}, u32[]{:S(2)}) collective-permute-start(f32[3,32,512]{2,1,0:T(8,128)} %get-tuple-element.29), channel_id=1, source_target_pairs={{1,0},{2,1},{3,2},{4,3},{5,4},{6,5},{7,6},{0,7},{9,8},{10,9},{11,1... | collective-permute-start | bytes 589832 | tf_op jit(solution)/shard_map/ppermute | solution.py:433
  5.4 0.2 load.1.own_ref
  5.6 3.3 %collective-permute-done.lo_ref.clo_ref = f32[3,32,512]{2,1,0:T(8,128)S(1)} collective-permute-done((f32[3,32,512]{2,1,0:T(8,128)}, f32[3,32,512]{2,1,0:T(8,128)S(1)}, u32[]{:S(2)}, u32[]{:S(2)}) %collective-permute-start) | collective-permute-done | bytes 196640 | tf_op jit(solution)/shard_map/ppermute | solution.py:432
  9.0 0.0 collective-permute-done.1.hi_ref.chi_ref
  9.0 7.7 %forward.1 = (f32[2,64,512]{2,1,0:T(8,128)S(1)}, f32[4,48,128]{2,1,0:T(8,128)S(1)}, f32[4,2,4,48,128]{4,3,2,1,0:T(8,128)}, f32[2,4,32,128]{3,2,1,0:T(8,128)}, f3...) custom-call(s32[1]{0:T(128)} %bitcast.where_ref.refs_0_, ...), custom_call_target="tpu_custom_call" | custom-call | tf_op jit(solution)/shard_map/forward/pallas_call | solution.py:438
  16.7 4.5 %all-to-all-start = ((f32[4,2,4,48,128]{4,3,2,1,0:T(8,128)}), f32[4,2,4,48,128]{4,3,2,1,0:T(8,128)S(1)}, u32[]{:S(2)}, u32[]{:S(2)}) async-start(f32[4,2,4,48,128]{4,3,2,1,0:T(8,128)} %get-tuple-element.34), calls=%async_computation | async-start | bytes 1572864 | tf_op jit(solution)/shard_map/all_to_all | solution.py:465
  21.2 1.0 %collective-permute-start.2 = (f32[2,4,32,128]{3,2,1,0:T(8,128)}, f32[2,4,32,128]{3,2,1,0:T(8,128)S(1)}, u32[]{:S(2)}, u32[]{:S(2)}) collective-permute-start(f32[2,4,32,128]{3,2,1,0:T(8,128)} %get-tuple-element.35), channel_id=1, source_target_pairs={{32,0},{0,32},{40,8},{8,40},{48,16},{16,48},{56,24},{24,56},{96,64... | collective-permute-start | bytes 393224 | tf_op jit(solution)/shard_map/ppermute | solution.py:473
  22.2 3.7 %collective-permute-start.3 = (f32[2,4,32,128]{3,2,1,0:T(8,128)}, f32[2,4,32,128]{3,2,1,0:T(8,128)S(1)}, u32[]{:S(2)}, u32[]{:S(2)}) collective-permute-start(f32[2,4,32,128]{3,2,1,0:T(8,128)} %get-tuple-element.36), channel_id=1, source_target_pairs={{32,8},{8,32},{40,16},{16,40},{48,24},{24,48},{56,0},{0,56},{96,72... | collective-permute-start | bytes 393224 | tf_op jit(solution)/shard_map/ppermute | solution.py:473
  25.9 1.9 %collective-permute-start.4 = (f32[2,4,32,128]{3,2,1,0:T(8,128)}, f32[2,4,32,128]{3,2,1,0:T(8,128)S(1)}, u32[]{:S(2)}, u32[]{:S(2)}) collective-permute-start(f32[2,4,32,128]{3,2,1,0:T(8,128)} %get-tuple-element.37), channel_id=1, source_target_pairs={{32,16},{16,32},{40,24},{24,40},{48,0},{0,48},{56,8},{8,56},{96,80... | collective-permute-start | bytes 393224 | tf_op jit(solution)/shard_map/ppermute | solution.py:473
  27.8 0.7 collective-permute-start.5
  28.5 0.2 prep.1
  28.7 0.0 collective-permute-done.2.refs_4_
  28.7 4.6 %collective-permute-done.3.refs_5_ = f32[2,4,32,128]{3,2,1,0:T(8,128)S(1)} collective-permute-done((f32[2,4,32,128]{3,2,1,0:T(8,128)}, f32[2,4,32,128]{3,2,1,0:T(8,128)S(1)}, u32[]{:S(2)}, u32[]{:S(2)}) %collective-permute-start.3) | collective-permute-done | bytes 131104 | tf_op jit(solution)/shard_map/ppermute | solution.py:473
  33.4 3.1 %collective-permute-done.4.refs_6_ = f32[2,4,32,128]{3,2,1,0:T(8,128)S(1)} collective-permute-done((f32[2,4,32,128]{3,2,1,0:T(8,128)}, f32[2,4,32,128]{3,2,1,0:T(8,128)S(1)}, u32[]{:S(2)}, u32[]{:S(2)}) %collective-permute-start.4) | collective-permute-done | bytes 131104 | tf_op jit(solution)/shard_map/ppermute | solution.py:473
  36.4 0.2 collective-permute-done.5.refs_7_
  36.6 3.0 %all-to-all-done.refs_3_.refs_4_.refs_5_ = f32[4,2,4,48,128]{4,3,2,1,0:T(8,128)S(1)} async-done(((f32[4,2,4,48,128]{4,3,2,1,0:T(8,128)}), f32[4,2,4,48,128]{4,3,2,1,0:T(8,128)S(1)}, u32[]{:S(2)}, u32[]{:S(2)}) %all-to-all-start) | async-done | bytes 786464 | tf_op jit(solution)/shard_map/all_to_all | solution.py:465
  39.7 0.7 collective-permute-start.8
  40.3 0.7 collective-permute-start.7
  41.0 0.7 collective-permute-start.6
  41.7 0.0 collective-permute-done.8.refs_8_
  41.7 0.0 collective-permute-done.7.refs_7_
  41.7 0.0 collective-permute-done.6.refs_6_
  41.7 0.1 chain1.1
  41.8 2.5 %collective-permute-start.9 = (f32[2,64,512]{2,1,0:T(8,128)S(1)}, f32[2,64,512]{2,1,0:T(8,128)S(1)}, u32[]{:S(2)}, u32[]{:S(2)}) collective-permute-start(f32[2,64,512]{2,1,0:T(8,128)S(1)} %get-tuple-element.42.refs_3_), channel_id=1, source_target_pairs={{32,40},{40,48},{48,56},{96,104},{104,112},{112,120},{120,128},{12... | collective-permute-start | bytes 786440 | tf_op jit(solution)/shard_map/ppermute | solution.py:511
  44.3 0.7 collective-permute-start.12
  45.0 0.7 collective-permute-start.11
  45.6 0.7 collective-permute-start.10
  46.3 0.0 collective-permute-done.12.refs_8_
  46.3 0.0 collective-permute-done.10.refs_6_
  46.4 6.9 %collective-permute-done.9.refs_3_.handed_ref = f32[2,64,512]{2,1,0:T(8,128)S(1)} collective-permute-done((f32[2,64,512]{2,1,0:T(8,128)S(1)}, f32[2,64,512]{2,1,0:T(8,128)S(1)}, u32[]{:S(2)}, u32[]{:S(2)}) %collective-permute-start.9) | collective-permute-done | bytes 262176 | tf_op jit(solution)/shard_map/ppermute | solution.py:511
  53.3 0.1 chain2.1
  53.3 0.7 collective-permute-start.13
  54.0 1.3 %collective-permute-start.16 = (f32[2,4,16,128]{3,2,1,0:T(8,128)S(1)}, f32[2,4,16,128]{3,2,1,0:T(8,128)S(1)}, u32[]{:S(2)}, u32[]{:S(2)}) collective-permute-start(f32[2,4,16,128]{3,2,1,0:T(8,128)S(1)} %get-tuple-element.46), channel_id=1, source_target_pairs={{128,223},{136,208},{144,200},{152,193},{129,216},{137,209},{145,2... | collective-permute-start | bytes 196616 | tf_op jit(solution)/shard_map/ppermute | solution.py:522
  55.3 1.3 %collective-permute-start.15 = (f32[2,4,16,128]{3,2,1,0:T(8,128)S(1)}, f32[2,4,16,128]{3,2,1,0:T(8,128)S(1)}, u32[]{:S(2)}, u32[]{:S(2)}) collective-permute-start(f32[2,4,16,128]{3,2,1,0:T(8,128)S(1)} %get-tuple-element.46), channel_id=1, source_target_pairs={{128,200},{136,192},{144,216},{152,208},{129,201},{137,193},{145,2... | collective-permute-start | bytes 196616 | tf_op jit(solution)/shard_map/ppermute | solution.py:522
  56.6 1.3 %collective-permute-start.14 = (f32[2,4,16,128]{3,2,1,0:T(8,128)S(1)}, f32[2,4,16,128]{3,2,1,0:T(8,128)S(1)}, u32[]{:S(2)}, u32[]{:S(2)}) collective-permute-start(f32[2,4,16,128]{3,2,1,0:T(8,128)S(1)} %get-tuple-element.46), channel_id=1, source_target_pairs={{128,192},{136,200},{144,208},{152,216},{129,193},{137,201},{145,2... | collective-permute-start | bytes 196616 | tf_op jit(solution)/shard_map/ppermute | solution.py:522
  57.9 10.5 %collective-permute-done.16.refs_9_ = f32[2,4,16,128]{3,2,1,0:T(8,128)S(1)} collective-permute-done((f32[2,4,16,128]{3,2,1,0:T(8,128)S(1)}, f32[2,4,16,128]{3,2,1,0:T(8,128)S(1)}, u32[]{:S(2)}, u32[]{:S(2)}) %collective-permute-start.16) | collective-permute-done | bytes 65568 | tf_op jit(solution)/shard_map/ppermute | solution.py:522
  68.5 0.9 collective-permute-done.14.refs_7_
  69.4 0.0 collective-permute-done.13.refs_4_.handed2_ref
  69.4 1.6 %chain3.1 = (f32[8,128]{1,0:T(8,128)}, f32[8,2,4,16,128]{4,3,2,1,0:T(8,128)S(1)}) custom-call(s32[1]{0:T(128)} %bitcast.where_ref.refs_0_, f32[4,7,8,512]{3,2,1,0:T(8,128)S(1)} %get-tuple-element.31.refs_1_, f32[4,5,8,512]{3,2,1,0:T(8,128)S(1)} %get-tuple-element.32.refs_2_, ...), custom_call_target="tpu_custom_call", output_to_operand_aliasing={{1}: (10, {})} | custom-call | tf_op jit(solution)/shard_map/chain3/pallas_call | solution.py:491
  70.9 11.9 %all_to_all.10.got_ref = f32[8,2,4,16,128]{4,3,2,1,0:T(8,128)S(1)} all-to-all(f32[8,2,4,16,128]{4,3,2,1,0:T(8,128)S(1)} %get-tuple-element.48), channel_id=1, replica_groups={{0,8,16,24,32,40,48,56},{64,72,80,88,96,104,112,120},{128,136,144,152,1..., dimensions={0} | all-to-all | bytes 1048576 | tf_op jit(solution)/shard_map/all_to_all | solution.py:524
  82.9 0.4 collective-permute-start.18
  83.2 0.1 collective-permute-start.17
  83.4 0.9 ready.1
  84.3 0.9 collective-permute-done.18.hi_ref
  85.1 3.0 %collective-permute-done.17.lo_ref = f32[2,4,16,128]{3,2,1,0:T(8,128)S(1)} collective-permute-done((f32[2,4,16,128]{3,2,1,0:T(8,128)S(1)}, f32[2,4,16,128]{3,2,1,0:T(8,128)S(1)}, u32[]{:S(2)}, u32[]{:S(2)}) %collective-permute-start.17) | collective-permute-done | bytes 65568 | tf_op jit(solution)/shard_map/ppermute | solution.py:525
  88.1 5.3 %final.1 = f32[1,2,64,512]{3,2,1,0:T(8,128)} custom-call(s32[1]{0:T(128)} %bitcast.where_ref.refs_0_, f32[2,4,64,128]{3,2,1,0:T(8,128)S(1)} %get-tuple-element.50.own_ref, f32[2,4,16,128]{3,2,1,0:T(8,128)S(1)} %collective-permute-done.17.lo_ref, f32[2,4,16,128]{3,2,1,0:T(8,128)S(1)} %collective-permute-done.18.hi_ref, ...), custom_call_target="tpu_custom_call" | custom-call | tf_op jit(solution)/shard_map/final/pallas_call | solution.py:539
  (8 shorter events, 0.1 us)
Async XLA Ops:
  0.6 4.8 %copy-start.1 = (f32[64,512]{1,0:T(8,128)S(1)}, f32[64,512]{1,0:T(8,128)}, u32[]{:S(2)}) copy-start(f32[64,512]{1,0:T(8,128)} %n_ref.5) | copy-start | bytes 393220
  0.6 4.8 %copy-start = (f32[1,2,64,512]{3,2,1,0:T(8,128)S(1)}, f32[1,2,64,512]{3,2,1,0:T(8,128)}, u32[]{:S(2)}) copy-start(f32[1,2,64,512]{3,2,1,0:T(8,128)} %c_ref.5) | copy-start | bytes 786436
  2.4 6.5 %collective-permute-start = (f32[3,32,512]{2,1,0:T(8,128)}, f32[3,32,512]{2,1,0:T(8,128)S(1)}, u32[]{:S(2)}, u32[]{:S(2)}) collective-permute-start(f32[3,32,512]{2,1,0:T(8,128)} %get-tuple-element.28), channel_id=1, source_target_pairs={{0,1},{1,2},{2,3},{3,4},{4,5},{5,6},{6,7},{7,0},{8,9},{9,10},{10,1... | collective-permute-start | bytes 589832 | tf_op jit(solution)/shard_map/ppermute | solution.py:432
  2.5 6.5 %collective-permute-start.1 = (f32[3,32,512]{2,1,0:T(8,128)}, f32[3,32,512]{2,1,0:T(8,128)S(1)}, u32[]{:S(2)}, u32[]{:S(2)}) collective-permute-start(f32[3,32,512]{2,1,0:T(8,128)} %get-tuple-element.29), channel_id=1, source_target_pairs={{1,0},{2,1},{3,2},{4,3},{5,4},{6,5},{7,6},{0,7},{9,8},{10,9},{11,1... | collective-permute-start | bytes 589832 | tf_op jit(solution)/shard_map/ppermute | solution.py:433
  16.7 22.9 %all-to-all-start = ((f32[4,2,4,48,128]{4,3,2,1,0:T(8,128)}), f32[4,2,4,48,128]{4,3,2,1,0:T(8,128)S(1)}, u32[]{:S(2)}, u32[]{:S(2)}) async-start(f32[4,2,4,48,128]{4,3,2,1,0:T(8,128)} %get-tuple-element.34), calls=%async_computation | async-start | bytes 1572864 | tf_op jit(solution)/shard_map/all_to_all | solution.py:465
  21.2 7.5 %collective-permute-start.2 = (f32[2,4,32,128]{3,2,1,0:T(8,128)}, f32[2,4,32,128]{3,2,1,0:T(8,128)S(1)}, u32[]{:S(2)}, u32[]{:S(2)}) collective-permute-start(f32[2,4,32,128]{3,2,1,0:T(8,128)} %get-tuple-element.35), channel_id=1, source_target_pairs={{32,0},{0,32},{40,8},{8,40},{48,16},{16,48},{56,24},{24,56},{96,64... | collective-permute-start | bytes 393224 | tf_op jit(solution)/shard_map/ppermute | solution.py:473
  22.2 11.1 %collective-permute-start.3 = (f32[2,4,32,128]{3,2,1,0:T(8,128)}, f32[2,4,32,128]{3,2,1,0:T(8,128)S(1)}, u32[]{:S(2)}, u32[]{:S(2)}) collective-permute-start(f32[2,4,32,128]{3,2,1,0:T(8,128)} %get-tuple-element.36), channel_id=1, source_target_pairs={{32,8},{8,32},{40,16},{16,40},{48,24},{24,48},{56,0},{0,56},{96,72... | collective-permute-start | bytes 393224 | tf_op jit(solution)/shard_map/ppermute | solution.py:473
  25.9 10.5 %collective-permute-start.4 = (f32[2,4,32,128]{3,2,1,0:T(8,128)}, f32[2,4,32,128]{3,2,1,0:T(8,128)S(1)}, u32[]{:S(2)}, u32[]{:S(2)}) collective-permute-start(f32[2,4,32,128]{3,2,1,0:T(8,128)} %get-tuple-element.37), channel_id=1, source_target_pairs={{32,16},{16,32},{40,24},{24,40},{48,0},{0,48},{56,8},{8,56},{96,80... | collective-permute-start | bytes 393224 | tf_op jit(solution)/shard_map/ppermute | solution.py:473
  27.8 8.8 %collective-permute-start.5 = (f32[2,4,32,128]{3,2,1,0:T(8,128)S(1)}, f32[2,4,32,128]{3,2,1,0:T(8,128)S(1)}, u32[]{:S(2)}, u32[]{:S(2)}) collective-permute-start(f32[2,4,32,128]{3,2,1,0:T(8,128)S(1)} %get-tuple-element.38), channel_id=1, source_target_pairs={{32,24},{24,32},{40,0},{0,40},{48,8},{8,48},{56,16},{16,56},{96,88... | collective-permute-start | bytes 393224 | tf_op jit(solution)/shard_map/ppermute | solution.py:473
  39.7 2.0 %collective-permute-start.8 = (f32[2,4,16,128]{3,2,1,0:T(8,128)S(1)}, f32[2,4,16,128]{3,2,1,0:T(8,128)S(1)}, u32[]{:S(2)}, u32[]{:S(2)}) collective-permute-start(f32[2,4,16,128]{3,2,1,0:T(8,128)S(1)} %get-tuple-element.40), channel_id=1, source_target_pairs={{0,95},{8,80},{16,72},{24,65},{1,88},{9,81},{17,73},{25,66},{2,89}... | collective-permute-start | bytes 196616 | tf_op jit(solution)/shard_map/ppermute | solution.py:522
  40.3 1.4 %collective-permute-start.7 = (f32[2,4,16,128]{3,2,1,0:T(8,128)S(1)}, f32[2,4,16,128]{3,2,1,0:T(8,128)S(1)}, u32[]{:S(2)}, u32[]{:S(2)}) collective-permute-start(f32[2,4,16,128]{3,2,1,0:T(8,128)S(1)} %get-tuple-element.40), channel_id=1, source_target_pairs={{0,72},{8,64},{16,88},{24,80},{1,73},{9,65},{17,89},{25,81},{2,74}... | collective-permute-start | bytes 196616 | tf_op jit(solution)/shard_map/ppermute | solution.py:522
  41.0 0.7 collective-permute-start.6
  41.8 11.5 %collective-permute-start.9 = (f32[2,64,512]{2,1,0:T(8,128)S(1)}, f32[2,64,512]{2,1,0:T(8,128)S(1)}, u32[]{:S(2)}, u32[]{:S(2)}) collective-permute-start(f32[2,64,512]{2,1,0:T(8,128)S(1)} %get-tuple-element.42.refs_3_), channel_id=1, source_target_pairs={{32,40},{40,48},{48,56},{96,104},{104,112},{112,120},{120,128},{12... | collective-permute-start | bytes 786440 | tf_op jit(solution)/shard_map/ppermute | solution.py:511
  44.3 2.0 %collective-permute-start.12 = (f32[2,4,16,128]{3,2,1,0:T(8,128)S(1)}, f32[2,4,16,128]{3,2,1,0:T(8,128)S(1)}, u32[]{:S(2)}, u32[]{:S(2)}) collective-permute-start(f32[2,4,16,128]{3,2,1,0:T(8,128)S(1)} %get-tuple-element.43), channel_id=1, source_target_pairs={{64,159},{72,144},{80,136},{88,129},{65,152},{73,145},{81,137},{89... | collective-permute-start | bytes 196616 | tf_op jit(solution)/shard_map/ppermute | solution.py:522
  45.0 1.4 %collective-permute-start.11 = (f32[2,4,16,128]{3,2,1,0:T(8,128)S(1)}, f32[2,4,16,128]{3,2,1,0:T(8,128)S(1)}, u32[]{:S(2)}, u32[]{:S(2)}) collective-permute-start(f32[2,4,16,128]{3,2,1,0:T(8,128)S(1)} %get-tuple-element.43), channel_id=1, source_target_pairs={{64,136},{72,128},{80,152},{88,144},{65,137},{73,129},{81,153},{89... | collective-permute-start | bytes 196616 | tf_op jit(solution)/shard_map/ppermute | solution.py:522
  45.6 0.7 collective-permute-start.10
  53.3 16.0 %collective-permute-start.13 = (f32[2,64,512]{2,1,0:T(8,128)S(1)}, f32[2,64,512]{2,1,0:T(8,128)S(1)}, u32[]{:S(2)}, u32[]{:S(2)}) collective-permute-start(f32[2,64,512]{2,1,0:T(8,128)S(1)} %get-tuple-element.45), channel_id=1, source_target_pairs={{0,8},{8,16},{16,24},{24,32},{56,64},{64,72},{72,80},{80,88},{88,9... | collective-permute-start | bytes 786440 | tf_op jit(solution)/shard_map/ppermute | solution.py:511
  54.0 14.4 %collective-permute-start.16 = (f32[2,4,16,128]{3,2,1,0:T(8,128)S(1)}, f32[2,4,16,128]{3,2,1,0:T(8,128)S(1)}, u32[]{:S(2)}, u32[]{:S(2)}) collective-permute-start(f32[2,4,16,128]{3,2,1,0:T(8,128)S(1)} %get-tuple-element.46), channel_id=1, source_target_pairs={{128,223},{136,208},{144,200},{152,193},{129,216},{137,209},{145,2... | collective-permute-start | bytes 196616 | tf_op jit(solution)/shard_map/ppermute | solution.py:522
  55.3 13.1 %collective-permute-start.15 = (f32[2,4,16,128]{3,2,1,0:T(8,128)S(1)}, f32[2,4,16,128]{3,2,1,0:T(8,128)S(1)}, u32[]{:S(2)}, u32[]{:S(2)}) collective-permute-start(f32[2,4,16,128]{3,2,1,0:T(8,128)S(1)} %get-tuple-element.46), channel_id=1, source_target_pairs={{128,200},{136,192},{144,216},{152,208},{129,201},{137,193},{145,2... | collective-permute-start | bytes 196616 | tf_op jit(solution)/shard_map/ppermute | solution.py:522
  56.6 12.7 %collective-permute-start.14 = (f32[2,4,16,128]{3,2,1,0:T(8,128)S(1)}, f32[2,4,16,128]{3,2,1,0:T(8,128)S(1)}, u32[]{:S(2)}, u32[]{:S(2)}) collective-permute-start(f32[2,4,16,128]{3,2,1,0:T(8,128)S(1)} %get-tuple-element.46), channel_id=1, source_target_pairs={{128,192},{136,200},{144,208},{152,216},{129,193},{137,201},{145,2... | collective-permute-start | bytes 196616 | tf_op jit(solution)/shard_map/ppermute | solution.py:522
  82.9 2.3 %collective-permute-start.18 = (f32[2,4,16,128]{3,2,1,0:T(8,128)S(1)}, f32[2,4,16,128]{3,2,1,0:T(8,128)S(1)}, u32[]{:S(2)}, u32[]{:S(2)}) collective-permute-start(f32[2,4,16,128]{3,2,1,0:T(8,128)S(1)} %get-tuple-element.53), channel_id=1, source_target_pairs={{1,0},{2,1},{3,2},{4,3},{5,4},{6,5},{7,6},{0,7},{9,8},{10,9},{11,1... | collective-permute-start | bytes 196616 | tf_op jit(solution)/shard_map/ppermute | solution.py:526
  83.2 4.9 %collective-permute-start.17 = (f32[2,4,16,128]{3,2,1,0:T(8,128)S(1)}, f32[2,4,16,128]{3,2,1,0:T(8,128)S(1)}, u32[]{:S(2)}, u32[]{:S(2)}) collective-permute-start(f32[2,4,16,128]{3,2,1,0:T(8,128)S(1)} %get-tuple-element.54), channel_id=1, source_target_pairs={{0,1},{1,2},{2,3},{3,4},{4,5},{5,6},{6,7},{7,0},{8,9},{9,10},{10,1... | collective-permute-start | bytes 196616 | tf_op jit(solution)/shard_map/ppermute | solution.py:525

commit v7 on v6

--- a/solution.py
+++ b/solution.py
@@ -18,6 +18,7 @@
 FINAL = 96
 LANES = 128
 SPLIT = 4
+FAR_ORDER = (2, 1, 3, 0)
 advect_scale = 0.1
 coarse_size = 1.0
 COARSE = 0.5 * advect_scale * coarse_size
@@ -234,9 +235,9 @@
     rest = refs[3 + carried :]
     if stage == 0:
         near_ref, far_ref = rest[0], refs[-8]
-        for k in range(SPLIT):
+        for i, k in enumerate(FAR_ORDER):
             source = lax.rem(position + SPLIT - k, SPLIT)
-            far_ref[source] = rest[1 + k][...]
+            far_ref[source] = rest[1 + i][...]
     else:
         near_ref, far_ref, own, pair, other, corr_in = rest[:6]
     active = position // SPLIT == stage * planes
@@ -464,7 +465,7 @@
     four = [[p + q for q in range(SPLIT)] for p in planes]
     near = lax.all_to_all(sent[0], "tm", 0, 0, axis_index_groups=four)
     gathered = [near]
-    for k in range(SPLIT):
+    for k in FAR_ORDER:
         pairs = []
         for p in range(0, intervals, GROUP):
             for q in range(SPLIT):

time: 93.8 us -> 93.8 us (level)
    ppermute x4, waiting for transfers between devices: 7.89 us -> 10 us  [shards(): gathered.append(lax.ppermute(sent[1 + k], 'tm', pairs))]
    all_to_all x1, waiting for transfers between devices: 3.03 us -> 1.58 us  [shards(): near = lax.all_to_all(sent[0], 'tm', 0, 0, axis_index_groups=four)]
  transfers between devices with their start and end apart: 20 -> 20, of which waited for: 10 -> 11; matrix products, arithmetic and copies ran while one was open for 0% -> 0% of each run, Pallas kernels for 1% -> 1%
where the time goes in v7:
time: 93.8 us; the launch traced here: 93.5 us
  waiting for transfers between devices  37.2 us (40%)
  starting transfers between devices  25.6 us (27%)
  Pallas kernels  17.9 us (19%)
  blocking collectives  11.9 us (13%)
    all_to_all x1, blocking collectives, shards(): got = lax.all_to_all(corr, 'tm', 0, 0, axis_index_groups=groups)  11.9 us
    ppermute x9, waiting for transfers between devices, shards(): pieces.append(lax.ppermute(last, ('tm', 'space'), pairs))  11.5 us
    ppermute x4, waiting for transfers between devices, shards(): gathered.append(lax.ppermute(sent[1 + k], 'tm', pairs))  10 us
    ppermute x9, starting transfers between devices, shards(): pieces.append(lax.ppermute(last, ('tm', 'space'), pairs))  7.86 us
    pallas_call x1, Pallas kernels, shards(): pl.pallas_call(forward_kernel, out_shape=(shape(2, rows, cols), shape(blo...  7.71 us
    ppermute x2, waiting for transfers between devices, shards(): handed = handed + [lax.ppermute(forward, 'tm', pairs)]  6.93 us
    ppermute x4, starting transfers between devices, shards(): gathered.append(lax.ppermute(sent[1 + k], 'tm', pairs))  6.62 us
    pallas_call x1, Pallas kernels, shards(): pl.pallas_call(final_kernel, out_shape=shape(1, 2, rows, cols), in_specs=...  5.35 us
  transfers between devices with their start and end apart: 20, of which 11 were waited for; matrix products, arithmetic and copies ran while one was open for 0% of the time, Pallas kernels for 1%

profile of v7, /device:TPU:192, one launch (start us, length us, event | category | flops | bytes accessed | tf_op | source)
XLA Modules:
  0.0 93.5 jit_solution(9494229829502838888)
XLA Ops:
  0.6 1.8 %edges.1 = (f32[3,32,512]{2,1,0:T(8,128)}, f32[3,32,512]{2,1,0:T(8,128)}) custom-call(f32[1,2,64,512]{3,2,1,0:T(8,128)} %c_ref.5, f32[64,512]{1,0:T(8,128)} %n_ref.5), custom_call_target="tpu_custom_call" | custom-call | tf_op jit(solution)/shard_map/edges/pallas_call | solution.py:414
  2.4 0.0 collective-permute-start
  2.5 2.9 %collective-permute-start.1 = (f32[3,32,512]{2,1,0:T(8,128)}, f32[3,32,512]{2,1,0:T(8,128)S(1)}, u32[]{:S(2)}, u32[]{:S(2)}) collective-permute-start(f32[3,32,512]{2,1,0:T(8,128)} %get-tuple-element.29), channel_id=1, source_target_pairs={{1,0},{2,1},{3,2},{4,3},{5,4},{6,5},{7,6},{0,7},{9,8},{10,9},{11,1... | collective-permute-start | bytes 589832 | tf_op jit(solution)/shard_map/ppermute | solution.py:434
  5.4 0.2 load.1.own_ref
  5.6 3.3 %collective-permute-done.lo_ref.clo_ref = f32[3,32,512]{2,1,0:T(8,128)S(1)} collective-permute-done((f32[3,32,512]{2,1,0:T(8,128)}, f32[3,32,512]{2,1,0:T(8,128)S(1)}, u32[]{:S(2)}, u32[]{:S(2)}) %collective-permute-start) | collective-permute-done | bytes 196640 | tf_op jit(solution)/shard_map/ppermute | solution.py:433
  9.0 0.0 collective-permute-done.1.hi_ref.chi_ref
  9.0 7.7 %forward.1 = (f32[2,64,512]{2,1,0:T(8,128)S(1)}, f32[4,48,128]{2,1,0:T(8,128)S(1)}, f32[4,2,4,48,128]{4,3,2,1,0:T(8,128)}, f32[2,4,32,128]{3,2,1,0:T(8,128)S(1)}...) custom-call(s32[1]{0:T(128)} %bitcast.where_ref.refs_0_, ...), custom_call_target="tpu_custom_call" | custom-call | tf_op jit(solution)/shard_map/forward/pallas_call | solution.py:439
  16.7 4.5 %all-to-all-start = ((f32[4,2,4,48,128]{4,3,2,1,0:T(8,128)}), f32[4,2,4,48,128]{4,3,2,1,0:T(8,128)S(1)}, u32[]{:S(2)}, u32[]{:S(2)}) async-start(f32[4,2,4,48,128]{4,3,2,1,0:T(8,128)} %get-tuple-element.34), calls=%async_computation | async-start | bytes 1572864 | tf_op jit(solution)/shard_map/all_to_all | solution.py:466
  21.2 4.0 %collective-permute-start.2 = (f32[2,4,32,128]{3,2,1,0:T(8,128)}, f32[2,4,32,128]{3,2,1,0:T(8,128)S(1)}, u32[]{:S(2)}, u32[]{:S(2)}) collective-permute-start(f32[2,4,32,128]{3,2,1,0:T(8,128)} %get-tuple-element.35), channel_id=1, source_target_pairs={{32,16},{16,32},{40,24},{24,40},{48,0},{0,48},{56,8},{8,56},{96,80... | collective-permute-start | bytes 393224 | tf_op jit(solution)/shard_map/ppermute | solution.py:474
  25.2 1.6 %collective-permute-start.3 = (f32[2,4,32,128]{3,2,1,0:T(8,128)}, f32[2,4,32,128]{3,2,1,0:T(8,128)S(1)}, u32[]{:S(2)}, u32[]{:S(2)}) collective-permute-start(f32[2,4,32,128]{3,2,1,0:T(8,128)} %get-tuple-element.36), channel_id=1, source_target_pairs={{32,8},{8,32},{40,16},{16,40},{48,24},{24,48},{56,0},{0,56},{96,72... | collective-permute-start | bytes 393224 | tf_op jit(solution)/shard_map/ppermute | solution.py:474
  26.8 0.0 collective-permute-start.4
  26.8 1.0 %collective-permute-start.5 = (f32[2,4,32,128]{3,2,1,0:T(8,128)S(1)}, f32[2,4,32,128]{3,2,1,0:T(8,128)S(1)}, u32[]{:S(2)}, u32[]{:S(2)}) collective-permute-start(f32[2,4,32,128]{3,2,1,0:T(8,128)S(1)} %get-tuple-element.38), channel_id=1, source_target_pairs={{32,0},{0,32},{40,8},{8,40},{48,16},{16,48},{56,24},{24,56},{96,64... | collective-permute-start | bytes 393224 | tf_op jit(solution)/shard_map/ppermute | solution.py:474
  27.8 0.2 prep.1
  28.0 1.7 %collective-permute-done.2.refs_4_ = f32[2,4,32,128]{3,2,1,0:T(8,128)S(1)} collective-permute-done((f32[2,4,32,128]{3,2,1,0:T(8,128)}, f32[2,4,32,128]{3,2,1,0:T(8,128)S(1)}, u32[]{:S(2)}, u32[]{:S(2)}) %collective-permute-start.2) | collective-permute-done | bytes 131104 | tf_op jit(solution)/shard_map/ppermute | solution.py:474
  29.7 4.3 %collective-permute-done.3.refs_5_ = f32[2,4,32,128]{3,2,1,0:T(8,128)S(1)} collective-permute-done((f32[2,4,32,128]{3,2,1,0:T(8,128)}, f32[2,4,32,128]{3,2,1,0:T(8,128)S(1)}, u32[]{:S(2)}, u32[]{:S(2)}) %collective-permute-start.3) | collective-permute-done | bytes 131104 | tf_op jit(solution)/shard_map/ppermute | solution.py:474
  33.9 2.5 %collective-permute-done.4.refs_6_ = f32[2,4,32,128]{3,2,1,0:T(8,128)S(1)} collective-permute-done((f32[2,4,32,128]{3,2,1,0:T(8,128)}, f32[2,4,32,128]{3,2,1,0:T(8,128)S(1)}, u32[]{:S(2)}, u32[]{:S(2)}) %collective-permute-start.4) | collective-permute-done | bytes 131104 | tf_op jit(solution)/shard_map/ppermute | solution.py:474
  36.4 1.6 %collective-permute-done.5.refs_7_ = f32[2,4,32,128]{3,2,1,0:T(8,128)S(1)} collective-permute-done((f32[2,4,32,128]{3,2,1,0:T(8,128)S(1)}, f32[2,4,32,128]{3,2,1,0:T(8,128)S(1)}, u32[]{:S(2)}, u32[]{:S(2)}) %collective-permute-start.5) | collective-permute-done | bytes 131104 | tf_op jit(solution)/shard_map/ppermute | solution.py:474
  38.1 1.6 %all-to-all-done.refs_3_.refs_4_.refs_5_ = f32[4,2,4,48,128]{4,3,2,1,0:T(8,128)S(1)} async-done(((f32[4,2,4,48,128]{4,3,2,1,0:T(8,128)}), f32[4,2,4,48,128]{4,3,2,1,0:T(8,128)S(1)}, u32[]{:S(2)}, u32[]{:S(2)}) %all-to-all-start) | async-done | bytes 786464 | tf_op jit(solution)/shard_map/all_to_all | solution.py:466
  39.7 0.7 collective-permute-start.8
  40.3 0.7 collective-permute-start.7
  41.0 0.7 collective-permute-start.6
  41.7 0.0 collective-permute-done.8.refs_8_
  41.7 0.0 collective-permute-done.7.refs_7_
  41.7 0.0 collective-permute-done.6.refs_6_
  41.7 0.1 chain1.1
  41.8 2.5 %collective-permute-start.9 = (f32[2,64,512]{2,1,0:T(8,128)S(1)}, f32[2,64,512]{2,1,0:T(8,128)S(1)}, u32[]{:S(2)}, u32[]{:S(2)}) collective-permute-start(f32[2,64,512]{2,1,0:T(8,128)S(1)} %get-tuple-element.42.refs_3_), channel_id=1, source_target_pairs={{32,40},{40,48},{48,56},{96,104},{104,112},{112,120},{120,128},{12... | collective-permute-start | bytes 786440 | tf_op jit(solution)/shard_map/ppermute | solution.py:512
  44.3 0.7 collective-permute-start.12
  45.0 0.7 collective-permute-start.11
  45.6 0.7 collective-permute-start.10
  46.3 0.0 collective-permute-done.12.refs_8_
  46.3 0.0 collective-permute-done.10.refs_6_
  46.4 6.9 %collective-permute-done.9.refs_3_.handed_ref = f32[2,64,512]{2,1,0:T(8,128)S(1)} collective-permute-done((f32[2,64,512]{2,1,0:T(8,128)S(1)}, f32[2,64,512]{2,1,0:T(8,128)S(1)}, u32[]{:S(2)}, u32[]{:S(2)}) %collective-permute-start.9) | collective-permute-done | bytes 262176 | tf_op jit(solution)/shard_map/ppermute | solution.py:512
  53.3 0.1 chain2.1
  53.3 0.7 collective-permute-start.13
  54.0 1.3 %collective-permute-start.16 = (f32[2,4,16,128]{3,2,1,0:T(8,128)S(1)}, f32[2,4,16,128]{3,2,1,0:T(8,128)S(1)}, u32[]{:S(2)}, u32[]{:S(2)}) collective-permute-start(f32[2,4,16,128]{3,2,1,0:T(8,128)S(1)} %get-tuple-element.46), channel_id=1, source_target_pairs={{128,223},{136,208},{144,200},{152,193},{129,216},{137,209},{145,2... | collective-permute-start | bytes 196616 | tf_op jit(solution)/shard_map/ppermute | solution.py:523
  55.3 1.3 %collective-permute-start.15 = (f32[2,4,16,128]{3,2,1,0:T(8,128)S(1)}, f32[2,4,16,128]{3,2,1,0:T(8,128)S(1)}, u32[]{:S(2)}, u32[]{:S(2)}) collective-permute-start(f32[2,4,16,128]{3,2,1,0:T(8,128)S(1)} %get-tuple-element.46), channel_id=1, source_target_pairs={{128,200},{136,192},{144,216},{152,208},{129,201},{137,193},{145,2... | collective-permute-start | bytes 196616 | tf_op jit(solution)/shard_map/ppermute | solution.py:523
  56.6 1.3 %collective-permute-start.14 = (f32[2,4,16,128]{3,2,1,0:T(8,128)S(1)}, f32[2,4,16,128]{3,2,1,0:T(8,128)S(1)}, u32[]{:S(2)}, u32[]{:S(2)}) collective-permute-start(f32[2,4,16,128]{3,2,1,0:T(8,128)S(1)} %get-tuple-element.46), channel_id=1, source_target_pairs={{128,192},{136,200},{144,208},{152,216},{129,193},{137,201},{145,2... | collective-permute-start | bytes 196616 | tf_op jit(solution)/shard_map/ppermute | solution.py:523
  57.9 10.5 %collective-permute-done.16.refs_9_ = f32[2,4,16,128]{3,2,1,0:T(8,128)S(1)} collective-permute-done((f32[2,4,16,128]{3,2,1,0:T(8,128)S(1)}, f32[2,4,16,128]{3,2,1,0:T(8,128)S(1)}, u32[]{:S(2)}, u32[]{:S(2)}) %collective-permute-start.16) | collective-permute-done | bytes 65568 | tf_op jit(solution)/shard_map/ppermute | solution.py:523
  68.5 0.9 collective-permute-done.14.refs_7_
  69.4 0.0 collective-permute-done.13.refs_4_.handed2_ref
  69.4 1.6 %chain3.1 = (f32[8,128]{1,0:T(8,128)}, f32[8,2,4,16,128]{4,3,2,1,0:T(8,128)S(1)}) custom-call(s32[1]{0:T(128)} %bitcast.where_ref.refs_0_, f32[4,7,8,512]{3,2,1,0:T(8,128)S(1)} %get-tuple-element.31.refs_1_, f32[4,5,8,512]{3,2,1,0:T(8,128)S(1)} %get-tuple-element.32.refs_2_, ...), custom_call_target="tpu_custom_call", output_to_operand_aliasing={{1}: (10, {})} | custom-call | tf_op jit(solution)/shard_map/chain3/pallas_call | solution.py:492
  70.9 11.9 %all_to_all.10.got_ref = f32[8,2,4,16,128]{4,3,2,1,0:T(8,128)S(1)} all-to-all(f32[8,2,4,16,128]{4,3,2,1,0:T(8,128)S(1)} %get-tuple-element.48), channel_id=1, replica_groups={{0,8,16,24,32,40,48,56},{64,72,80,88,96,104,112,120},{128,136,144,152,1..., dimensions={0} | all-to-all | bytes 1048576 | tf_op jit(solution)/shard_map/all_to_all | solution.py:525
  82.9 0.4 collective-permute-start.18
  83.2 0.1 collective-permute-start.17
  83.4 0.9 ready.1
  84.3 0.9 collective-permute-done.18.hi_ref
  85.1 3.0 %collective-permute-done.17.lo_ref = f32[2,4,16,128]{3,2,1,0:T(8,128)S(1)} collective-permute-done((f32[2,4,16,128]{3,2,1,0:T(8,128)S(1)}, f32[2,4,16,128]{3,2,1,0:T(8,128)S(1)}, u32[]{:S(2)}, u32[]{:S(2)}) %collective-permute-start.17) | collective-permute-done | bytes 65568 | tf_op jit(solution)/shard_map/ppermute | solution.py:526
  88.1 5.3 %final.1 = f32[1,2,64,512]{3,2,1,0:T(8,128)} custom-call(s32[1]{0:T(128)} %bitcast.where_ref.refs_0_, f32[2,4,64,128]{3,2,1,0:T(8,128)S(1)} %get-tuple-element.50.own_ref, f32[2,4,16,128]{3,2,1,0:T(8,128)S(1)} %collective-permute-done.17.lo_ref, f32[2,4,16,128]{3,2,1,0:T(8,128)S(1)} %collective-permute-done.18.hi_ref, ...), custom_call_target="tpu_custom_call" | custom-call | tf_op jit(solution)/shard_map/final/pallas_call | solution.py:540
  (8 shorter events, 0.1 us)
Async XLA Ops:
  0.6 4.8 %copy-start.1 = (f32[64,512]{1,0:T(8,128)S(1)}, f32[64,512]{1,0:T(8,128)}, u32[]{:S(2)}) copy-start(f32[64,512]{1,0:T(8,128)} %n_ref.5) | copy-start | bytes 393220
  0.6 4.8 %copy-start = (f32[1,2,64,512]{3,2,1,0:T(8,128)S(1)}, f32[1,2,64,512]{3,2,1,0:T(8,128)}, u32[]{:S(2)}) copy-start(f32[1,2,64,512]{3,2,1,0:T(8,128)} %c_ref.5) | copy-start | bytes 786436
  2.4 6.5 %collective-permute-start = (f32[3,32,512]{2,1,0:T(8,128)}, f32[3,32,512]{2,1,0:T(8,128)S(1)}, u32[]{:S(2)}, u32[]{:S(2)}) collective-permute-start(f32[3,32,512]{2,1,0:T(8,128)} %get-tuple-element.28), channel_id=1, source_target_pairs={{0,1},{1,2},{2,3},{3,4},{4,5},{5,6},{6,7},{7,0},{8,9},{9,10},{10,1... | collective-permute-start | bytes 589832 | tf_op jit(solution)/shard_map/ppermute | solution.py:433
  2.5 6.5 %collective-permute-start.1 = (f32[3,32,512]{2,1,0:T(8,128)}, f32[3,32,512]{2,1,0:T(8,128)S(1)}, u32[]{:S(2)}, u32[]{:S(2)}) collective-permute-start(f32[3,32,512]{2,1,0:T(8,128)} %get-tuple-element.29), channel_id=1, source_target_pairs={{1,0},{2,1},{3,2},{4,3},{5,4},{6,5},{7,6},{0,7},{9,8},{10,9},{11,1... | collective-permute-start | bytes 589832 | tf_op jit(solution)/shard_map/ppermute | solution.py:434
  16.7 22.9 %all-to-all-start = ((f32[4,2,4,48,128]{4,3,2,1,0:T(8,128)}), f32[4,2,4,48,128]{4,3,2,1,0:T(8,128)S(1)}, u32[]{:S(2)}, u32[]{:S(2)}) async-start(f32[4,2,4,48,128]{4,3,2,1,0:T(8,128)} %get-tuple-element.34), calls=%async_computation | async-start | bytes 1572864 | tf_op jit(solution)/shard_map/all_to_all | solution.py:466
  21.2 8.5 %collective-permute-start.2 = (f32[2,4,32,128]{3,2,1,0:T(8,128)}, f32[2,4,32,128]{3,2,1,0:T(8,128)S(1)}, u32[]{:S(2)}, u32[]{:S(2)}) collective-permute-start(f32[2,4,32,128]{3,2,1,0:T(8,128)} %get-tuple-element.35), channel_id=1, source_target_pairs={{32,16},{16,32},{40,24},{24,40},{48,0},{0,48},{56,8},{8,56},{96,80... | collective-permute-start | bytes 393224 | tf_op jit(solution)/shard_map/ppermute | solution.py:474
  25.2 8.8 %collective-permute-start.3 = (f32[2,4,32,128]{3,2,1,0:T(8,128)}, f32[2,4,32,128]{3,2,1,0:T(8,128)S(1)}, u32[]{:S(2)}, u32[]{:S(2)}) collective-permute-start(f32[2,4,32,128]{3,2,1,0:T(8,128)} %get-tuple-element.36), channel_id=1, source_target_pairs={{32,8},{8,32},{40,16},{16,40},{48,24},{24,48},{56,0},{0,56},{96,72... | collective-permute-start | bytes 393224 | tf_op jit(solution)/shard_map/ppermute | solution.py:474
  26.8 9.6 %collective-permute-start.4 = (f32[2,4,32,128]{3,2,1,0:T(8,128)}, f32[2,4,32,128]{3,2,1,0:T(8,128)S(1)}, u32[]{:S(2)}, u32[]{:S(2)}) collective-permute-start(f32[2,4,32,128]{3,2,1,0:T(8,128)} %get-tuple-element.37), channel_id=1, source_target_pairs={{32,24},{24,32},{40,0},{0,40},{48,8},{8,48},{56,16},{16,56},{96,88... | collective-permute-start | bytes 393224 | tf_op jit(solution)/shard_map/ppermute | solution.py:474
  26.8 11.3 %collective-permute-start.5 = (f32[2,4,32,128]{3,2,1,0:T(8,128)S(1)}, f32[2,4,32,128]{3,2,1,0:T(8,128)S(1)}, u32[]{:S(2)}, u32[]{:S(2)}) collective-permute-start(f32[2,4,32,128]{3,2,1,0:T(8,128)S(1)} %get-tuple-element.38), channel_id=1, source_target_pairs={{32,0},{0,32},{40,8},{8,40},{48,16},{16,48},{56,24},{24,56},{96,64... | collective-permute-start | bytes 393224 | tf_op jit(solution)/shard_map/ppermute | solution.py:474
  39.7 2.0 %collective-permute-start.8 = (f32[2,4,16,128]{3,2,1,0:T(8,128)S(1)}, f32[2,4,16,128]{3,2,1,0:T(8,128)S(1)}, u32[]{:S(2)}, u32[]{:S(2)}) collective-permute-start(f32[2,4,16,128]{3,2,1,0:T(8,128)S(1)} %get-tuple-element.40), channel_id=1, source_target_pairs={{0,95},{8,80},{16,72},{24,65},{1,88},{9,81},{17,73},{25,66},{2,89}... | collective-permute-start | bytes 196616 | tf_op jit(solution)/shard_map/ppermute | solution.py:523
  40.3 1.4 %collective-permute-start.7 = (f32[2,4,16,128]{3,2,1,0:T(8,128)S(1)}, f32[2,4,16,128]{3,2,1,0:T(8,128)S(1)}, u32[]{:S(2)}, u32[]{:S(2)}) collective-permute-start(f32[2,4,16,128]{3,2,1,0:T(8,128)S(1)} %get-tuple-element.40), channel_id=1, source_target_pairs={{0,72},{8,64},{16,88},{24,80},{1,73},{9,65},{17,89},{25,81},{2,74}... | collective-permute-start | bytes 196616 | tf_op jit(solution)/shard_map/ppermute | solution.py:523
  41.0 0.7 collective-permute-start.6
  41.8 11.5 %collective-permute-start.9 = (f32[2,64,512]{2,1,0:T(8,128)S(1)}, f32[2,64,512]{2,1,0:T(8,128)S(1)}, u32[]{:S(2)}, u32[]{:S(2)}) collective-permute-start(f32[2,64,512]{2,1,0:T(8,128)S(1)} %get-tuple-element.42.refs_3_), channel_id=1, source_target_pairs={{32,40},{40,48},{48,56},{96,104},{104,112},{112,120},{120,128},{12... | collective-permute-start | bytes 786440 | tf_op jit(solution)/shard_map/ppermute | solution.py:512
  44.3 2.0 %collective-permute-start.12 = (f32[2,4,16,128]{3,2,1,0:T(8,128)S(1)}, f32[2,4,16,128]{3,2,1,0:T(8,128)S(1)}, u32[]{:S(2)}, u32[]{:S(2)}) collective-permute-start(f32[2,4,16,128]{3,2,1,0:T(8,128)S(1)} %get-tuple-element.43), channel_id=1, source_target_pairs={{64,159},{72,144},{80,136},{88,129},{65,152},{73,145},{81,137},{89... | collective-permute-start | bytes 196616 | tf_op jit(solution)/shard_map/ppermute | solution.py:523
  45.0 1.4 %collective-permute-start.11 = (f32[2,4,16,128]{3,2,1,0:T(8,128)S(1)}, f32[2,4,16,128]{3,2,1,0:T(8,128)S(1)}, u32[]{:S(2)}, u32[]{:S(2)}) collective-permute-start(f32[2,4,16,128]{3,2,1,0:T(8,128)S(1)} %get-tuple-element.43), channel_id=1, source_target_pairs={{64,136},{72,128},{80,152},{88,144},{65,137},{73,129},{81,153},{89... | collective-permute-start | bytes 196616 | tf_op jit(solution)/shard_map/ppermute | solution.py:523
  45.6 0.7 collective-permute-start.10
  53.3 16.0 %collective-permute-start.13 = (f32[2,64,512]{2,1,0:T(8,128)S(1)}, f32[2,64,512]{2,1,0:T(8,128)S(1)}, u32[]{:S(2)}, u32[]{:S(2)}) collective-permute-start(f32[2,64,512]{2,1,0:T(8,128)S(1)} %get-tuple-element.45), channel_id=1, source_target_pairs={{0,8},{8,16},{16,24},{24,32},{56,64},{64,72},{72,80},{80,88},{88,9... | collective-permute-start | bytes 786440 | tf_op jit(solution)/shard_map/ppermute | solution.py:512
  54.0 14.4 %collective-permute-start.16 = (f32[2,4,16,128]{3,2,1,0:T(8,128)S(1)}, f32[2,4,16,128]{3,2,1,0:T(8,128)S(1)}, u32[]{:S(2)}, u32[]{:S(2)}) collective-permute-start(f32[2,4,16,128]{3,2,1,0:T(8,128)S(1)} %get-tuple-element.46), channel_id=1, source_target_pairs={{128,223},{136,208},{144,200},{152,193},{129,216},{137,209},{145,2... | collective-permute-start | bytes 196616 | tf_op jit(solution)/shard_map/ppermute | solution.py:523
  55.3 13.1 %collective-permute-start.15 = (f32[2,4,16,128]{3,2,1,0:T(8,128)S(1)}, f32[2,4,16,128]{3,2,1,0:T(8,128)S(1)}, u32[]{:S(2)}, u32[]{:S(2)}) collective-permute-start(f32[2,4,16,128]{3,2,1,0:T(8,128)S(1)} %get-tuple-element.46), channel_id=1, source_target_pairs={{128,200},{136,192},{144,216},{152,208},{129,201},{137,193},{145,2... | collective-permute-start | bytes 196616 | tf_op jit(solution)/shard_map/ppermute | solution.py:523
  56.6 12.7 %collective-permute-start.14 = (f32[2,4,16,128]{3,2,1,0:T(8,128)S(1)}, f32[2,4,16,128]{3,2,1,0:T(8,128)S(1)}, u32[]{:S(2)}, u32[]{:S(2)}) collective-permute-start(f32[2,4,16,128]{3,2,1,0:T(8,128)S(1)} %get-tuple-element.46), channel_id=1, source_target_pairs={{128,192},{136,200},{144,208},{152,216},{129,193},{137,201},{145,2... | collective-permute-start | bytes 196616 | tf_op jit(solution)/shard_map/ppermute | solution.py:523
  82.9 2.3 %collective-permute-start.18 = (f32[2,4,16,128]{3,2,1,0:T(8,128)S(1)}, f32[2,4,16,128]{3,2,1,0:T(8,128)S(1)}, u32[]{:S(2)}, u32[]{:S(2)}) collective-permute-start(f32[2,4,16,128]{3,2,1,0:T(8,128)S(1)} %get-tuple-element.53), channel_id=1, source_target_pairs={{1,0},{2,1},{3,2},{4,3},{5,4},{6,5},{7,6},{0,7},{9,8},{10,9},{11,1... | collective-permute-start | bytes 196616 | tf_op jit(solution)/shard_map/ppermute | solution.py:527
  83.2 4.9 %collective-permute-start.17 = (f32[2,4,16,128]{3,2,1,0:T(8,128)S(1)}, f32[2,4,16,128]{3,2,1,0:T(8,128)S(1)}, u32[]{:S(2)}, u32[]{:S(2)}) collective-permute-start(f32[2,4,16,128]{3,2,1,0:T(8,128)S(1)} %get-tuple-element.54), channel_id=1, source_target_pairs={{0,1},{1,2},{2,3},{3,4},{4,5},{5,6},{6,7},{7,0},{8,9},{9,10},{10,1... | collective-permute-start | bytes 196616 | tf_op jit(solution)/shard_map/ppermute | solution.py:526
